TPU v7x, 32 devices: a whole 2x2x4 slice. The times are simulated.
32 devices in a mesh: energy: 8 (over y, x, core), domain: 4 (over z).
Axes of the slice: x: 2, y: 2, z: 4, core: 2. Of those that a mesh axis runs over, the one named last changes fastest.
Arguments:
- inverses: bfloat16 [16, 4, 2, 416, 416], P('energy', 'domain'), may hold values from -6 to 6
- coupling: bfloat16 [4, 416, 416], P('domain'), may hold values from -0.015625 to 0.015625
- lead_green: bfloat16 [16, 2, 416, 416], P('energy'), may hold values from -6 to 6
- phonon: bfloat16 [16, 4, 2, 6656], P('energy', 'domain'), may hold values from -0.0024414062 to 0.0024414062
- neighbors: int32 [4, 416, 16], P('domain'), may hold values from 0 to 415
- shifts: int32 [16], replicated, may hold values from -4 to 4
Outputs:
- green_out: bfloat16 [16, 4, 2, 416, 416], P('energy', 'domain')
Inputs may be any that keep to these rules, and one draw needn't show every extreme that they name: `neighbors`: each entry is an orbital of the same block; an orbital may stand more than once in a row.
All inputs are finite; a program needn't handle non-finite values.
Results may differ from a plain program's by a relative error of at most 0.025.
Values may be sent and summed in bfloat16 or wider, within the bound.
No kernel may reach another device: no remote copies, remote signals or barrier semaphores. Data moves between devices by JAX's collectives and lax.ppermute only.
A program may use at most 128 MiB of HBM per device.

v0:
```python
import functools

import jax
import jax.numpy as jnp
from jax import lax
from jax.experimental import pallas as pl
from jax.experimental.pallas import tpu as pltpu
from jax.sharding import PartitionSpec as P

LANES = 128
SUBLANES = 8
VMEM_LIMIT = 48 * 1024 * 1024


def product(first, second):
    return jnp.dot(first, second, preferred_element_type=jnp.float32)


def product_nt(first, second):
    return lax.dot_general(
        first, second, (((1,), (1,)), ((), ())), preferred_element_type=jnp.float32
    )


def product_tn(first, second):
    return lax.dot_general(
        first, second, (((0,), (0,)), ((), ())), preferred_element_type=jnp.float32
    )


def packed_rows(orbitals):
    return 2 * orbitals * orbitals // LANES


def pack_planes(out_ref, planes):
    orbitals = planes[0].shape[0]
    whole = orbitals // LANES
    rest = orbitals - whole * LANES
    pieces = LANES // rest // 2
    height = orbitals // pieces
    for c, plane in enumerate(planes):
        for t in range(whole):
            out_ref[pl.ds((c * whole + t) * orbitals, orbitals), :] = plane[
                :, t * LANES : (t + 1) * LANES
            ]
    tails = [
        plane[h * height : (h + 1) * height, whole * LANES :]
        for plane in planes
        for h in range(pieces)
    ]
    out_ref[pl.ds(2 * whole * orbitals, height), :] = jnp.concatenate(tails, axis=1)


def unpack_planes(packed_ref, plane_ref):
    orbitals = plane_ref.shape[1]
    whole = orbitals // LANES
    rest = orbitals - whole * LANES
    pieces = LANES // rest // 2
    height = orbitals // pieces
    tails = packed_ref[pl.ds(2 * whole * orbitals, height), :]
    for c in range(2):
        for t in range(whole):
            plane_ref[c, :, t * LANES : (t + 1) * LANES] = packed_ref[
                pl.ds((c * whole + t) * orbitals, orbitals), :
            ]
        for h in range(pieces):
            start = (c * pieces + h) * rest
            plane_ref[c, h * height : (h + 1) * height, whole * LANES :] = tails[
                :, start : start + rest
            ]


def pack_kernel(e, inverse_ref, up_ref):
    pack_planes(up_ref, [inverse_ref[e, 0, 0], inverse_ref[e, 0, 1]])


def right_kernel(e, inverse_ref, coupling_ref, down_ref):
    coupling = coupling_ref[0]
    planes = []
    for c in range(2):
        right_product = product_nt(inverse_ref[e, 0, c], coupling).astype(jnp.bfloat16)
        planes.append(product(coupling, right_product).astype(jnp.bfloat16))
    pack_planes(down_ref, planes)


def group_iotas():
    sublane = lax.broadcasted_iota(jnp.int32, (SUBLANES, LANES), 0)
    lane = lax.broadcasted_iota(jnp.int32, (SUBLANES, LANES), 1)
    return sublane, lane


def along_lanes(values, lanes):
    return jnp.take_along_axis(values, lanes, axis=1, mode="promise_in_bounds")


def table_kernel(width, neighbors_ref, phonon_ref, columns_ref, slots_ref, same_ref, phonon_out_ref, wide, flat, samples):
    orbitals = neighbors_ref.shape[1]
    groups = orbitals // SUBLANES
    sublane, lane = group_iotas()
    own = sublane == lane // width
    wide[...] = jnp.zeros(wide.shape, wide.dtype)
    wide[:, :width] = neighbors_ref[0]
    flat[...] = jnp.full(flat.shape, -1.0, flat.dtype)
    tiles = slots_ref.shape[1] // LANES
    for r in range(groups):
        rows = slice(r * SUBLANES, (r + 1) * SUBLANES)
        group = wide[rows, :]
        columns = along_lanes(group, lane % width)
        columns_ref[rows, :] = columns
        flat[r : r + 1, :] = jnp.sum(
            jnp.where(own, columns.astype(jnp.float32), 0.0), axis=0, keepdims=True
        )
        found = [jnp.full((SUBLANES, LANES), -1, jnp.int32) for _ in range(tiles)]
        for k in range(width):
            column = jnp.broadcast_to(group[:, k : k + 1], (SUBLANES, LANES))
            slot = sublane * width + k
            for t in range(tiles):
                found[t] = jnp.where(column == lane + t * LANES, slot, found[t])
        for t in range(tiles):
            slots_ref[rows, t * LANES : (t + 1) * LANES] = found[t]
    for d in range(1, width):
        turned = (lane // width) * width + (lane + d) % width
        for r in range(flat.shape[0] // SUBLANES):
            rows = slice(r * SUBLANES, (r + 1) * SUBLANES)
            here = flat[rows, :]
            there = along_lanes(here, turned)
            same_ref[d - 1, rows, :] = jnp.where(here == there, 1.0, 0.0)
    samples[...] = jnp.zeros(samples.shape, samples.dtype)
    for e in range(phonon_ref.shape[0]):
        for r in range(groups):
            samples[e, :, r, :] = phonon_ref[e, 0, :, r * LANES : (r + 1) * LANES].astype(
                jnp.float32
            )
    phonon_out_ref[...] = samples[...].astype(jnp.bfloat16)


def green_kernel(
    e, width, up_ref, down_ref, lead_ref, inverse_ref, coupling_ref, columns_ref,
    green_ref, pair_ref, previous, right_self, wide, flat,
):
    orbitals = inverse_ref.shape[3]
    at_start = lax.axis_index("domain") == 0

    @pl.when(at_start)
    def _():
        previous[...] = lead_ref[e]

    @pl.when(jnp.logical_not(at_start))
    def _():
        unpack_planes(up_ref, previous)

    unpack_planes(down_ref, right_self)
    coupling = coupling_ref[0]
    inverse = [inverse_ref[e, 0, c] for c in range(2)]
    coupled = []
    for c in range(2):
        left_product = product(previous[c], coupling).astype(jnp.bfloat16)
        left_self = product_tn(coupling, left_product).astype(jnp.bfloat16)
        coupled.append(
            (left_self.astype(jnp.float32) + right_self[c].astype(jnp.float32)).astype(jnp.bfloat16)
        )
    inner_real = (product(coupled[0], inverse[0]) - product(coupled[1], inverse[1])).astype(jnp.bfloat16)
    inner_imag = (product(coupled[0], inverse[1]) + product(coupled[1], inverse[0])).astype(jnp.bfloat16)
    real = product(inverse[0], inner_real) - product(inverse[1], inner_imag)
    imag = product(inverse[0], inner_imag) + product(inverse[1], inner_real)
    for c, part in enumerate((real, imag)):
        green = (inverse[c].astype(jnp.float32) + part).astype(jnp.bfloat16)
        green_ref[c] = green
        wide[c, :, :orbitals] = green.astype(jnp.float32)
    gather_pairs(width, wide, columns_ref, flat, pair_ref)


def gather_pairs(width, wide, columns_ref, flat, pair_ref):
    orbitals = columns_ref.shape[0]
    tiles = wide.shape[2] // LANES
    sublane, lane = group_iotas()
    own = sublane == lane // width
    flat[...] = jnp.zeros(flat.shape, flat.dtype)
    for r in range(orbitals // SUBLANES):
        rows = slice(r * SUBLANES, (r + 1) * SUBLANES)
        columns = columns_ref[rows, :]
        within = columns & (LANES - 1)
        tile = columns // LANES
        for c in range(2):
            taken = jnp.zeros((SUBLANES, LANES), jnp.float32)
            for t in range(tiles):
                candidate = along_lanes(wide[c, rows, t * LANES : (t + 1) * LANES], within)
                taken = jnp.where(own & (tile == t), candidate, taken)
            flat[c, r : r + 1, :] = jnp.sum(taken, axis=0, keepdims=True)
    pair_ref[0] = flat[...].astype(jnp.bfloat16)


def final_kernel(
    width, shifts_ref, phonon_ref, even_ref, odd_ref, slots_ref, same_ref, green_even_ref, green_odd_ref,
    out_ref, merged, self_block,
):
    points = phonon_ref.shape[0]
    orbitals = out_ref.shape[3]
    height = phonon_ref.shape[2]
    groups = orbitals // SUBLANES
    tiles = slots_ref.shape[1] // LANES
    me = lax.axis_index("energy")
    _, lane = group_iotas()
    for e, green_ref in enumerate((green_even_ref, green_odd_ref)):

        def add_point(w, sums):
            source = 2 * me + e - shifts_ref[w]
            inside = (source >= 0) & (source < points)
            source = jnp.clip(source, 0, points - 1)
            owner = source // 2
            keep = jnp.where(inside, 1.0, 0.0)
            odd = source - 2 * owner == 1
            sample = [phonon_ref[w, c].astype(jnp.float32) * keep for c in range(2)]
            taken = [
                jnp.where(odd, odd_ref[owner, c], even_ref[owner, c]).astype(jnp.float32)
                for c in range(2)
            ]
            return (
                sums[0] + (sample[0] * taken[0] - sample[1] * taken[1]),
                sums[1] + (sample[0] * taken[1] + sample[1] * taken[0]),
            )

        zero = jnp.zeros((height, LANES), jnp.float32)
        sums = lax.fori_loop(0, points, add_point, (zero, zero))
        for c in range(2):
            pairs = sums[c].astype(jnp.bfloat16).astype(jnp.float32)
            for r in range(height // SUBLANES):
                rows = slice(r * SUBLANES, (r + 1) * SUBLANES)
                group = pairs[rows]
                total = group
                for d in range(1, width):
                    turned = (lane // width) * width + (lane + d) % width
                    total = total + same_ref[d - 1, rows, :] * along_lanes(group, turned)
                merged[c, rows, :] = total
        for q in range(groups // 2):
            for t in range(tiles):
                found = [[], []]
                for r in (2 * q, 2 * q + 1):
                    slot = slots_ref[r * SUBLANES : (r + 1) * SUBLANES, t * LANES : (t + 1) * LANES]
                    within = slot & (LANES - 1)
                    for c in range(2):
                        row = jnp.broadcast_to(merged[c, r : r + 1, :], (SUBLANES, LANES))
                        found[c].append(jnp.where(slot >= 0, along_lanes(row, within), 0.0))
                for c in range(2):
                    self_block[c, q * 16 : (q + 1) * 16, t * LANES : (t + 1) * LANES] = (
                        jnp.concatenate(found[c], axis=0).astype(jnp.bfloat16)
                    )
        green = [green_ref[c] for c in range(2)]
        sigma = [self_block[c, :, :orbitals] for c in range(2)]
        real = (product(green[0], sigma[0]) - product(green[1], sigma[1])).astype(jnp.bfloat16)
        imag = (product(green[0], sigma[1]) + product(green[1], sigma[0])).astype(jnp.bfloat16)
        out_ref[e, 0, 0] = (
            green[0].astype(jnp.float32) + (product(real, green[0]) - product(imag, green[1]))
        ).astype(jnp.bfloat16)
        out_ref[e, 0, 1] = (
            green[1].astype(jnp.float32) + (product(real, green[1]) + product(imag, green[0]))
        ).astype(jnp.bfloat16)


IN_VMEM = pl.BlockSpec(memory_space=pltpu.VMEM)
IN_SMEM = pl.BlockSpec(memory_space=pltpu.SMEM)


def call(kernel, out_shape, in_specs, scratch=(), flops=0, bytes_accessed=1 << 20):
    return pl.pallas_call(
        kernel,
        out_shape=out_shape,
        in_specs=in_specs,
        out_specs=jax.tree.map(lambda s: IN_VMEM, out_shape),
        scratch_shapes=list(scratch),
        compiler_params=pltpu.CompilerParams(vmem_limit_bytes=VMEM_LIMIT),
        cost_estimate=pl.CostEstimate(flops=flops, bytes_accessed=bytes_accessed, transcendentals=0),
    )


def body(inverses, coupling, lead_green, phonon, neighbors, shifts):
    energies = inverses.shape[0]
    orbitals = inverses.shape[3]
    width = neighbors.shape[2]
    points = shifts.shape[0]
    rows = packed_rows(orbitals)
    groups = orbitals * width // LANES
    height = -(-groups // 16) * 16
    padded = -(-orbitals // LANES) * LANES
    bf16, f32 = jnp.bfloat16, jnp.float32
    shape = jax.ShapeDtypeStruct
    cube = 2 * orbitals**3
    ends = lax.axis_size("domain") - 1
    upward = [(i, i + 1) for i in range(ends)]
    downward = [(i + 1, i) for i in range(ends)]

    from_below, from_above = [], []
    for e in range(energies):
        up = call(functools.partial(pack_kernel, e), shape((rows, LANES), bf16), [IN_VMEM])(inverses)
        from_below.append(lax.ppermute(up, "domain", upward))
        down = call(
            functools.partial(right_kernel, e),
            shape((rows, LANES), bf16),
            [IN_VMEM] * 2,
            flops=4 * cube,
        )(inverses, coupling)
        from_above.append(lax.ppermute(down, "domain", downward))

    columns, slots, same, samples = call(
        functools.partial(table_kernel, width),
        (
            shape((orbitals, LANES), jnp.int32),
            shape((orbitals, padded), jnp.int32),
            shape((width - 1, height, LANES), f32),
            shape((energies, 2, height, LANES), bf16),
        ),
        [IN_VMEM] * 2,
        [
            pltpu.VMEM((orbitals, LANES), jnp.int32),
            pltpu.VMEM((height, LANES), f32),
            pltpu.VMEM((energies, 2, height, LANES), f32),
        ],
    )(neighbors, phonon)
    phonon_all = lax.all_gather(samples, "energy", axis=0, tiled=True)

    greens, pairs = [], []
    for e in range(energies):
        green, pair = call(
            functools.partial(green_kernel, e, width),
            (shape((2, orbitals, orbitals), bf16), shape((1, 2, height, LANES), bf16)),
            [IN_VMEM] * 6,
            [
                pltpu.VMEM((2, orbitals, orbitals), bf16),
                pltpu.VMEM((2, orbitals, orbitals), bf16),
                pltpu.VMEM((2, orbitals, padded), f32),
                pltpu.VMEM((2, height, LANES), f32),
            ],
            flops=12 * cube,
        )(from_below[e], from_above[e], lead_green, inverses, coupling, columns)
        greens.append(green)
        pairs.append(lax.all_gather(pair, "energy", axis=0, tiled=True))

    return call(
        functools.partial(final_kernel, width),
        shape((energies, 1, 2, orbitals, orbitals), bf16),
        [IN_SMEM] + [IN_VMEM] * 7,
        [
            pltpu.VMEM((2, height, LANES), f32),
            pltpu.VMEM((2, orbitals, padded), bf16),
        ],
        flops=16 * cube,
    )(shifts, phonon_all, pairs[0], pairs[1], slots, same, greens[0], greens[1])


def solution(mesh):
    return jax.shard_map(
        body,
        mesh=mesh,
        in_specs=(
            P("energy", "domain", None, None, None),
            P("domain", None, None),
            P("energy", None, None, None),
            P("energy", "domain", None, None),
            P("domain", None, None),
            P(),
        ),
        out_specs=P("energy", "domain", None, None, None),
        check_vma=False,
    )
```

profile of v0, /device:TPU:25, one launch (start us, length us, event | category | flops | bytes accessed | tf_op | source)
XLA Modules:
  0.0 70.9 jit_solution(5258781726506590073)
XLA Ops:
  0.0 0.0 copy-start
  0.0 1.5 %copy-done = bf16[2,1,2,416,416]{4,3,2,1,0:T(8,128)(2,1)S(1)} copy-done((bf16[2,1,2,416,416]{4,3,2,1,0:T(8,128)(2,1)S(1)}, bf16[2,1,2,416,416]{4,3,2,1,0:T(8,128)(2,1)}, u32[]{:S(2)}) %copy-start) | copy-done | bytes 1384472
  1.5 0.0 copy-start.1
  1.5 0.1 shard_map.68
  1.6 1.3 %collective-permute-start.2 = (bf16[2704,128]{1,0:T(8,128)(2,1)S(1)}, bf16[2704,128]{1,0:T(8,128)(2,1)}, u32[]{:S(2)}, u32[]{:S(2)}) collective-permute-start(bf16[2704,128]{1,0:T(8,128)(2,1)S(1)} %shard_map.68), channel_id=1, source_target_pairs={{0,1},{1,2},{2,3},{4,5},{5,6},{6,7},{8,9},{9,10},{10,11},{12,13},{... | collective-permute-start | bytes 2076680 | tf_op jit(solution)/shard_map/ppermute | solution.py:295
  2.9 0.0 copy-done.1
  2.9 1.3 %shard_map.69 = bf16[2704,128]{1,0:T(8,128)(2,1)S(1)} custom-call(bf16[2,1,2,416,416]{4,3,2,1,0:T(8,128)(2,1)S(1)} %copy-done, bf16[1,416,416]{2,1,0:T(8,128)(2,1)S(1)} %copy-done.1), custom_call_target="tpu_custom_call" | custom-call | flops 575930368 | bytes 1048576 | tf_op jit(solution)/shard_map/pallas_call | solution.py:296
  4.2 4.8 %collective-permute-start.3 = (bf16[2704,128]{1,0:T(8,128)(2,1)S(1)}, bf16[2704,128]{1,0:T(8,128)(2,1)}, u32[]{:S(2)}, u32[]{:S(2)}) collective-permute-start(bf16[2704,128]{1,0:T(8,128)(2,1)S(1)} %shard_map.69), channel_id=1, source_target_pairs={{1,0},{2,1},{3,2},{5,4},{6,5},{7,6},{9,8},{10,9},{11,10},{13,12},{... | collective-permute-start | bytes 2076680 | tf_op jit(solution)/shard_map/ppermute | solution.py:302
  9.1 0.1 shard_map.65
  9.2 0.0 copy-start.6
  9.2 0.0 copy-start.2
  9.2 1.4 %collective-permute-start = (bf16[2704,128]{1,0:T(8,128)(2,1)S(1)}, bf16[2704,128]{1,0:T(8,128)(2,1)}, u32[]{:S(2)}, u32[]{:S(2)}) collective-permute-start(bf16[2704,128]{1,0:T(8,128)(2,1)S(1)} %shard_map.65), channel_id=1, source_target_pairs={{0,1},{1,2},{2,3},{4,5},{5,6},{6,7},{8,9},{9,10},{10,11},{12,13},{... | collective-permute-start | bytes 2076680 | tf_op jit(solution)/shard_map/ppermute | solution.py:295
  10.6 1.3 %shard_map.66 = bf16[2704,128]{1,0:T(8,128)(2,1)S(1)} custom-call(bf16[2,1,2,416,416]{4,3,2,1,0:T(8,128)(2,1)S(1)} %copy-done, bf16[1,416,416]{2,1,0:T(8,128)(2,1)S(1)} %copy-done.1), custom_call_target="tpu_custom_call" | custom-call | flops 575930368 | bytes 1048576 | tf_op jit(solution)/shard_map/pallas_call | solution.py:296
  12.0 4.9 %collective-permute-start.1 = (bf16[2704,128]{1,0:T(8,128)(2,1)S(1)}, bf16[2704,128]{1,0:T(8,128)(2,1)}, u32[]{:S(2)}, u32[]{:S(2)}) collective-permute-start(bf16[2704,128]{1,0:T(8,128)(2,1)S(1)} %shard_map.66), channel_id=1, source_target_pairs={{1,0},{2,1},{3,2},{5,4},{6,5},{7,6},{9,8},{10,9},{11,10},{13,12},{... | collective-permute-start | bytes 2076680 | tf_op jit(solution)/shard_map/ppermute | solution.py:302
  16.8 0.0 copy-done.6
  16.8 0.1 copy.8.neighbors_ref
  17.0 0.0 copy-done.2
  17.0 2.2 %shard_map.64 = (s32[416,128]{1,0:T(8,128)S(1)}, s32[416,512]{1,0:T(8,128)S(1)}, f32[15,64,128]{2,1,0:T(8,128)S(1)}, bf16[2,2,64,128]{3,2,1,0:T(8,128)(2,1)S(1)}) custom-call(s32[1,416,16]{2,1,0:T(8,128)S(1)} %copy.8.neighbors_ref, bf16[2,1,2,6656]{3,2,1,0:T(2,128)(2,1)S(1)} %copy-done.2), custom_call_target="tpu_custom_call" | custom-call | bytes 1048576 | tf_op jit(solution)/shard_map/pallas_call | solution.py:304
  19.2 11.5 %all_gather.9.phonon_ref = bf16[16,2,64,128]{3,2,1,0:T(8,128)(2,1)S(1)} all-gather(bf16[2,2,64,128]{3,2,1,0:T(8,128)(2,1)S(1)} %get-tuple-element.13), channel_id=1, replica_groups=mesh['energy'=8,'domain'=4] {'energy'}, dimensions={0}, use_global_device_ids=true | all-gather | bytes 589824 | tf_op jit(solution)/shard_map/all_gather | solution.py:319
  30.7 0.0 collective-permute-done.2.up_ref
  30.7 0.0 collective-permute-done.3.down_ref
  30.7 0.0 copy-start.3
  30.7 1.4 %copy-done.3 = bf16[2,2,416,416]{3,2,1,0:T(8,128)(2,1)S(1)} copy-done((bf16[2,2,416,416]{3,2,1,0:T(8,128)(2,1)S(1)}, bf16[2,2,416,416]{3,2,1,0:T(8,128)(2,1)}, u32[]{:S(2)}) %copy-start.3) | copy-done | bytes 1384472
  32.1 0.0 copy-start.4
  32.1 5.6 %shard_map.70 = (bf16[2,416,416]{2,1,0:T(8,128)(2,1)S(1)}, bf16[1,2,64,128]{3,2,1,0:T(8,128)(2,1)S(1)}) custom-call(bf16[2704,128]{1,0:T(8,128)(2,1)} %collective-permute-done.2.up_ref, bf16[2704,128]{1,0:T(8,128)(2,1)} %collective-permute-done.3.down_ref, bf16[2,2,416,416]{3,2,1,0:T(8,128)(2,1)S(1)} %copy-done.3, bf16[2,1,2,416,416]{4,3,2,1,0:T(8,128)(2,1)} %inverse_ref.11, ...), custom_call_target="tpu_custom_call" | custom-call | flops 1727791104 | bytes 1048576 | tf_op jit(solution)/shard_map/pallas_call | solution.py:323
  37.8 9.3 %all_gather.11.odd_ref = bf16[8,2,64,128]{3,2,1,0:T(8,128)(2,1)S(1)} all-gather(bf16[1,2,64,128]{3,2,1,0:T(8,128)(2,1)S(1)} %get-tuple-element.16), channel_id=1, replica_groups=mesh['energy'=8,'domain'=4] {'energy'}, dimensions={0}, use_global_device_ids=true | all-gather | bytes 294912 | tf_op jit(solution)/shard_map/all_gather | solution.py:336
  47.0 0.0 copy-start.5
  47.1 0.0 collective-permute-done.up_ref
  47.1 0.0 collective-permute-done.1.down_ref
  47.1 0.0 copy-done.4
  47.1 5.7 %shard_map.67 = (bf16[2,416,416]{2,1,0:T(8,128)(2,1)S(1)}, bf16[1,2,64,128]{3,2,1,0:T(8,128)(2,1)S(1)}) custom-call(bf16[2704,128]{1,0:T(8,128)(2,1)} %collective-permute-done.up_ref, bf16[2704,128]{1,0:T(8,128)(2,1)} %collective-permute-done.1.down_ref, bf16[2,2,416,416]{3,2,1,0:T(8,128)(2,1)S(1)} %copy-done.4, bf16[2,1,2,416,416]{4,3,2,1,0:T(8,128)(2,1)} %inverse_ref.11, ...), custom_call_target="tpu_custom_call" | custom-call | flops 1727791104 | bytes 1048576 | tf_op jit(solution)/shard_map/pallas_call | solution.py:323
  52.8 8.3 %all_gather.10.even_ref = bf16[8,2,64,128]{3,2,1,0:T(8,128)(2,1)S(1)} all-gather(bf16[1,2,64,128]{3,2,1,0:T(8,128)(2,1)S(1)} %get-tuple-element.15), channel_id=1, replica_groups=mesh['energy'=8,'domain'=4] {'energy'}, dimensions={0}, use_global_device_ids=true | all-gather | bytes 294912 | tf_op jit(solution)/shard_map/all_gather | solution.py:336
  61.1 0.0 copy-done.5
  61.1 9.8 %shard_map.71 = bf16[2,1,2,416,416]{4,3,2,1,0:T(8,128)(2,1)} custom-call(s32[16]{0:T(128)S(1)} %copy-done.5, bf16[16,2,64,128]{3,2,1,0:T(8,128)(2,1)S(1)} %all_gather.9.phonon_ref, bf16[8,2,64,128]{3,2,1,0:T(8,128)(2,1)S(1)} %all_gather.10.even_ref, bf16[8,2,64,128]{3,2,1,0:T(8,128)(2,1)S(1)} %all_gather.11.odd_ref, ...), custom_call_target="tpu_custom_call" | custom-call | flops 2303721472 | bytes 1048576 | tf_op jit(solution)/shard_map/pallas_call | solution.py:338
Async XLA Ops:
  0.0 1.5 %copy-start = (bf16[2,1,2,416,416]{4,3,2,1,0:T(8,128)(2,1)S(1)}, bf16[2,1,2,416,416]{4,3,2,1,0:T(8,128)(2,1)}, u32[]{:S(2)}) copy-start(bf16[2,1,2,416,416]{4,3,2,1,0:T(8,128)(2,1)} %inverse_ref.11) | copy-start | bytes 4153348
  1.5 1.4 %copy-start.1 = (bf16[1,416,416]{2,1,0:T(8,128)(2,1)S(1)}, bf16[1,416,416]{2,1,0:T(8,128)(2,1)}, u32[]{:S(2)}) copy-start(bf16[1,416,416]{2,1,0:T(8,128)(2,1)} %coupling_ref.7) | copy-start | bytes 1038340
  1.6 29.1 %collective-permute-start.2 = (bf16[2704,128]{1,0:T(8,128)(2,1)S(1)}, bf16[2704,128]{1,0:T(8,128)(2,1)}, u32[]{:S(2)}, u32[]{:S(2)}) collective-permute-start(bf16[2704,128]{1,0:T(8,128)(2,1)S(1)} %shard_map.68), channel_id=1, source_target_pairs={{0,1},{1,2},{2,3},{4,5},{5,6},{6,7},{8,9},{9,10},{10,11},{12,13},{... | collective-permute-start | bytes 2076680 | tf_op jit(solution)/shard_map/ppermute | solution.py:295
  4.2 26.4 %collective-permute-start.3 = (bf16[2704,128]{1,0:T(8,128)(2,1)S(1)}, bf16[2704,128]{1,0:T(8,128)(2,1)}, u32[]{:S(2)}, u32[]{:S(2)}) collective-permute-start(bf16[2704,128]{1,0:T(8,128)(2,1)S(1)} %shard_map.69), channel_id=1, source_target_pairs={{1,0},{2,1},{3,2},{5,4},{6,5},{7,6},{9,8},{10,9},{11,10},{13,12},{... | collective-permute-start | bytes 2076680 | tf_op jit(solution)/shard_map/ppermute | solution.py:302
  9.2 7.6 %copy-start.6 = (s32[1,416,16]{1,2,0:T(8,128)S(1)}, s32[1,416,16]{1,2,0:T(8,128)}, u32[]{:S(2)}) copy-start(s32[1,416,16]{1,2,0:T(8,128)} %param.10) | copy-start | bytes 79876
  9.2 7.8 %copy-start.2 = (bf16[2,1,2,6656]{3,2,1,0:T(2,128)(2,1)S(1)}, bf16[2,1,2,6656]{3,2,1,0:T(2,128)(2,1)}, u32[]{:S(2)}) copy-start(bf16[2,1,2,6656]{3,2,1,0:T(2,128)(2,1)} %phonon_ref.1) | copy-start | bytes 159748
  9.2 37.8 %collective-permute-start = (bf16[2704,128]{1,0:T(8,128)(2,1)S(1)}, bf16[2704,128]{1,0:T(8,128)(2,1)}, u32[]{:S(2)}, u32[]{:S(2)}) collective-permute-start(bf16[2704,128]{1,0:T(8,128)(2,1)S(1)} %shard_map.65), channel_id=1, source_target_pairs={{0,1},{1,2},{2,3},{4,5},{5,6},{6,7},{8,9},{9,10},{10,11},{12,13},{... | collective-permute-start | bytes 2076680 | tf_op jit(solution)/shard_map/ppermute | solution.py:295
  12.0 35.1 %collective-permute-start.1 = (bf16[2704,128]{1,0:T(8,128)(2,1)S(1)}, bf16[2704,128]{1,0:T(8,128)(2,1)}, u32[]{:S(2)}, u32[]{:S(2)}) collective-permute-start(bf16[2704,128]{1,0:T(8,128)(2,1)S(1)} %shard_map.66), channel_id=1, source_target_pairs={{1,0},{2,1},{3,2},{5,4},{6,5},{7,6},{9,8},{10,9},{11,10},{13,12},{... | collective-permute-start | bytes 2076680 | tf_op jit(solution)/shard_map/ppermute | solution.py:302
  30.7 1.5 %copy-start.3 = (bf16[2,2,416,416]{3,2,1,0:T(8,128)(2,1)S(1)}, bf16[2,2,416,416]{3,2,1,0:T(8,128)(2,1)}, u32[]{:S(2)}) copy-start(bf16[2,2,416,416]{3,2,1,0:T(8,128)(2,1)} %lead_ref.3) | copy-start | bytes 4153348
  32.1 14.9 %copy-start.4 = (bf16[2,2,416,416]{3,2,1,0:T(8,128)(2,1)S(1)}, bf16[2,2,416,416]{3,2,1,0:T(8,128)(2,1)}, u32[]{:S(2)}) copy-start(bf16[2,2,416,416]{3,2,1,0:T(8,128)(2,1)} %lead_ref.3) | copy-start | bytes 4153348
  47.0 14.1 %copy-start.5 = (s32[16]{0:T(128)S(1)}, s32[16]{0:T(128)}, u32[]{:S(2)}) copy-start(s32[16]{0:T(128)} %shifts_ref.1) | copy-start | bytes 196
where the time goes:
time: 71.3 us; the launch traced here: 70.9 us
  blocking collectives  29.1 us (41%)
  Pallas kernels  26.2 us (37%)
  starting transfers between devices  12.4 us (17%)
  local copies, waits for them, and re-layouts  3.05 us (4%)
    all_gather x2, blocking collectives, body(): pairs.append(lax.all_gather(pair, 'energy', axis=0, tiled=True))  17.6 us
    all_gather x1, blocking collectives, body(): phonon_all = lax.all_gather(samples, 'energy', axis=0, tiled=True)  11.5 us
    pallas_call x2, Pallas kernels, body(): call(functools.partial(green_kernel, e, width), (shape((2, orbitals, orbi...  11.3 us
    pallas_call x1, Pallas kernels, body(): call(functools.partial(final_kernel, width), shape((energies, 1, 2, orbit...  9.83 us
    ppermute x2, starting transfers between devices, body(): from_above.append(lax.ppermute(down, 'domain', downward))  9.71 us
    unnamed x15, local copies, waits for them, and re-layouts  3.05 us
    ppermute x2, starting transfers between devices, body(): from_below.append(lax.ppermute(up, 'domain', upward))  2.72 us
    pallas_call x2, Pallas kernels, body(): call(functools.partial(right_kernel, e), shape((rows, LANES), bf16), [IN_...  2.64 us
  transfers between devices with their start and end apart: 4, of which 0 were waited for; matrix products, arithmetic and copies ran while one was open for 0% of the time, Pallas kernels for 15%

commit v1 on v0

v1 whole, which is shorter than its diff:
```python
import functools

import jax
import jax.numpy as jnp
from jax import lax
from jax.experimental import pallas as pl
from jax.experimental.pallas import tpu as pltpu
from jax.sharding import PartitionSpec as P

LANES = 128
SUBLANES = 8
MIB = 1024 * 1024


def product(first, second):
    return jnp.dot(first, second, preferred_element_type=jnp.float32)


def product_nt(first, second):
    return lax.dot_general(
        first, second, (((1,), (1,)), ((), ())), preferred_element_type=jnp.float32
    )


def product_tn(first, second):
    return lax.dot_general(
        first, second, (((0,), (0,)), ((), ())), preferred_element_type=jnp.float32
    )


def packed_rows(orbitals):
    return 2 * orbitals * orbitals // LANES


def pack_planes(out_ref, planes):
    orbitals = planes[0].shape[0]
    whole = orbitals // LANES
    rest = orbitals - whole * LANES
    pieces = LANES // rest // 2
    height = orbitals // pieces
    for c, plane in enumerate(planes):
        for t in range(whole):
            out_ref[pl.ds((c * whole + t) * orbitals, orbitals), :] = plane[
                :, t * LANES : (t + 1) * LANES
            ]
    tails = [
        plane[h * height : (h + 1) * height, whole * LANES :]
        for plane in planes
        for h in range(pieces)
    ]
    out_ref[pl.ds(2 * whole * orbitals, height), :] = jnp.concatenate(tails, axis=1)


def unpack_planes(packed_ref, plane_ref):
    orbitals = plane_ref.shape[1]
    whole = orbitals // LANES
    rest = orbitals - whole * LANES
    pieces = LANES // rest // 2
    height = orbitals // pieces
    tails = packed_ref[pl.ds(2 * whole * orbitals, height), :]
    for c in range(2):
        for t in range(whole):
            plane_ref[c, :, t * LANES : (t + 1) * LANES] = packed_ref[
                pl.ds((c * whole + t) * orbitals, orbitals), :
            ]
        for h in range(pieces):
            start = (c * pieces + h) * rest
            plane_ref[c, h * height : (h + 1) * height, whole * LANES :] = tails[
                :, start : start + rest
            ]


def send_kernel(e, inverses_ref, coupling_ref, up_ref, down_ref, inverse, coupling, sems):
    copies = [pltpu.make_async_copy(coupling_ref.at[0], coupling, sems.at[2])]
    for c in range(2):
        copies.append(pltpu.make_async_copy(inverses_ref.at[e, 0, c], inverse.at[c], sems.at[c]))
    for copy in copies:
        copy.start()
    copies[0].wait()
    planes = []
    for c in range(2):
        copies[1 + c].wait()
        right_product = product_nt(inverse[c], coupling[...]).astype(jnp.bfloat16)
        planes.append(product(coupling[...], right_product).astype(jnp.bfloat16))
    pack_planes(down_ref, planes)
    pack_planes(up_ref, [inverse[c] for c in range(2)])


def group_iotas():
    sublane = lax.broadcasted_iota(jnp.int32, (SUBLANES, LANES), 0)
    lane = lax.broadcasted_iota(jnp.int32, (SUBLANES, LANES), 1)
    return sublane, lane


def along_lanes(values, lanes):
    return jnp.take_along_axis(values, lanes, axis=1, mode="promise_in_bounds")


def table_kernel(
    width, neighbors_ref, phonon_ref, lead_ref, inverses_ref, coupling_ref,
    columns_ref, slots_ref, samples_ref, lead_held, inverses_held, coupling_held,
    wide, flat, samples, sems,
):
    fetches = [
        pltpu.make_async_copy(source, held, sems.at[i])
        for i, (source, held) in enumerate(
            ((coupling_ref, coupling_held), (inverses_ref, inverses_held), (lead_ref, lead_held))
        )
    ]
    for fetch in fetches:
        fetch.start()
    orbitals = neighbors_ref.shape[1]
    groups = orbitals // SUBLANES
    energies = phonon_ref.shape[0]
    sublane, lane = group_iotas()
    own = sublane == lane // width
    wide[...] = jnp.zeros(wide.shape, wide.dtype)
    wide[:, :width] = neighbors_ref[0]
    flat[...] = jnp.full(flat.shape, -1.0, flat.dtype)
    samples[...] = jnp.zeros(samples.shape, samples.dtype)
    tiles = slots_ref.shape[1] // LANES
    for r in range(groups):
        rows = slice(r * SUBLANES, (r + 1) * SUBLANES)
        group = wide[rows, :]
        columns = along_lanes(group, lane % width)
        columns_ref[rows, :] = columns
        flat[r : r + 1, :] = jnp.sum(
            jnp.where(own, columns.astype(jnp.float32), 0.0), axis=0, keepdims=True
        )
        found = [jnp.full((SUBLANES, LANES), -1, jnp.int32) for _ in range(tiles)]
        for k in range(width):
            column = jnp.broadcast_to(group[:, k : k + 1], (SUBLANES, LANES))
            slot = sublane * width + k
            for t in range(tiles):
                found[t] = jnp.where(column == lane + t * LANES, slot, found[t])
        for t in range(tiles):
            slots_ref[rows, t * LANES : (t + 1) * LANES] = found[t]
        for e in range(energies):
            samples[e, :, r, :] = phonon_ref[e, 0, :, r * LANES : (r + 1) * LANES].astype(
                jnp.float32
            )
    for r in range(flat.shape[0] // SUBLANES):
        rows = slice(r * SUBLANES, (r + 1) * SUBLANES)
        here = flat[rows, :]
        values = [[samples[e, c, rows, :] for c in range(2)] for e in range(energies)]
        totals = [list(pair) for pair in values]
        for d in range(1, width):
            turned = (lane // width) * width + (lane + d) % width
            same = here == along_lanes(here, turned)
            for e in range(energies):
                for c in range(2):
                    totals[e][c] = totals[e][c] + jnp.where(
                        same, along_lanes(values[e][c], turned), 0.0
                    )
        for e in range(energies):
            for c in range(2):
                samples[e, c, rows, :] = totals[e][c]
    samples_ref[...] = samples[...].astype(jnp.bfloat16)
    for fetch in fetches:
        fetch.wait()


def unpack_kernel(packed_ref, plane_ref):
    unpack_planes(packed_ref, plane_ref)


def green_kernel(
    e, width, up_ref, right_self, lead_ref, inverses_ref, coupling_ref, columns_ref, *rest
):
    *pair_before, green_ref, pair_ref, previous, wide, flat = rest
    orbitals = inverses_ref.shape[3]
    at_start = lax.axis_index("domain") == 0

    @pl.when(at_start)
    def _():
        previous[...] = lead_ref[e]

    @pl.when(jnp.logical_not(at_start))
    def _():
        unpack_planes(up_ref, previous)

    coupling = coupling_ref[0]
    inverse = [inverses_ref[e, 0, c] for c in range(2)]
    coupled = []
    for c in range(2):
        left_product = product(previous[c], coupling).astype(jnp.bfloat16)
        left_self = product_tn(coupling, left_product).astype(jnp.bfloat16)
        coupled.append(
            (left_self.astype(jnp.float32) + right_self[c].astype(jnp.float32)).astype(jnp.bfloat16)
        )
    inner_real = (product(coupled[0], inverse[0]) - product(coupled[1], inverse[1])).astype(jnp.bfloat16)
    inner_imag = (product(coupled[0], inverse[1]) + product(coupled[1], inverse[0])).astype(jnp.bfloat16)
    real = product(inverse[0], inner_real) - product(inverse[1], inner_imag)
    imag = product(inverse[0], inner_imag) + product(inverse[1], inner_real)
    for c, part in enumerate((real, imag)):
        green = (inverse[c].astype(jnp.float32) + part).astype(jnp.bfloat16)
        green_ref[c] = green
        wide[c, :, :orbitals] = green.astype(jnp.float32)
    for k, ref in enumerate(pair_before):
        pair_ref[k] = ref[0]
    gather_pairs(width, wide, columns_ref, flat, pair_ref, len(pair_before))


def gather_pairs(width, wide, columns_ref, flat, pair_ref, place):
    orbitals = columns_ref.shape[0]
    tiles = wide.shape[2] // LANES
    sublane, lane = group_iotas()
    own = sublane == lane // width
    flat[...] = jnp.zeros(flat.shape, flat.dtype)
    for r in range(orbitals // SUBLANES):
        rows = slice(r * SUBLANES, (r + 1) * SUBLANES)
        columns = columns_ref[rows, :]
        within = columns & (LANES - 1)
        tile = columns // LANES
        for c in range(2):
            taken = jnp.zeros((SUBLANES, LANES), jnp.float32)
            for t in range(tiles):
                candidate = along_lanes(wide[c, rows, t * LANES : (t + 1) * LANES], within)
                taken = jnp.where(own & (tile == t), candidate, taken)
            flat[c, r : r + 1, :] = jnp.sum(taken, axis=0, keepdims=True)
    pair_ref[place] = flat[...].astype(jnp.bfloat16)


def final_kernel(
    shifts_ref, samples_ref, pairs_ref, slots_ref, green_even_ref, green_odd_ref,
    out_ref, sources, merged, self_block, result, sems,
):
    points = shifts_ref.shape[0]
    orbitals = result.shape[2]
    groups = orbitals // SUBLANES
    tiles = slots_ref.shape[1] // LANES
    used = merged.shape[2]
    me = lax.axis_index("energy")

    def widen(p, _):
        for c in range(2):
            sources[p, c] = pairs_ref[p, c].astype(jnp.float32)
        return _

    lax.fori_loop(0, points, widen, 0, unroll=4)

    def add_point(w, sums):
        shift = shifts_ref[w]
        sample = [samples_ref[w, c].astype(jnp.float32)[:used] for c in range(2)]
        after = []
        for e in range(2):
            source = 2 * me + e - shift
            keep = jnp.where((source >= 0) & (source < points), 1.0, 0.0)
            source = jnp.clip(source, 0, points - 1)
            real, imag = (sources[source, c, :used, :] for c in range(2))
            after.append(
                (
                    sums[e][0] + keep * (sample[0] * real - sample[1] * imag),
                    sums[e][1] + keep * (sample[0] * imag + sample[1] * real),
                )
            )
        return tuple(after)

    zero = jnp.zeros((used, LANES), jnp.float32)
    sums = lax.fori_loop(0, points, add_point, ((zero, zero), (zero, zero)), unroll=4)
    for e in range(2):
        for c in range(2):
            merged[e, c] = sums[e][c]
    copies = []
    for e, green_ref in enumerate((green_even_ref, green_odd_ref)):
        for q in range(groups // 2):
            for t in range(tiles):
                found = [[], []]
                for r in (2 * q, 2 * q + 1):
                    slot = slots_ref[r * SUBLANES : (r + 1) * SUBLANES, t * LANES : (t + 1) * LANES]
                    within = slot & (LANES - 1)
                    for c in range(2):
                        row = jnp.broadcast_to(merged[e, c, r : r + 1, :], (SUBLANES, LANES))
                        found[c].append(jnp.where(slot >= 0, along_lanes(row, within), 0.0))
                for c in range(2):
                    self_block[e, c, q * 16 : (q + 1) * 16, t * LANES : (t + 1) * LANES] = (
                        jnp.concatenate(found[c], axis=0).astype(jnp.bfloat16)
                    )
    for e, green_ref in enumerate((green_even_ref, green_odd_ref)):
        green = [green_ref[c] for c in range(2)]
        sigma = [self_block[e, c, :, :orbitals] for c in range(2)]
        real = (product(green[0], sigma[0]) - product(green[1], sigma[1])).astype(jnp.bfloat16)
        imag = (product(green[0], sigma[1]) + product(green[1], sigma[0])).astype(jnp.bfloat16)
        result[e, 0] = (
            green[0].astype(jnp.float32) + (product(real, green[0]) - product(imag, green[1]))
        ).astype(jnp.bfloat16)
        copies.append(pltpu.make_async_copy(result.at[e, 0], out_ref.at[e, 0, 0], sems.at[e, 0]))
        copies[-1].start()
        result[e, 1] = (
            green[1].astype(jnp.float32) + (product(real, green[1]) + product(imag, green[0]))
        ).astype(jnp.bfloat16)
        copies.append(pltpu.make_async_copy(result.at[e, 1], out_ref.at[e, 0, 1], sems.at[e, 1]))
        copies[-1].start()
    for copy in copies:
        copy.wait()


IN_VMEM = pl.BlockSpec(memory_space=pltpu.VMEM)
IN_SMEM = pl.BlockSpec(memory_space=pltpu.SMEM)
IN_HBM = pl.BlockSpec(memory_space=pltpu.HBM)


def call(kernel, out_shape, in_specs, scratch=(), flops=0, bytes_accessed=1 << 20, out_spec=None, limit=4):
    return pl.pallas_call(
        kernel,
        out_shape=out_shape,
        in_specs=in_specs,
        out_specs=out_spec or (IN_VMEM if not isinstance(out_shape, tuple) else (IN_VMEM,) * len(out_shape)),
        scratch_shapes=list(scratch),
        compiler_params=pltpu.CompilerParams(vmem_limit_bytes=limit * MIB),
        cost_estimate=pl.CostEstimate(flops=flops, bytes_accessed=bytes_accessed, transcendentals=0),
    )


def body(inverses, coupling, lead_green, phonon, neighbors, shifts):
    energies = inverses.shape[0]
    orbitals = inverses.shape[3]
    width = neighbors.shape[2]
    rows = packed_rows(orbitals)
    groups = orbitals * width // LANES
    used = -(-groups // SUBLANES) * SUBLANES
    height = -(-groups // 16) * 16
    padded = -(-orbitals // LANES) * LANES
    bf16, f32 = jnp.bfloat16, jnp.float32
    shape = jax.ShapeDtypeStruct
    cube = 2 * orbitals**3
    plane = (orbitals, orbitals)
    ends = lax.axis_size("domain") - 1
    upward = [(i, i + 1) for i in range(ends)]
    downward = [(i + 1, i) for i in range(ends)]

    from_below, from_above = [], []

    in_hbm = [
        pltpu.with_memory_space_constraint(array, pltpu.HBM)
        for array in (inverses, coupling, lead_green)
    ]

    barred = in_hbm[0]
    for e in range(energies):
        up, down = call(
            functools.partial(send_kernel, e),
            (shape((rows, LANES), bf16), shape((rows, LANES), bf16)),
            [IN_HBM] * 2,
            [
                pltpu.VMEM((2, *plane), bf16),
                pltpu.VMEM(plane, bf16),
                pltpu.SemaphoreType.DMA((3,)),
            ],
            flops=4 * cube,
        )(barred, in_hbm[1])
        from_above.append(lax.ppermute(down, "domain", downward))
        from_below.append(lax.ppermute(up, "domain", upward))
        barred, neighbors, _ = lax.optimization_barrier((barred, neighbors, down))
        barred = pltpu.with_memory_space_constraint(barred, pltpu.HBM)
    columns, slots, samples, lead, inverses, coupling = call(
        functools.partial(table_kernel, width),
        (
            shape((orbitals, LANES), jnp.int32),
            shape((orbitals, padded), jnp.int32),
            shape((energies, 2, height, LANES), bf16),
            pltpu.VMEM(lead_green.shape, bf16),
            pltpu.VMEM(inverses.shape, bf16),
            pltpu.VMEM(coupling.shape, bf16),
        ),
        [IN_VMEM, IN_VMEM, IN_HBM, IN_HBM, IN_HBM],
        [
            pltpu.VMEM((orbitals, LANES), jnp.int32),
            pltpu.VMEM((height, LANES), f32),
            pltpu.VMEM((energies, 2, height, LANES), f32),
            pltpu.SemaphoreType.DMA((3,)),
        ],
        flops=4 * cube,
    )(neighbors, phonon, in_hbm[2], in_hbm[0], in_hbm[1])
    samples = lax.all_gather(samples, "energy", axis=0, tiled=True)
    columns, samples = lax.optimization_barrier((columns, samples))

    greens, pairs = [], []
    for e in range(energies):
        if e:
            from_above[e], *pairs = lax.optimization_barrier((from_above[e], *pairs))
        right_self = call(unpack_kernel, shape((2, *plane), bf16), [IN_VMEM])(from_above[e])
        green, pair = call(
            functools.partial(green_kernel, e, width),
            (shape((2, *plane), bf16), shape((1 + e, 2, height, LANES), bf16)),
            [IN_VMEM] * (6 + e),
            [
                pltpu.VMEM((2, *plane), bf16),
                pltpu.VMEM((2, orbitals, padded), f32),
                pltpu.VMEM((2, height, LANES), f32),
            ],
            flops=12 * cube,
            limit=8,
        )(
            from_below[e],
            right_self,
            lead, inverses, coupling, columns, *pairs)
        greens.append(green)
        pairs.append(pair)
    sources = lax.all_gather(pairs[-1], "energy", axis=0, tiled=True)

    return call(
        final_kernel,
        shape((energies, 1, 2, *plane), bf16),
        [IN_SMEM] + [IN_VMEM] * 5,
        [
            pltpu.VMEM((shifts.shape[0], 2, height, LANES), f32),
            pltpu.VMEM((2, 2, used, LANES), f32),
            pltpu.VMEM((2, 2, orbitals, padded), bf16),
            pltpu.VMEM((2, 2, *plane), bf16),
            pltpu.SemaphoreType.DMA((2, 2)),
        ],
        flops=16 * cube,
        out_spec=IN_HBM,
        limit=16,
    )(shifts, samples, sources, slots, *greens)


def solution(mesh):
    return jax.shard_map(
        body,
        mesh=mesh,
        in_specs=(
            P("energy", "domain", None, None, None),
            P("domain", None, None),
            P("energy", None, None, None),
            P("energy", "domain", None, None),
            P("domain", None, None),
            P(),
        ),
        out_specs=P("energy", "domain", None, None, None),
        check_vma=False,
    )
```

time: 71.3 us -> 61.6 us (0.86)
  the two profiles are of different devices: /device:TPU:25 before, /device:TPU:17 now
where the time goes in v1:
time: 61.6 us; the launch traced here: 61.2 us
  Pallas kernels  26.1 us (42%)
  blocking collectives  23.1 us (38%)
  starting transfers between devices  10.8 us (18%)
  waiting for transfers between devices  0.87 us (1%)
    all_gather x1, blocking collectives, body(): sources = lax.all_gather(pairs[-1], 'energy', axis=0, tiled=True)  11.6 us
    all_gather x1, blocking collectives, body(): samples = lax.all_gather(samples, 'energy', axis=0, tiled=True)  11.5 us
    pallas_call x2, Pallas kernels, body(): call(functools.partial(green_kernel, e, width), (shape((2, *plane), bf16)...  8.57 us
    pallas_call x2, Pallas kernels, body(): call(functools.partial(send_kernel, e), (shape((rows, LANES), bf16), shap...  7.35 us
    pallas_call x1, Pallas kernels, body(): call(final_kernel, shape((energies, 1, 2, *plane), bf16), [IN_SMEM] + [IN...  6.65 us
    ppermute x2, starting transfers between devices, body(): from_below.append(lax.ppermute(up, 'domain', upward))  6.52 us
    ppermute x2, starting transfers between devices, body(): from_above.append(lax.ppermute(down, 'domain', downward))  4.26 us
    pallas_call x1, Pallas kernels, body(): call(functools.partial(table_kernel, width), (shape((orbitals, LANES), jn...  3 us
  transfers between devices with their start and end apart: 4, of which 1 were waited for; matrix products, arithmetic and copies ran while one was open for 0% of the time, Pallas kernels for 19%

profile of v1, /device:TPU:17, one launch (start us, length us, event | category | flops | bytes accessed | tf_op | source)
XLA Modules:
  0.0 61.2 jit_solution(6534862566680887488)
XLA Ops:
  0.0 0.0 copy-start.2
  0.0 3.8 %shard_map.64 = (bf16[2704,128]{1,0:T(8,128)(2,1)}, bf16[2704,128]{1,0:T(8,128)(2,1)}) custom-call(bf16[2,1,2,416,416]{4,3,2,1,0:T(8,128)(2,1)} %inverses_ref.4, bf16[1,416,416]{2,1,0:T(8,128)(2,1)} %coupling_ref.5), custom_call_target="tpu_custom_call" | custom-call | flops 575930368 | bytes 1048576 | tf_op jit(solution)/shard_map/pallas_call | solution.py:341
  3.8 0.0 copy-start
  3.8 2.2 %collective-permute-start.3 = (bf16[2704,128]{1,0:T(8,128)(2,1)}, bf16[2704,128]{1,0:T(8,128)(2,1)S(1)}, u32[]{:S(2)}, u32[]{:S(2)}) collective-permute-start(bf16[2704,128]{1,0:T(8,128)(2,1)} %get-tuple-element.26), channel_id=1, source_target_pairs={{1,0},{2,1},{3,2},{5,4},{6,5},{7,6},{9,8},{10,9},{11,10},{13,12},{... | collective-permute-start | bytes 2076680 | tf_op jit(solution)/shard_map/ppermute | solution.py:352
  6.0 3.2 %collective-permute-start.2 = (bf16[2704,128]{1,0:T(8,128)(2,1)}, bf16[2704,128]{1,0:T(8,128)(2,1)}, u32[]{:S(2)}, u32[]{:S(2)}) collective-permute-start(bf16[2704,128]{1,0:T(8,128)(2,1)} %get-tuple-element.35), channel_id=1, source_target_pairs={{0,1},{1,2},{2,3},{4,5},{5,6},{6,7},{8,9},{9,10},{10,11},{12,13},{... | collective-permute-start | bytes 2076680 | tf_op jit(solution)/shard_map/ppermute | solution.py:353
  9.3 3.6 %shard_map.65 = (bf16[2704,128]{1,0:T(8,128)(2,1)S(1)}, bf16[2704,128]{1,0:T(8,128)(2,1)}) custom-call(bf16[2,1,2,416,416]{4,3,2,1,0:T(8,128)(2,1)} %inverses_ref.4, bf16[1,416,416]{2,1,0:T(8,128)(2,1)} %coupling_ref.5), custom_call_target="tpu_custom_call" | custom-call | flops 575930368 | bytes 1048576 | tf_op jit(solution)/shard_map/pallas_call | solution.py:341
  12.8 2.0 %collective-permute-start.1 = (bf16[2704,128]{1,0:T(8,128)(2,1)}, bf16[2704,128]{1,0:T(8,128)(2,1)S(1)}, u32[]{:S(2)}, u32[]{:S(2)}) collective-permute-start(bf16[2704,128]{1,0:T(8,128)(2,1)} %get-tuple-element.29), channel_id=1, source_target_pairs={{1,0},{2,1},{3,2},{5,4},{6,5},{7,6},{9,8},{10,9},{11,10},{13,12},{... | collective-permute-start | bytes 2076680 | tf_op jit(solution)/shard_map/ppermute | solution.py:352
  14.9 3.3 %collective-permute-start = (bf16[2704,128]{1,0:T(8,128)(2,1)S(1)}, bf16[2704,128]{1,0:T(8,128)(2,1)S(1)}, u32[]{:S(2)}, u32[]{:S(2)}) collective-permute-start(bf16[2704,128]{1,0:T(8,128)(2,1)S(1)} %get-tuple-element.34), channel_id=1, source_target_pairs={{0,1},{1,2},{2,3},{4,5},{5,6},{6,7},{8,9},{9,10},{10,11},{12,13},{... | collective-permute-start | bytes 2076680 | tf_op jit(solution)/shard_map/ppermute | solution.py:353
  18.2 0.0 copy-done.2
  18.2 0.1 copy.8.neighbors_ref
  18.3 0.0 copy-done
  18.3 3.0 %shard_map.66 = (s32[416,128]{1,0:T(8,128)S(1)}, s32[416,512]{1,0:T(8,128)S(1)}, bf16[2,2,64,128]{3,2,1,0:T(8,128)(2,1)S(1)}, bf16[2,2,416,416]{3,2,1,0:T(8,128)...) custom-call(s32[1,416,16]{2,1,0:T(8,128)S(1)} %copy.8.neighbors_ref, ...), custom_call_target="tpu_custom_call" | custom-call | flops 575930368 | bytes 1048576 | tf_op jit(solution)/shard_map/pallas_call | solution.py:356
  21.3 11.5 %all_gather.6.samples_ref = bf16[16,2,64,128]{3,2,1,0:T(8,128)(2,1)S(1)} all-gather(bf16[2,2,64,128]{3,2,1,0:T(8,128)(2,1)S(1)} %get-tuple-element.32), channel_id=1, replica_groups=mesh['energy'=8,'domain'=4] {'energy'}, dimensions={0}, use_global_device_ids=true | all-gather | bytes 589824 | tf_op jit(solution)/shard_map/all_gather | solution.py:375
  32.9 0.0 collective-permute-done.3.packed_ref
  32.9 0.3 shard_map.67.right_self
  33.1 0.0 collective-permute-done.2.up_ref
  33.1 4.7 %shard_map.68 = (bf16[2,416,416]{2,1,0:T(8,128)(2,1)S(1)}, bf16[1,2,64,128]{3,2,1,0:T(8,128)(2,1)S(1)}) custom-call(bf16[2704,128]{1,0:T(8,128)(2,1)} %collective-permute-done.2.up_ref, bf16[2,416,416]{2,1,0:T(8,128)(2,1)S(1)} %shard_map.67.right_self, bf16[2,2,416,416]{3,2,1,0:T(8,128)(2,1)S(1)} %get-tuple-element.36.lead_ref, ...), custom_call_target="tpu_custom_call" | custom-call | flops 1727791104 | bytes 1048576 | tf_op jit(solution)/shard_map/pallas_call | solution.py:383
  37.9 0.0 collective-permute-done.1.packed_ref
  37.9 0.3 shard_map.69.right_self
  38.1 0.0 copy-start.1
  38.2 0.9 %collective-permute-done.up_ref = bf16[2704,128]{1,0:T(8,128)(2,1)S(1)} collective-permute-done((bf16[2704,128]{1,0:T(8,128)(2,1)S(1)}, bf16[2704,128]{1,0:T(8,128)(2,1)S(1)}, u32[]{:S(2)}, u32[]{:S(2)}) %collective-permute-start) | collective-permute-done | bytes 692256 | tf_op jit(solution)/shard_map/ppermute | solution.py:353
  39.0 3.8 %shard_map.70 = (bf16[2,416,416]{2,1,0:T(8,128)(2,1)S(1)}, bf16[2,2,64,128]{3,2,1,0:T(8,128)(2,1)S(1)}) custom-call(bf16[2704,128]{1,0:T(8,128)(2,1)S(1)} %collective-permute-done.up_ref, bf16[2,416,416]{2,1,0:T(8,128)(2,1)S(1)} %shard_map.69.right_self, bf16[2,2,416,416]{3,2,1,0:T(8,128)(2,1)S(1)} %get-tuple-element.36.lead_ref, ...), custom_call_target="tpu_custom_call" | custom-call | flops 1727791104 | bytes 1048576 | tf_op jit(solution)/shard_map/pallas_call | solution.py:383
  42.8 11.6 %all_gather.7.pairs_ref = bf16[16,2,64,128]{3,2,1,0:T(8,128)(2,1)S(1)} all-gather(bf16[2,2,64,128]{3,2,1,0:T(8,128)(2,1)S(1)} %get-tuple-element.43), channel_id=1, replica_groups=mesh['energy'=8,'domain'=4] {'energy'}, dimensions={0}, use_global_device_ids=true | all-gather | bytes 589824 | tf_op jit(solution)/shard_map/all_gather | solution.py:400
  54.4 0.0 copy-done.1
  54.4 6.6 %shard_map.71 = bf16[2,1,2,416,416]{4,3,2,1,0:T(8,128)(2,1)} custom-call(s32[16]{0:T(128)S(1)} %copy-done.1, bf16[16,2,64,128]{3,2,1,0:T(8,128)(2,1)S(1)} %all_gather.6.samples_ref, bf16[16,2,64,128]{3,2,1,0:T(8,128)(2,1)S(1)} %all_gather.7.pairs_ref, s32[416,512]{1,0:T(8,128)S(1)} %get-tuple-element.44.slots_ref, ...), custom_call_target="tpu_custom_call" | custom-call | flops 2303721472 | bytes 1048576 | tf_op jit(solution)/shard_map/pallas_call | solution.py:402
Async XLA Ops:
  0.0 18.2 %copy-start.2 = (s32[1,416,16]{1,2,0:T(8,128)S(1)}, s32[1,416,16]{1,2,0:T(8,128)}, u32[]{:S(2)}) copy-start(s32[1,416,16]{1,2,0:T(8,128)} %param.10) | copy-start | bytes 79876
  3.8 14.5 %copy-start = (bf16[2,1,2,6656]{3,2,1,0:T(2,128)(2,1)S(1)}, bf16[2,1,2,6656]{3,2,1,0:T(2,128)(2,1)}, u32[]{:S(2)}) copy-start(bf16[2,1,2,6656]{3,2,1,0:T(2,128)(2,1)} %phonon_ref.1) | copy-start | bytes 159748
  3.8 29.1 %collective-permute-start.3 = (bf16[2704,128]{1,0:T(8,128)(2,1)}, bf16[2704,128]{1,0:T(8,128)(2,1)S(1)}, u32[]{:S(2)}, u32[]{:S(2)}) collective-permute-start(bf16[2704,128]{1,0:T(8,128)(2,1)} %get-tuple-element.26), channel_id=1, source_target_pairs={{1,0},{2,1},{3,2},{5,4},{6,5},{7,6},{9,8},{10,9},{11,10},{13,12},{... | collective-permute-start | bytes 2076680 | tf_op jit(solution)/shard_map/ppermute | solution.py:352
  6.0 27.1 %collective-permute-start.2 = (bf16[2704,128]{1,0:T(8,128)(2,1)}, bf16[2704,128]{1,0:T(8,128)(2,1)}, u32[]{:S(2)}, u32[]{:S(2)}) collective-permute-start(bf16[2704,128]{1,0:T(8,128)(2,1)} %get-tuple-element.35), channel_id=1, source_target_pairs={{0,1},{1,2},{2,3},{4,5},{5,6},{6,7},{8,9},{9,10},{10,11},{12,13},{... | collective-permute-start | bytes 2076680 | tf_op jit(solution)/shard_map/ppermute | solution.py:353
  12.8 25.0 %collective-permute-start.1 = (bf16[2704,128]{1,0:T(8,128)(2,1)}, bf16[2704,128]{1,0:T(8,128)(2,1)S(1)}, u32[]{:S(2)}, u32[]{:S(2)}) collective-permute-start(bf16[2704,128]{1,0:T(8,128)(2,1)} %get-tuple-element.29), channel_id=1, source_target_pairs={{1,0},{2,1},{3,2},{5,4},{6,5},{7,6},{9,8},{10,9},{11,10},{13,12},{... | collective-permute-start | bytes 2076680 | tf_op jit(solution)/shard_map/ppermute | solution.py:352
  14.9 24.1 %collective-permute-start = (bf16[2704,128]{1,0:T(8,128)(2,1)S(1)}, bf16[2704,128]{1,0:T(8,128)(2,1)S(1)}, u32[]{:S(2)}, u32[]{:S(2)}) collective-permute-start(bf16[2704,128]{1,0:T(8,128)(2,1)S(1)} %get-tuple-element.34), channel_id=1, source_target_pairs={{0,1},{1,2},{2,3},{4,5},{5,6},{6,7},{8,9},{9,10},{10,11},{12,13},{... | collective-permute-start | bytes 2076680 | tf_op jit(solution)/shard_map/ppermute | solution.py:353
  38.1 16.3 %copy-start.1 = (s32[16]{0:T(128)S(1)}, s32[16]{0:T(128)}, u32[]{:S(2)}) copy-start(s32[16]{0:T(128)} %shifts_ref.1) | copy-start | bytes 196

commit v2 on v1

--- a/solution.py
+++ b/solution.py
@@ -8,6 +8,7 @@
 from jax.sharding import PartitionSpec as P
 
 LANES = 128
+NEAR = (0, 2, 6)
 SUBLANES = 8
 MIB = 1024 * 1024
 
@@ -26,6 +27,13 @@
     return lax.dot_general(
         first, second, (((0,), (0,)), ((), ())), preferred_element_type=jnp.float32
     )
+
+
+def complex_product(first, second):
+    reals = product(first[0], second[0])
+    imags = product(first[1], second[1])
+    both = product(first[0] + first[1], second[0] + second[1])
+    return reals - imags, both - reals - imags
 
 
 def packed_rows(orbitals):
@@ -70,20 +78,32 @@
             ]
 
 
-def send_kernel(e, inverses_ref, coupling_ref, up_ref, down_ref, inverse, coupling, sems):
+def send_kernel(
+    e, inverses_ref, coupling_ref, first_ref, second_ref, inverse, right_self, coupling, sems
+):
     copies = [pltpu.make_async_copy(coupling_ref.at[0], coupling, sems.at[2])]
     for c in range(2):
         copies.append(pltpu.make_async_copy(inverses_ref.at[e, 0, c], inverse.at[c], sems.at[c]))
     for copy in copies:
         copy.start()
     copies[0].wait()
-    planes = []
     for c in range(2):
         copies[1 + c].wait()
         right_product = product_nt(inverse[c], coupling[...]).astype(jnp.bfloat16)
-        planes.append(product(coupling[...], right_product).astype(jnp.bfloat16))
-    pack_planes(down_ref, planes)
-    pack_planes(up_ref, [inverse[c] for c in range(2)])
+        right_self[c] = product(coupling[...], right_product).astype(jnp.bfloat16)
+    even = lax.axis_index("domain") % 2 == 0
+
+    def pack(next_ref, before_ref):
+        pack_planes(next_ref, [inverse[c] for c in range(2)])
+        pack_planes(before_ref, [right_self[c] for c in range(2)])
+
+    @pl.when(even)
+    def _():
+        pack(first_ref, second_ref)
+
+    @pl.when(jnp.logical_not(even))
+    def _():
+        pack(second_ref, first_ref)
 
 
 def group_iotas():
@@ -97,14 +117,14 @@
 
 
 def table_kernel(
-    width, neighbors_ref, phonon_ref, lead_ref, inverses_ref, coupling_ref,
-    columns_ref, slots_ref, samples_ref, lead_held, inverses_held, coupling_held,
+    width, neighbors_ref, phonon_ref, lead_ref, coupling_ref,
+    columns_ref, slots_ref, samples_ref, lead_held, coupling_held,
     wide, flat, samples, sems,
 ):
     fetches = [
         pltpu.make_async_copy(source, held, sems.at[i])
         for i, (source, held) in enumerate(
-            ((coupling_ref, coupling_held), (inverses_ref, inverses_held), (lead_ref, lead_held))
+            ((coupling_ref, coupling_held), (lead_ref, lead_held))
         )
     ]
     for fetch in fetches:
@@ -165,22 +185,36 @@
 
 
 def green_kernel(
-    e, width, up_ref, right_self, lead_ref, inverses_ref, coupling_ref, columns_ref, *rest
+    e, width, second_ref, first_planes, lead_ref, inverses_ref, coupling_ref, columns_ref, *rest
 ):
-    *pair_before, green_ref, pair_ref, previous, wide, flat = rest
-    orbitals = inverses_ref.shape[3]
-    at_start = lax.axis_index("domain") == 0
-
-    @pl.when(at_start)
+    *pair_before, green_ref, pair_ref, previous, right_self, inverse, wide, flat, sems = rest
+    orbitals = inverse.shape[1]
+    copies = [
+        pltpu.make_async_copy(inverses_ref.at[e, 0, c], inverse.at[c], sems.at[c]) for c in range(2)
+    ]
+    for copy in copies:
+        copy.start()
+    domain = lax.axis_index("domain")
+    even = domain % 2 == 0
+
+    @pl.when(domain == 0)
     def _():
         previous[...] = lead_ref[e]
 
-    @pl.when(jnp.logical_not(at_start))
-    def _():
-        unpack_planes(up_ref, previous)
+    @pl.when(even & (domain > 0))
+    def _():
+        unpack_planes(second_ref, previous)
+
+    @pl.when(even)
+    def _():
+        right_self[...] = first_planes[...]
+
+    @pl.when(jnp.logical_not(even))
+    def _():
+        previous[...] = first_planes[...]
+        unpack_planes(second_ref, right_self)
 
     coupling = coupling_ref[0]
-    inverse = [inverses_ref[e, 0, c] for c in range(2)]
     coupled = []
     for c in range(2):
         left_product = product(previous[c], coupling).astype(jnp.bfloat16)
@@ -188,12 +222,12 @@
         coupled.append(
             (left_self.astype(jnp.float32) + right_self[c].astype(jnp.float32)).astype(jnp.bfloat16)
         )
-    inner_real = (product(coupled[0], inverse[0]) - product(coupled[1], inverse[1])).astype(jnp.bfloat16)
-    inner_imag = (product(coupled[0], inverse[1]) + product(coupled[1], inverse[0])).astype(jnp.bfloat16)
-    real = product(inverse[0], inner_real) - product(inverse[1], inner_imag)
-    imag = product(inverse[0], inner_imag) + product(inverse[1], inner_real)
-    for c, part in enumerate((real, imag)):
-        green = (inverse[c].astype(jnp.float32) + part).astype(jnp.bfloat16)
+    for copy in copies:
+        copy.wait()
+    own = [inverse[c] for c in range(2)]
+    inner = [part.astype(jnp.bfloat16) for part in complex_product(coupled, own)]
+    for c, part in enumerate(complex_product(own, inner)):
+        green = (own[c].astype(jnp.float32) + part).astype(jnp.bfloat16)
         green_ref[c] = green
         wide[c, :, :orbitals] = green.astype(jnp.float32)
     for k, ref in enumerate(pair_before):
@@ -221,23 +255,28 @@
     pair_ref[place] = flat[...].astype(jnp.bfloat16)
 
 
-def final_kernel(
-    shifts_ref, samples_ref, pairs_ref, slots_ref, green_even_ref, green_odd_ref,
-    out_ref, sources, merged, self_block, result, sems,
-):
+def final_kernel(shifts_ref, samples_ref, slots_ref, green_even_ref, green_odd_ref, *rest):
+    *pairs, out_ref, sources, merged, self_block, result, sems = rest
     points = shifts_ref.shape[0]
     orbitals = result.shape[2]
     groups = orbitals // SUBLANES
     tiles = slots_ref.shape[1] // LANES
     used = merged.shape[2]
     me = lax.axis_index("energy")
-
-    def widen(p, _):
-        for c in range(2):
-            sources[p, c] = pairs_ref[p, c].astype(jnp.float32)
-        return _
-
-    lax.fori_loop(0, points, widen, 0, unroll=4)
+    if len(pairs) == 1:
+
+        def widen(p, carry):
+            for c in range(2):
+                sources[p, c] = pairs[0][p, c].astype(jnp.float32)
+            return carry
+
+        lax.fori_loop(0, points, widen, 0, unroll=4)
+    else:
+        for k, array in enumerate(pairs):
+            owner = (me ^ NEAR[k // 2 % 3]) ^ (k % 2)
+            for e in range(2):
+                for c in range(2):
+                    sources[2 * owner + e, c] = array[e, c].astype(jnp.float32)
 
     def add_point(w, sums):
         shift = shifts_ref[w]
@@ -279,18 +318,11 @@
     for e, green_ref in enumerate((green_even_ref, green_odd_ref)):
         green = [green_ref[c] for c in range(2)]
         sigma = [self_block[e, c, :, :orbitals] for c in range(2)]
-        real = (product(green[0], sigma[0]) - product(green[1], sigma[1])).astype(jnp.bfloat16)
-        imag = (product(green[0], sigma[1]) + product(green[1], sigma[0])).astype(jnp.bfloat16)
-        result[e, 0] = (
-            green[0].astype(jnp.float32) + (product(real, green[0]) - product(imag, green[1]))
-        ).astype(jnp.bfloat16)
-        copies.append(pltpu.make_async_copy(result.at[e, 0], out_ref.at[e, 0, 0], sems.at[e, 0]))
-        copies[-1].start()
-        result[e, 1] = (
-            green[1].astype(jnp.float32) + (product(real, green[1]) + product(imag, green[0]))
-        ).astype(jnp.bfloat16)
-        copies.append(pltpu.make_async_copy(result.at[e, 1], out_ref.at[e, 0, 1], sems.at[e, 1]))
-        copies[-1].start()
+        scattered = [part.astype(jnp.bfloat16) for part in complex_product(green, sigma)]
+        for c, part in enumerate(complex_product(scattered, green)):
+            result[e, c] = (green[c].astype(jnp.float32) + part).astype(jnp.bfloat16)
+            copies.append(pltpu.make_async_copy(result.at[e, c], out_ref.at[e, 0, c], sems.at[e, c]))
+            copies[-1].start()
     for copy in copies:
         copy.wait()
 
@@ -325,11 +357,11 @@
     shape = jax.ShapeDtypeStruct
     cube = 2 * orbitals**3
     plane = (orbitals, orbitals)
-    ends = lax.axis_size("domain") - 1
-    upward = [(i, i + 1) for i in range(ends)]
-    downward = [(i + 1, i) for i in range(ends)]
-
-    from_below, from_above = [], []
+    domains = lax.axis_size("domain")
+    routes = [
+        [swap for i in range(start, domains - 1, 2) for swap in ((i, i + 1), (i + 1, i))]
+        for start in range(2)
+    ]
 
     in_hbm = [
         pltpu.with_memory_space_constraint(array, pltpu.HBM)
@@ -337,72 +369,82 @@
     ]
 
     barred = in_hbm[0]
+    received = []
     for e in range(energies):
-        up, down = call(
+        sent = call(
             functools.partial(send_kernel, e),
             (shape((rows, LANES), bf16), shape((rows, LANES), bf16)),
             [IN_HBM] * 2,
             [
+                pltpu.VMEM((2, *plane), bf16),
                 pltpu.VMEM((2, *plane), bf16),
                 pltpu.VMEM(plane, bf16),
                 pltpu.SemaphoreType.DMA((3,)),
             ],
             flops=4 * cube,
         )(barred, in_hbm[1])
-        from_above.append(lax.ppermute(down, "domain", downward))
-        from_below.append(lax.ppermute(up, "domain", upward))
-        barred, neighbors, _ = lax.optimization_barrier((barred, neighbors, down))
+        received.append([lax.ppermute(x, "domain", route) for x, route in zip(sent, routes)])
+        barred, neighbors, _ = lax.optimization_barrier((barred, neighbors, sent[0]))
         barred = pltpu.with_memory_space_constraint(barred, pltpu.HBM)
-    columns, slots, samples, lead, inverses, coupling = call(
+    columns, slots, samples, lead, coupling = call(
         functools.partial(table_kernel, width),
         (
             shape((orbitals, LANES), jnp.int32),
             shape((orbitals, padded), jnp.int32),
             shape((energies, 2, height, LANES), bf16),
             pltpu.VMEM(lead_green.shape, bf16),
-            pltpu.VMEM(inverses.shape, bf16),
             pltpu.VMEM(coupling.shape, bf16),
         ),
-        [IN_VMEM, IN_VMEM, IN_HBM, IN_HBM, IN_HBM],
+        [IN_VMEM, IN_VMEM, IN_HBM, IN_HBM],
         [
             pltpu.VMEM((orbitals, LANES), jnp.int32),
             pltpu.VMEM((height, LANES), f32),
             pltpu.VMEM((energies, 2, height, LANES), f32),
-            pltpu.SemaphoreType.DMA((3,)),
+            pltpu.SemaphoreType.DMA((2,)),
         ],
         flops=4 * cube,
-    )(neighbors, phonon, in_hbm[2], in_hbm[0], in_hbm[1])
+    )(neighbors, phonon, in_hbm[2], in_hbm[1])
     samples = lax.all_gather(samples, "energy", axis=0, tiled=True)
     columns, samples = lax.optimization_barrier((columns, samples))
 
     greens, pairs = [], []
     for e in range(energies):
+        first, second = received[e]
         if e:
-            from_above[e], *pairs = lax.optimization_barrier((from_above[e], *pairs))
-        right_self = call(unpack_kernel, shape((2, *plane), bf16), [IN_VMEM])(from_above[e])
+            first, *pairs = lax.optimization_barrier((first, *pairs))
+        first = call(unpack_kernel, shape((2, *plane), bf16), [IN_VMEM])(first)
         green, pair = call(
             functools.partial(green_kernel, e, width),
             (shape((2, *plane), bf16), shape((1 + e, 2, height, LANES), bf16)),
-            [IN_VMEM] * (6 + e),
+            [IN_VMEM] * 3 + [IN_HBM] + [IN_VMEM] * (2 + e),
             [
+                pltpu.VMEM((2, *plane), bf16),
+                pltpu.VMEM((2, *plane), bf16),
                 pltpu.VMEM((2, *plane), bf16),
                 pltpu.VMEM((2, orbitals, padded), f32),
                 pltpu.VMEM((2, height, LANES), f32),
+                pltpu.SemaphoreType.DMA((2,)),
             ],
             flops=12 * cube,
-            limit=8,
-        )(
-            from_below[e],
-            right_self,
-            lead, inverses, coupling, columns, *pairs)
+            limit=12,
+        )(second, first, lead, in_hbm[0], coupling, columns, *pairs)
         greens.append(green)
         pairs.append(pair)
-    sources = lax.all_gather(pairs[-1], "energy", axis=0, tiled=True)
+    pair = pairs[-1]
+    devices = lax.axis_size("energy")
+    if devices == 8 and energies == 2:
+        across = lax.ppermute(pair, "energy", [(i, i ^ 6) for i in range(2, 6)])
+        beside = lax.ppermute(pair, "energy", [(i, i ^ 2) for i in range(8)])
+        sources = []
+        for array in (pair, beside, across):
+            sources += [array, lax.ppermute(array, "energy", [(i, i ^ 1) for i in range(8)])]
+    else:
+        sources = [lax.all_gather(pair, "energy", axis=0, tiled=True)]
 
     return call(
         final_kernel,
         shape((energies, 1, 2, *plane), bf16),
-        [IN_SMEM] + [IN_VMEM] * 5,
+        [IN_SMEM] + [IN_VMEM] * (4 + len(sources)),
         [
             pltpu.VMEM((shifts.shape[0], 2, height, LANES), f32),
             pltpu.VMEM((2, 2, used, LANES), f32),
@@ -413,7 +455,7 @@
         flops=16 * cube,
         out_spec=IN_HBM,
         limit=16,
-    )(shifts, samples, sources, slots, *greens)
+    )(shifts, samples, slots, *greens, *sources)
 
 
 def solution(mesh):

time: 61.6 us -> 59.2 us (0.961)
  blocking collectives: 23.1 us -> 11.2 us
  starting transfers between devices: 10.8 us -> 16.4 us
  waiting for transfers between devices: 0.87 us -> 5.11 us
    all_gather x1 -> x0, blocking collectives: 11.6 us -> none  [body(): sources = lax.all_gather(pairs[-1], 'energy', axis=0, tiled=True)]
    ppermute x4 -> x9, starting transfers between devices: 10.8 us -> 16.4 us  [the longest x4 6.7 us: body(): lax.ppermute(x, 'domain', route)]
    ppermute x4 -> x9, waiting for transfers between devices: 0.87 us -> 5.11 us  [the longest x4 4.2 us: body(): lax.ppermute(x, 'domain', route)]
    pallas_call x1, Pallas kernels: 6.65 us -> 5.94 us  [body(): call(final_kernel, shape((energies, 1, 2, *plane), bf16), [IN_SMEM] + [IN...]
  transfers between devices with their start and end apart: 4 -> 9, of which waited for: 1 -> 3; matrix products, arithmetic and copies ran while one was open for 0% -> 0% of each run, Pallas kernels for 19% -> 20%
where the time goes in v2:
time: 59.2 us; the launch traced here: 58.9 us
  Pallas kernels  25.7 us (43%)
  starting transfers between devices  16.4 us (28%)
  blocking collectives  11.2 us (19%)
  waiting for transfers between devices  5.11 us (9%)
    all_gather x1, blocking collectives, body(): samples = lax.all_gather(samples, 'energy', axis=0, tiled=True)  11.2 us
    pallas_call x2, Pallas kernels, body(): call(functools.partial(green_kernel, e, width), (shape((2, *plane), bf16)...  8.69 us
    pallas_call x2, Pallas kernels, body(): call(functools.partial(send_kernel, e), (shape((rows, LANES), bf16), shap...  7.63 us
    ppermute x4, starting transfers between devices, body(): lax.ppermute(x, 'domain', route)  6.7 us
    pallas_call x1, Pallas kernels, body(): call(final_kernel, shape((energies, 1, 2, *plane), bf16), [IN_SMEM] + [IN...  5.94 us
    ppermute x3, starting transfers between devices, body(): lax.ppermute(array, 'energy', [(i, i ^ 1) for i in range(8)])  5.27 us
    ppermute x4, waiting for transfers between devices, body(): lax.ppermute(x, 'domain', route)  4.2 us
    ppermute x1, starting transfers between devices, body(): beside = lax.ppermute(pair, 'energy', [(i, i ^ 2) for i in range(8)])  3.73 us
  transfers between devices with their start and end apart: 9, of which 3 were waited for; matrix products, arithmetic and copies ran while one was open for 0% of the time, Pallas kernels for 20%

profile of v2, /device:TPU:17, one launch (start us, length us, event | category | flops | bytes accessed | tf_op | source)
XLA Modules:
  0.0 58.9 jit_solution(5394828118896335227)
XLA Ops:
  0.0 0.0 copy-start.2
  0.0 3.9 %shard_map.64 = (bf16[2704,128]{1,0:T(8,128)(2,1)}, bf16[2704,128]{1,0:T(8,128)(2,1)}) custom-call(bf16[2,1,2,416,416]{4,3,2,1,0:T(8,128)(2,1)} %inverses_ref.6, bf16[1,416,416]{2,1,0:T(8,128)(2,1)} %coupling_ref.5), custom_call_target="tpu_custom_call" | custom-call | flops 575930368 | bytes 1048576 | tf_op jit(solution)/shard_map/pallas_call | solution.py:374
  3.9 0.0 copy-start
  3.9 1.4 %collective-permute-start.1 = (bf16[2704,128]{1,0:T(8,128)(2,1)}, bf16[2704,128]{1,0:T(8,128)(2,1)S(1)}, u32[]{:S(2)}, u32[]{:S(2)}) collective-permute-start(bf16[2704,128]{1,0:T(8,128)(2,1)} %get-tuple-element.25), channel_id=1, source_target_pairs={{0,1},{1,0},{2,3},{3,2},{4,5},{5,4},{6,7},{7,6},{8,9},{9,8},{10,11... | collective-permute-start | bytes 2076680 | tf_op jit(solution)/shard_map/ppermute | solution.py:386
  5.3 1.9 %collective-permute-start = (bf16[2704,128]{1,0:T(8,128)(2,1)}, bf16[2704,128]{1,0:T(8,128)(2,1)}, u32[]{:S(2)}, u32[]{:S(2)}) collective-permute-start(bf16[2704,128]{1,0:T(8,128)(2,1)} %get-tuple-element.34), channel_id=1, source_target_pairs={{1,2},{2,1},{5,6},{6,5},{9,10},{10,9},{13,14},{14,13},{17,18},{18,... | collective-permute-start | bytes 2076680 | tf_op jit(solution)/shard_map/ppermute | solution.py:386
  7.2 3.7 %shard_map.65 = (bf16[2704,128]{1,0:T(8,128)(2,1)}, bf16[2704,128]{1,0:T(8,128)(2,1)S(1)}) custom-call(bf16[2,1,2,416,416]{4,3,2,1,0:T(8,128)(2,1)} %inverses_ref.6, bf16[1,416,416]{2,1,0:T(8,128)(2,1)} %coupling_ref.5), custom_call_target="tpu_custom_call" | custom-call | flops 575930368 | bytes 1048576 | tf_op jit(solution)/shard_map/pallas_call | solution.py:374
  10.9 0.1 collective-permute-start.3
  11.0 3.4 %collective-permute-start.2 = (bf16[2704,128]{1,0:T(8,128)(2,1)S(1)}, bf16[2704,128]{1,0:T(8,128)(2,1)S(1)}, u32[]{:S(2)}, u32[]{:S(2)}) collective-permute-start(bf16[2704,128]{1,0:T(8,128)(2,1)S(1)} %get-tuple-element.39), channel_id=1, source_target_pairs={{1,2},{2,1},{5,6},{6,5},{9,10},{10,9},{13,14},{14,13},{17,18},{18,... | collective-permute-start | bytes 2076680 | tf_op jit(solution)/shard_map/ppermute | solution.py:386
  14.4 0.0 copy-done.2
  14.4 0.1 copy.8.neighbors_ref
  14.5 0.0 copy-done
  14.5 3.0 %shard_map.66 = (s32[416,128]{1,0:T(8,128)S(1)}, s32[416,512]{1,0:T(8,128)S(1)}, bf16[2,2,64,128]{3,2,1,0:T(8,128)(2,1)S(1)}, bf16[2,2,416,416]{3,2,1,0:T(8,128)(2,1)S(1)}, bf16[1,416,416]{2,1,0:T(8,128)(2,1)S(1)}) custom-call(s32[1,416,16]{2,1,0:T(8,128)S(1)} %copy.8.neighbors_ref, bf16[2,1,2,6656]{3,2,1,0:T(2,128)(2,1)S(1)} %copy-done, ...), custom_call_target="tpu_custom_call" | custom-call | flops 575930368 | bytes 1048576 | tf_op jit(solution)/shard_map/pallas_call | solution.py:389
  17.5 11.2 %all_gather.3.samples_ref = bf16[16,2,64,128]{3,2,1,0:T(8,128)(2,1)S(1)} all-gather(bf16[2,2,64,128]{3,2,1,0:T(8,128)(2,1)S(1)} %get-tuple-element.31), channel_id=1, replica_groups=mesh['energy'=8,'domain'=4] {'energy'}, dimensions={0}, use_global_device_ids=true | all-gather | bytes 589824 | tf_op jit(solution)/shard_map/all_gather | solution.py:407
  28.8 0.0 collective-permute-done.1.packed_ref
  28.8 0.3 shard_map.67.first_planes
  29.0 0.0 collective-permute-done.second_ref
  29.0 4.8 %shard_map.68 = (bf16[2,416,416]{2,1,0:T(8,128)(2,1)S(1)}, bf16[1,2,64,128]{3,2,1,0:T(8,128)(2,1)S(1)}) custom-call(bf16[2704,128]{1,0:T(8,128)(2,1)} %collective-permute-done.second_ref, bf16[2,416,416]{2,1,0:T(8,128)(2,1)S(1)} %shard_map.67.first_planes, bf16[2,2,416,416]{3,2,1,0:T(8,128)(2,1)S(1)} %get-tuple-element.35.lead_ref, ...), custom_call_target="tpu_custom_call" | custom-call | flops 1727791104 | bytes 1048576 | tf_op jit(solution)/shard_map/pallas_call | solution.py:416
  33.8 1.6 %collective-permute-done.3.packed_ref = bf16[2704,128]{1,0:T(8,128)(2,1)S(1)} collective-permute-done((bf16[2704,128]{1,0:T(8,128)(2,1)}, bf16[2704,128]{1,0:T(8,128)(2,1)S(1)}, u32[]{:S(2)}, u32[]{:S(2)}) %collective-permute-start.3) | collective-permute-done | bytes 692256 | tf_op jit(solution)/shard_map/ppermute | solution.py:386
  35.4 0.3 shard_map.69.first_planes
  35.7 0.0 copy-start.1
  35.7 2.6 %collective-permute-done.2.second_ref = bf16[2704,128]{1,0:T(8,128)(2,1)S(1)} collective-permute-done((bf16[2704,128]{1,0:T(8,128)(2,1)S(1)}, bf16[2704,128]{1,0:T(8,128)(2,1)S(1)}, u32[]{:S(2)}, u32[]{:S(2)}) %collective-permute-start.2) | collective-permute-done | bytes 692256 | tf_op jit(solution)/shard_map/ppermute | solution.py:386
  38.3 3.9 %shard_map.70 = (bf16[2,416,416]{2,1,0:T(8,128)(2,1)S(1)}, bf16[2,2,64,128]{3,2,1,0:T(8,128)(2,1)S(1)}) custom-call(bf16[2704,128]{1,0:T(8,128)(2,1)S(1)} %collective-permute-done.2.second_ref, bf16[2,416,416]{2,1,0:T(8,128)(2,1)S(1)} %shard_map.69.first_planes, bf16[2,2,416,416]{3,2,1,0:T(8,128)(2,1)S(1)} %get-tuple-element.35.lead_ref, ...), custom_call_target="tpu_custom_call" | custom-call | flops 1727791104 | bytes 1048576 | tf_op jit(solution)/shard_map/pallas_call | solution.py:416
  42.2 0.7 %collective-permute-start.7 = (bf16[2,2,64,128]{3,2,1,0:T(8,128)(2,1)S(1)}, bf16[2,2,64,128]{3,2,1,0:T(8,128)(2,1)S(1)}, u32[]{:S(2)}, u32[]{:S(2)}) collective-permute-start(bf16[2,2,64,128]{3,2,1,0:T(8,128)(2,1)S(1)} %get-tuple-element.44.rest_0_), channel_id=1, source_target_pairs={{8,16},{12,20},{16,8},{20,12},{9,17},{13,21},{17,9},{21,13},{10,18... | collective-permute-start | bytes 196616 | tf_op jit(solution)/shard_map/ppermute | solution.py:436
  42.9 3.7 %collective-permute-start.5 = (bf16[2,2,64,128]{3,2,1,0:T(8,128)(2,1)S(1)}, bf16[2,2,64,128]{3,2,1,0:T(8,128)(2,1)S(1)}, u32[]{:S(2)}, u32[]{:S(2)}) collective-permute-start(bf16[2,2,64,128]{3,2,1,0:T(8,128)(2,1)S(1)} %get-tuple-element.44.rest_0_), channel_id=1, source_target_pairs={{0,8},{4,12},{8,0},{12,4},{16,24},{20,28},{24,16},{28,20},{1,9},{5... | collective-permute-start | bytes 196616 | tf_op jit(solution)/shard_map/ppermute | solution.py:437
  46.6 2.4 %collective-permute-start.4 = (bf16[2,2,64,128]{3,2,1,0:T(8,128)(2,1)S(1)}, bf16[2,2,64,128]{3,2,1,0:T(8,128)(2,1)S(1)}, u32[]{:S(2)}, u32[]{:S(2)}) collective-permute-start(bf16[2,2,64,128]{3,2,1,0:T(8,128)(2,1)S(1)} %get-tuple-element.44.rest_0_), channel_id=1, source_target_pairs={{0,4},{4,0},{8,12},{12,8},{16,20},{20,16},{24,28},{28,24},{1,5},{5... | collective-permute-start | bytes 196616 | tf_op jit(solution)/shard_map/ppermute | solution.py:440
  49.0 0.0 collective-permute-done.7.rest_4_
  49.0 0.0 collective-permute-start.8
  49.0 0.0 collective-permute-done.5.rest_2_
  49.0 2.8 %collective-permute-start.6 = (bf16[2,2,64,128]{3,2,1,0:T(8,128)(2,1)S(1)}, bf16[2,2,64,128]{3,2,1,0:T(8,128)(2,1)S(1)}, u32[]{:S(2)}, u32[]{:S(2)}) collective-permute-start(bf16[2,2,64,128]{3,2,1,0:T(8,128)(2,1)S(1)} %collective-permute-done.5.rest_2_), channel_id=1, source_target_pairs={{0,4},{4,0},{8,12},{12,8},{16,20},{20,16},{24,28},{28,24},{1,5},{5... | collective-permute-start | bytes 196616 | tf_op jit(solution)/shard_map/ppermute | solution.py:440
  51.9 0.0 collective-permute-done.4.rest_1_
  51.9 0.0 collective-permute-done.8.rest_5_
  51.9 0.9 %collective-permute-done.6.rest_3_ = bf16[2,2,64,128]{3,2,1,0:T(8,128)(2,1)S(1)} collective-permute-done((bf16[2,2,64,128]{3,2,1,0:T(8,128)(2,1)S(1)}, bf16[2,2,64,128]{3,2,1,0:T(8,128)(2,1)S(1)}, u32[]{:S(2)}, u32[]{:S(2)}) %collective-permute-start.6) | collective-permute-done | bytes 65568 | tf_op jit(solution)/shard_map/ppermute | solution.py:440
  52.8 0.0 copy-done.1
  52.8 5.9 %shard_map.71 = bf16[2,1,2,416,416]{4,3,2,1,0:T(8,128)(2,1)} custom-call(s32[16]{0:T(128)S(1)} %copy-done.1, bf16[16,2,64,128]{3,2,1,0:T(8,128)(2,1)S(1)} %all_gather.3.samples_ref, s32[416,512]{1,0:T(8,128)S(1)} %get-tuple-element.33.slots_ref, bf16[2,416,416]{2,1,0:T(8,128)(2,1)S(1)} %get-tuple-element.38.green_even_ref, ...), custom_call_target="tpu_custom_call" | custom-call | flops 2303721472 | bytes 1048576 | tf_op jit(solution)/shard_map/pallas_call | solution.py:444
Async XLA Ops:
  0.0 14.4 %copy-start.2 = (s32[1,416,16]{1,2,0:T(8,128)S(1)}, s32[1,416,16]{1,2,0:T(8,128)}, u32[]{:S(2)}) copy-start(s32[1,416,16]{1,2,0:T(8,128)} %param.10) | copy-start | bytes 79876
  3.9 10.6 %copy-start = (bf16[2,1,2,6656]{3,2,1,0:T(2,128)(2,1)S(1)}, bf16[2,1,2,6656]{3,2,1,0:T(2,128)(2,1)}, u32[]{:S(2)}) copy-start(bf16[2,1,2,6656]{3,2,1,0:T(2,128)(2,1)} %phonon_ref.1) | copy-start | bytes 159748
  3.9 24.8 %collective-permute-start.1 = (bf16[2704,128]{1,0:T(8,128)(2,1)}, bf16[2704,128]{1,0:T(8,128)(2,1)S(1)}, u32[]{:S(2)}, u32[]{:S(2)}) collective-permute-start(bf16[2704,128]{1,0:T(8,128)(2,1)} %get-tuple-element.25), channel_id=1, source_target_pairs={{0,1},{1,0},{2,3},{3,2},{4,5},{5,4},{6,7},{7,6},{8,9},{9,8},{10,11... | collective-permute-start | bytes 2076680 | tf_op jit(solution)/shard_map/ppermute | solution.py:386
  5.3 23.7 %collective-permute-start = (bf16[2704,128]{1,0:T(8,128)(2,1)}, bf16[2704,128]{1,0:T(8,128)(2,1)}, u32[]{:S(2)}, u32[]{:S(2)}) collective-permute-start(bf16[2704,128]{1,0:T(8,128)(2,1)} %get-tuple-element.34), channel_id=1, source_target_pairs={{1,2},{2,1},{5,6},{6,5},{9,10},{10,9},{13,14},{14,13},{17,18},{18,... | collective-permute-start | bytes 2076680 | tf_op jit(solution)/shard_map/ppermute | solution.py:386
  10.9 24.5 %collective-permute-start.3 = (bf16[2704,128]{1,0:T(8,128)(2,1)}, bf16[2704,128]{1,0:T(8,128)(2,1)S(1)}, u32[]{:S(2)}, u32[]{:S(2)}) collective-permute-start(bf16[2704,128]{1,0:T(8,128)(2,1)} %get-tuple-element.28), channel_id=1, source_target_pairs={{0,1},{1,0},{2,3},{3,2},{4,5},{5,4},{6,7},{7,6},{8,9},{9,8},{10,11... | collective-permute-start | bytes 2076680 | tf_op jit(solution)/shard_map/ppermute | solution.py:386
  11.0 27.3 %collective-permute-start.2 = (bf16[2704,128]{1,0:T(8,128)(2,1)S(1)}, bf16[2704,128]{1,0:T(8,128)(2,1)S(1)}, u32[]{:S(2)}, u32[]{:S(2)}) collective-permute-start(bf16[2704,128]{1,0:T(8,128)(2,1)S(1)} %get-tuple-element.39), channel_id=1, source_target_pairs={{1,2},{2,1},{5,6},{6,5},{9,10},{10,9},{13,14},{14,13},{17,18},{18,... | collective-permute-start | bytes 2076680 | tf_op jit(solution)/shard_map/ppermute | solution.py:386
  35.7 17.1 %copy-start.1 = (s32[16]{0:T(128)S(1)}, s32[16]{0:T(128)}, u32[]{:S(2)}) copy-start(s32[16]{0:T(128)} %shifts_ref.1) | copy-start | bytes 196
  42.2 6.8 %collective-permute-start.7 = (bf16[2,2,64,128]{3,2,1,0:T(8,128)(2,1)S(1)}, bf16[2,2,64,128]{3,2,1,0:T(8,128)(2,1)S(1)}, u32[]{:S(2)}, u32[]{:S(2)}) collective-permute-start(bf16[2,2,64,128]{3,2,1,0:T(8,128)(2,1)S(1)} %get-tuple-element.44.rest_0_), channel_id=1, source_target_pairs={{8,16},{12,20},{16,8},{20,12},{9,17},{13,21},{17,9},{21,13},{10,18... | collective-permute-start | bytes 196616 | tf_op jit(solution)/shard_map/ppermute | solution.py:436
  42.9 6.2 %collective-permute-start.5 = (bf16[2,2,64,128]{3,2,1,0:T(8,128)(2,1)S(1)}, bf16[2,2,64,128]{3,2,1,0:T(8,128)(2,1)S(1)}, u32[]{:S(2)}, u32[]{:S(2)}) collective-permute-start(bf16[2,2,64,128]{3,2,1,0:T(8,128)(2,1)S(1)} %get-tuple-element.44.rest_0_), channel_id=1, source_target_pairs={{0,8},{4,12},{8,0},{12,4},{16,24},{20,28},{24,16},{28,20},{1,9},{5... | collective-permute-start | bytes 196616 | tf_op jit(solution)/shard_map/ppermute | solution.py:437
  46.6 5.3 %collective-permute-start.4 = (bf16[2,2,64,128]{3,2,1,0:T(8,128)(2,1)S(1)}, bf16[2,2,64,128]{3,2,1,0:T(8,128)(2,1)S(1)}, u32[]{:S(2)}, u32[]{:S(2)}) collective-permute-start(bf16[2,2,64,128]{3,2,1,0:T(8,128)(2,1)S(1)} %get-tuple-element.44.rest_0_), channel_id=1, source_target_pairs={{0,4},{4,0},{8,12},{12,8},{16,20},{20,16},{24,28},{28,24},{1,5},{5... | collective-permute-start | bytes 196616 | tf_op jit(solution)/shard_map/ppermute | solution.py:440
  49.0 2.9 %collective-permute-start.8 = (bf16[2,2,64,128]{3,2,1,0:T(8,128)(2,1)S(1)}, bf16[2,2,64,128]{3,2,1,0:T(8,128)(2,1)S(1)}, u32[]{:S(2)}, u32[]{:S(2)}) collective-permute-start(bf16[2,2,64,128]{3,2,1,0:T(8,128)(2,1)S(1)} %collective-permute-done.7.rest_4_), channel_id=1, source_target_pairs={{0,4},{4,0},{8,12},{12,8},{16,20},{20,16},{24,28},{28,24},{1,5},{5... | collective-permute-start | bytes 196616 | tf_op jit(solution)/shard_map/ppermute | solution.py:440
  49.0 3.7 %collective-permute-start.6 = (bf16[2,2,64,128]{3,2,1,0:T(8,128)(2,1)S(1)}, bf16[2,2,64,128]{3,2,1,0:T(8,128)(2,1)S(1)}, u32[]{:S(2)}, u32[]{:S(2)}) collective-permute-start(bf16[2,2,64,128]{3,2,1,0:T(8,128)(2,1)S(1)} %collective-permute-done.5.rest_2_), channel_id=1, source_target_pairs={{0,4},{4,0},{8,12},{12,8},{16,20},{20,16},{24,28},{28,24},{1,5},{5... | collective-permute-start | bytes 196616 | tf_op jit(solution)/shard_map/ppermute | solution.py:440

commit v3 on v2

--- a/solution.py
+++ b/solution.py
@@ -40,17 +40,22 @@
     return 2 * orbitals * orbitals // LANES
 
 
-def pack_planes(out_ref, planes):
+def pack_planes(out_ref, planes, place):
+    orbitals = planes[0].shape[0]
+    whole = orbitals // LANES
+    for c, plane in enumerate(planes, place):
+        for t in range(whole):
+            out_ref[pl.ds((c * whole + t) * orbitals, orbitals), :] = plane[
+                :, t * LANES : (t + 1) * LANES
+            ]
+
+
+def pack_tails(out_ref, planes):
     orbitals = planes[0].shape[0]
     whole = orbitals // LANES
     rest = orbitals - whole * LANES
     pieces = LANES // rest // 2
     height = orbitals // pieces
-    for c, plane in enumerate(planes):
-        for t in range(whole):
-            out_ref[pl.ds((c * whole + t) * orbitals, orbitals), :] = plane[
-                :, t * LANES : (t + 1) * LANES
-            ]
     tails = [
         plane[h * height : (h + 1) * height, whole * LANES :]
         for plane in planes
@@ -79,31 +84,51 @@
 
 
 def send_kernel(
-    e, inverses_ref, coupling_ref, first_ref, second_ref, inverse, right_self, coupling, sems
+    e, inverses_ref, coupling_ref, first_ref, second_ref,
+    inverse, coupling, up, down, sems, up_sem, down_sems,
 ):
     copies = [pltpu.make_async_copy(coupling_ref.at[0], coupling, sems.at[2])]
     for c in range(2):
         copies.append(pltpu.make_async_copy(inverses_ref.at[e, 0, c], inverse.at[c], sems.at[c]))
     for copy in copies:
         copy.start()
+    even = lax.axis_index("domain") % 2 == 0
+    split = inverse.shape[1] * (inverse.shape[2] // LANES)
+
+    def on_parity(act):
+        for parity, next_ref, before_ref in ((True, first_ref, second_ref), (False, second_ref, first_ref)):
+
+            @pl.when(even == parity)
+            def _():
+                act(
+                    pltpu.make_async_copy(up, next_ref, up_sem),
+                    pltpu.make_async_copy(
+                        down.at[pl.ds(0, split)], before_ref.at[pl.ds(0, split)], down_sems.at[0]
+                    ),
+                    pltpu.make_async_copy(
+                        down.at[pl.ds(split, down.shape[0] - split)],
+                        before_ref.at[pl.ds(split, down.shape[0] - split)],
+                        down_sems.at[1],
+                    ),
+                )
+
+    def right_self(c):
+        right_product = product_nt(inverse[c], coupling[...]).astype(jnp.bfloat16)
+        return product(coupling[...], right_product).astype(jnp.bfloat16)
+
     copies[0].wait()
-    for c in range(2):
-        copies[1 + c].wait()
-        right_product = product_nt(inverse[c], coupling[...]).astype(jnp.bfloat16)
-        right_self[c] = product(coupling[...], right_product).astype(jnp.bfloat16)
-    even = lax.axis_index("domain") % 2 == 0
-
-    def pack(next_ref, before_ref):
-        pack_planes(next_ref, [inverse[c] for c in range(2)])
-        pack_planes(before_ref, [right_self[c] for c in range(2)])
-
-    @pl.when(even)
-    def _():
-        pack(first_ref, second_ref)
-
-    @pl.when(jnp.logical_not(even))
-    def _():
-        pack(second_ref, first_ref)
+    copies[1].wait()
+    real = right_self(0)
+    pack_planes(down, [real], 0)
+    copies[2].wait()
+    pack_planes(up, [inverse[0], inverse[1]], 0)
+    pack_tails(up, [inverse[0], inverse[1]])
+    on_parity(lambda whole, head, tail: (whole.start(), head.start()))
+    imag = right_self(1)
+    pack_planes(down, [imag], 1)
+    pack_tails(down, [real, imag])
+    on_parity(lambda whole, head, tail: tail.start())
+    on_parity(lambda whole, head, tail: (whole.wait(), head.wait(), tail.wait()))
 
 
 def group_iotas():
@@ -185,12 +210,12 @@
 
 
 def green_kernel(
-    e, width, second_ref, first_planes, lead_ref, inverses_ref, coupling_ref, columns_ref, *rest
+    width, second_ref, first_planes, lead_ref, inverses_ref, coupling_ref, columns_ref,
+    green_ref, pair_ref, previous, right_self, inverse, wide, flat, sems,
 ):
-    *pair_before, green_ref, pair_ref, previous, right_self, inverse, wide, flat, sems = rest
     orbitals = inverse.shape[1]
     copies = [
-        pltpu.make_async_copy(inverses_ref.at[e, 0, c], inverse.at[c], sems.at[c]) for c in range(2)
+        pltpu.make_async_copy(inverses_ref.at[0, 0, c], inverse.at[c], sems.at[c]) for c in range(2)
     ]
     for copy in copies:
         copy.start()
@@ -199,7 +224,7 @@
 
     @pl.when(domain == 0)
     def _():
-        previous[...] = lead_ref[e]
+        previous[...] = lead_ref[0]
 
     @pl.when(even & (domain > 0))
     def _():
@@ -230,9 +255,94 @@
         green = (own[c].astype(jnp.float32) + part).astype(jnp.bfloat16)
         green_ref[c] = green
         wide[c, :, :orbitals] = green.astype(jnp.float32)
-    for k, ref in enumerate(pair_before):
-        pair_ref[k] = ref[0]
-    gather_pairs(width, wide, columns_ref, flat, pair_ref, len(pair_before))
+    gather_pairs(width, wide, columns_ref, flat, pair_ref, 0)
+
+
+def sides_kernel(inverses_ref, coupling_ref, before_ref, after_ref, inverse_ref, sems):
+    last = inverses_ref.shape[0] - 1
+    copies = [
+        pltpu.make_async_copy(inverses_ref.at[last, 0, c], inverse_ref.at[c], sems.at[c])
+        for c in range(2)
+    ]
+    for copy in copies:
+        copy.start()
+    coupling = coupling_ref[0]
+    for c in range(2):
+        copies[c].wait()
+        before_ref[c] = product_nt(inverse_ref[c], coupling).astype(jnp.bfloat16)
+        after_ref[c] = product(coupling, inverse_ref[c]).astype(jnp.bfloat16)
+
+
+def add_side(left, value, middle, right):
+    inner = complex_product([middle[c] for c in range(2)], [right[c] for c in range(2)])
+    outer = complex_product(
+        [left[c] for c in range(2)], [part.astype(jnp.bfloat16) for part in inner]
+    )
+    return [value[c].astype(jnp.float32) + outer[c] for c in range(2)]
+
+
+def early_kernel(
+    first_planes, lead_ref, before_ref, after_ref, inverse_ref, sum_ref
+):
+    domain = lax.axis_index("domain")
+    none = (domain % 2 == 1) & (domain == lax.axis_size("domain") - 1)
+
+    def write(values):
+        for c in range(2):
+            sum_ref[c] = values[c]
+
+    @pl.when(domain == 0)
+    def _():
+        lead = lead_ref[lead_ref.shape[0] - 1]
+        write(add_side(before_ref, inverse_ref, lead, after_ref))
+
+    @pl.when((domain % 2 == 1) & jnp.logical_not(none))
+    def _():
+        write(add_side(before_ref, inverse_ref, first_planes, after_ref))
+
+    @pl.when((domain % 2 == 0) & (domain > 0))
+    def _():
+        write(add_side(inverse_ref, inverse_ref, first_planes, inverse_ref))
+
+    @pl.when(none)
+    def _():
+        write([inverse_ref[c].astype(jnp.float32) for c in range(2)])
+
+
+def late_kernel(
+    width, second_ref, first_planes, before_ref, after_ref, inverse_ref, sum_ref, columns_ref, pair_before,
+    green_ref, pair_ref, middle, wide, flat,
+):
+    orbitals = inverse_ref.shape[1]
+    domain = lax.axis_index("domain")
+    ends = (domain == 0) | ((domain % 2 == 1) & (domain == lax.axis_size("domain") - 1))
+
+    @pl.when(ends)
+    def _():
+        middle[...] = first_planes[...]
+
+    @pl.when(jnp.logical_not(ends))
+    def _():
+        unpack_planes(second_ref, middle)
+
+    from_before = (domain > 0) & ((domain % 2 == 0) | ends)
+
+    def write(values):
+        for c in range(2):
+            green = values[c].astype(jnp.bfloat16)
+            green_ref[c] = green
+            wide[c, :, :orbitals] = green.astype(jnp.float32)
+
+    @pl.when(from_before)
+    def _():
+        write(add_side(before_ref, sum_ref, middle, after_ref))
+
+    @pl.when(jnp.logical_not(from_before))
+    def _():
+        write(add_side(inverse_ref, sum_ref, middle, inverse_ref))
+
+    pair_ref[0] = pair_before[0]
+    gather_pairs(width, wide, columns_ref, flat, pair_ref, 1)
 
 
 def gather_pairs(width, wide, columns_ref, flat, pair_ref, place):
@@ -377,11 +487,15 @@
             [IN_HBM] * 2,
             [
                 pltpu.VMEM((2, *plane), bf16),
-                pltpu.VMEM((2, *plane), bf16),
                 pltpu.VMEM(plane, bf16),
+                pltpu.VMEM((rows, LANES), bf16),
+                pltpu.VMEM((rows, LANES), bf16),
                 pltpu.SemaphoreType.DMA((3,)),
+                pltpu.SemaphoreType.DMA,
+                pltpu.SemaphoreType.DMA((2,)),
             ],
             flops=4 * cube,
+            out_spec=(IN_HBM,) * 2,
         )(barred, in_hbm[1])
         received.append([lax.ppermute(x, "domain", route) for x, route in zip(sent, routes)])
         barred, neighbors, _ = lax.optimization_barrier((barred, neighbors, sent[0]))
@@ -407,30 +521,54 @@
     samples = lax.all_gather(samples, "energy", axis=0, tiled=True)
     columns, samples = lax.optimization_barrier((columns, samples))
 
-    greens, pairs = [], []
-    for e in range(energies):
-        first, second = received[e]
-        if e:
-            first, *pairs = lax.optimization_barrier((first, *pairs))
-        first = call(unpack_kernel, shape((2, *plane), bf16), [IN_VMEM])(first)
-        green, pair = call(
-            functools.partial(green_kernel, e, width),
-            (shape((2, *plane), bf16), shape((1 + e, 2, height, LANES), bf16)),
-            [IN_VMEM] * 3 + [IN_HBM] + [IN_VMEM] * (2 + e),
-            [
-                pltpu.VMEM((2, *plane), bf16),
-                pltpu.VMEM((2, *plane), bf16),
-                pltpu.VMEM((2, *plane), bf16),
-                pltpu.VMEM((2, orbitals, padded), f32),
-                pltpu.VMEM((2, height, LANES), f32),
-                pltpu.SemaphoreType.DMA((2,)),
-            ],
-            flops=12 * cube,
-            limit=12,
-        )(second, first, lead, in_hbm[0], coupling, columns, *pairs)
-        greens.append(green)
-        pairs.append(pair)
-    pair = pairs[-1]
+    pair_shape = (1, 2, height, LANES)
+    block = shape((2, *plane), bf16)
+    before, after, inverse = call(
+        sides_kernel,
+        (block,) * 3,
+        [IN_HBM, IN_VMEM],
+        [pltpu.SemaphoreType.DMA((2,))],
+        flops=4 * cube,
+    )(in_hbm[0], coupling)
+
+    def unpacked(first):
+        return call(unpack_kernel, block, [IN_VMEM])(first)
+
+    first, second = received[0]
+    green_even, pair = call(
+        functools.partial(green_kernel, width),
+        (block, shape(pair_shape, bf16)),
+        [IN_VMEM] * 3 + [IN_HBM] + [IN_VMEM] * 2,
+        [
+            pltpu.VMEM((2, *plane), bf16),
+            pltpu.VMEM((2, *plane), bf16),
+            pltpu.VMEM((2, *plane), bf16),
+            pltpu.VMEM((2, orbitals, padded), f32),
+            pltpu.VMEM((2, height, LANES), f32),
+            pltpu.SemaphoreType.DMA((2,)),
+        ],
+        flops=12 * cube,
+        limit=12,
+    )(second, unpacked(first), lead, in_hbm[0], coupling, columns)
+
+    first, second = received[1]
+    first, pair = lax.optimization_barrier((first, pair))
+    first = unpacked(first)
+    partial_sum = call(
+        early_kernel, shape((2, *plane), f32), [IN_VMEM] * 5, flops=6 * cube, limit=12
+    )(first, lead, before, after, inverse)
+    green_odd, pair = call(
+        functools.partial(late_kernel, width),
+        (block, shape((2, *pair_shape[1:]), bf16)),
+        [IN_VMEM] * 8,
+        [
+            pltpu.VMEM((2, *plane), bf16),
+            pltpu.VMEM((2, orbitals, padded), f32),
+            pltpu.VMEM((2, height, LANES), f32),
+        ],
+        flops=6 * cube,
+        limit=12,
+    )(second, first, before, after, inverse, partial_sum, columns, pair)
     devices = lax.axis_size("energy")
     if devices == 8 and energies == 2:
         across = lax.ppermute(pair, "energy", [(i, i ^ 6) for i in range(2, 6)])
@@ -455,7 +593,7 @@
         flops=16 * cube,
         out_spec=IN_HBM,
         limit=16,
-    )(shifts, samples, slots, *greens, *sources)
+    )(shifts, samples, slots, green_even, green_odd, *sources)
 
 
 def solution(mesh):

time: 59.2 us -> 57.4 us (0.970)
  waiting for transfers between devices: 5.11 us -> 0.92 us
  Pallas kernels: 25.7 us -> 27.4 us
  starting transfers between devices: 16.4 us -> 17.1 us
    ppermute x4, waiting for transfers between devices: 4.2 us -> 0.01 us  [body(): lax.ppermute(x, 'domain', route)]
    pallas_call x4 -> x6, Pallas kernels: 9.19 us -> 11.9 us  [the longest x1 4.78 us: body(): call(functools.partial(green_kernel, width), (block, shape(pair_shape, bf...]
    pallas_call x2, Pallas kernels: 7.63 us -> 6.63 us  [body(): call(functools.partial(send_kernel, e), (shape((rows, LANES), bf16), shap...]
    ppermute x4, starting transfers between devices: 6.7 us -> 7.53 us  [body(): lax.ppermute(x, 'domain', route)]
  transfers between devices with their start and end apart: 9 -> 9, of which waited for: 3 -> 1; matrix products, arithmetic and copies ran while one was open for 0% -> 0% of each run, Pallas kernels for 20% -> 27%
where the time goes in v3:
time: 57.4 us; the launch traced here: 57.1 us
  Pallas kernels  27.4 us (48%)
  starting transfers between devices  17.1 us (30%)
  blocking collectives  11.2 us (20%)
  waiting for transfers between devices  0.92 us (2%)
    all_gather x1, blocking collectives, body(): samples = lax.all_gather(samples, 'energy', axis=0, tiled=True)  11.2 us
    ppermute x4, starting transfers between devices, body(): lax.ppermute(x, 'domain', route)  7.53 us
    pallas_call x2, Pallas kernels, body(): call(functools.partial(send_kernel, e), (shape((rows, LANES), bf16), shap...  6.63 us
    pallas_call x1, Pallas kernels, body(): call(final_kernel, shape((energies, 1, 2, *plane), bf16), [IN_SMEM] + [IN...  5.89 us
    ppermute x3, starting transfers between devices, body(): lax.ppermute(array, 'energy', [(i, i ^ 1) for i in range(8)])  5.19 us
    pallas_call x1, Pallas kernels, body(): call(functools.partial(green_kernel, width), (block, shape(pair_shape, bf...  4.78 us
    ppermute x1, starting transfers between devices, body(): beside = lax.ppermute(pair, 'energy', [(i, i ^ 2) for i in range(8)])  3.71 us
    pallas_call x1, Pallas kernels, body(): call(functools.partial(table_kernel, width), (shape((orbitals, LANES), jn...  2.99 us
  transfers between devices with their start and end apart: 9, of which 1 were waited for; matrix products, arithmetic and copies ran while one was open for 0% of the time, Pallas kernels for 27%

profile of v3, /device:TPU:17, one launch (start us, length us, event | category | flops | bytes accessed | tf_op | source)
XLA Modules:
  0.0 57.1 jit_solution(12458640496477746837)
XLA Ops:
  0.0 0.0 copy-start.2
  0.0 3.5 %shard_map.64 = (bf16[2704,128]{1,0:T(8,128)(2,1)}, bf16[2704,128]{1,0:T(8,128)(2,1)}) custom-call(bf16[2,1,2,416,416]{4,3,2,1,0:T(8,128)(2,1)} %inverses_ref.6, bf16[1,416,416]{2,1,0:T(8,128)(2,1)} %coupling_ref.5), custom_call_target="tpu_custom_call" | custom-call | flops 575930368 | bytes 1048576 | tf_op jit(solution)/shard_map/pallas_call | solution.py:484
  3.5 0.0 copy-start
  3.5 1.4 %collective-permute-start.1 = (bf16[2704,128]{1,0:T(8,128)(2,1)}, bf16[2704,128]{1,0:T(8,128)(2,1)S(1)}, u32[]{:S(2)}, u32[]{:S(2)}) collective-permute-start(bf16[2704,128]{1,0:T(8,128)(2,1)} %get-tuple-element.28), channel_id=1, source_target_pairs={{0,1},{1,0},{2,3},{3,2},{4,5},{5,4},{6,7},{7,6},{8,9},{9,8},{10,11... | collective-permute-start | bytes 2076680 | tf_op jit(solution)/shard_map/ppermute | solution.py:500
  4.9 1.9 %collective-permute-start = (bf16[2704,128]{1,0:T(8,128)(2,1)}, bf16[2704,128]{1,0:T(8,128)(2,1)}, u32[]{:S(2)}, u32[]{:S(2)}) collective-permute-start(bf16[2704,128]{1,0:T(8,128)(2,1)} %get-tuple-element.37), channel_id=1, source_target_pairs={{1,2},{2,1},{5,6},{6,5},{9,10},{10,9},{13,14},{14,13},{17,18},{18,... | collective-permute-start | bytes 2076680 | tf_op jit(solution)/shard_map/ppermute | solution.py:500
  6.8 3.1 %shard_map.65 = (bf16[2704,128]{1,0:T(8,128)(2,1)}, bf16[2704,128]{1,0:T(8,128)(2,1)S(1)}) custom-call(bf16[2,1,2,416,416]{4,3,2,1,0:T(8,128)(2,1)} %inverses_ref.6, bf16[1,416,416]{2,1,0:T(8,128)(2,1)} %coupling_ref.5), custom_call_target="tpu_custom_call" | custom-call | flops 575930368 | bytes 1048576 | tf_op jit(solution)/shard_map/pallas_call | solution.py:484
  10.0 0.5 collective-permute-start.3
  10.5 3.7 %collective-permute-start.2 = (bf16[2704,128]{1,0:T(8,128)(2,1)S(1)}, bf16[2704,128]{1,0:T(8,128)(2,1)S(1)}, u32[]{:S(2)}, u32[]{:S(2)}) collective-permute-start(bf16[2704,128]{1,0:T(8,128)(2,1)S(1)} %get-tuple-element.42), channel_id=1, source_target_pairs={{1,2},{2,1},{5,6},{6,5},{9,10},{10,9},{13,14},{14,13},{17,18},{18,... | collective-permute-start | bytes 2076680 | tf_op jit(solution)/shard_map/ppermute | solution.py:500
  14.2 0.0 copy-done.2
  14.2 0.1 copy.8.neighbors_ref
  14.3 0.0 copy-done
  14.4 3.0 %shard_map.66 = (s32[416,128]{1,0:T(8,128)S(1)}, s32[416,512]{1,0:T(8,128)S(1)}, bf16[2,2,64,128]{3,2,1,0:T(8,128)(2,1)S(1)}, bf16[2,2,416,416]{3,2,1,0:T(8,128)(2,1)S(1)}, bf16[1,416,416]{2,1,0:T(8,128)(2,1)S(1)}) custom-call(s32[1,416,16]{2,1,0:T(8,128)S(1)} %copy.8.neighbors_ref, bf16[2,1,2,6656]{3,2,1,0:T(2,128)(2,1)S(1)} %copy-done, ...), custom_call_target="tpu_custom_call" | custom-call | flops 575930368 | bytes 1048576 | tf_op jit(solution)/shard_map/pallas_call | solution.py:503
  17.3 11.2 %all_gather.3.samples_ref = bf16[16,2,64,128]{3,2,1,0:T(8,128)(2,1)S(1)} all-gather(bf16[2,2,64,128]{3,2,1,0:T(8,128)(2,1)S(1)} %get-tuple-element.34), channel_id=1, replica_groups=mesh['energy'=8,'domain'=4] {'energy'}, dimensions={0}, use_global_device_ids=true | all-gather | bytes 589824 | tf_op jit(solution)/shard_map/all_gather | solution.py:521
  28.6 2.3 %shard_map.70 = (bf16[2,416,416]{2,1,0:T(8,128)(2,1)S(1)}, bf16[2,416,416]{2,1,0:T(8,128)(2,1)S(1)}, bf16[2,416,416]{2,1,0:T(8,128)(2,1)S(1)}) custom-call(bf16[2,1,2,416,416]{4,3,2,1,0:T(8,128)(2,1)} %inverses_ref.6, bf16[1,416,416]{2,1,0:T(8,128)(2,1)S(1)} %get-tuple-element.39.coupling_ref), custom_call_target="tpu_custom_call" | custom-call | flops 575930368 | bytes 1048576 | tf_op jit(solution)/shard_map/pallas_call | solution.py:526
  30.9 0.0 collective-permute-done.1.packed_ref
  30.9 0.3 shard_map.67.first_planes
  31.2 0.0 collective-permute-done.second_ref
  31.2 4.8 %shard_map.68 = (bf16[2,416,416]{2,1,0:T(8,128)(2,1)S(1)}, bf16[1,2,64,128]{3,2,1,0:T(8,128)(2,1)S(1)}) custom-call(bf16[2704,128]{1,0:T(8,128)(2,1)} %collective-permute-done.second_ref, bf16[2,416,416]{2,1,0:T(8,128)(2,1)S(1)} %shard_map.67.first_planes, bf16[2,2,416,416]{3,2,1,0:T(8,128)(2,1)S(1)} %get-tuple-element.38.lead_ref, ...), custom_call_target="tpu_custom_call" | custom-call | flops 1727791104 | bytes 1048576 | tf_op jit(solution)/shard_map/pallas_call | solution.py:538
  36.0 0.0 collective-permute-done.3.packed_ref
  36.0 0.3 shard_map.69.first_planes
  36.2 1.7 %shard_map.71.sum_ref = f32[2,416,416]{2,1,0:T(8,128)S(1)} custom-call(bf16[2,416,416]{2,1,0:T(8,128)(2,1)S(1)} %shard_map.69.first_planes, bf16[2,2,416,416]{3,2,1,0:T(8,128)(2,1)S(1)} %get-tuple-element.38.lead_ref, bf16[2,416,416]{2,1,0:T(8,128)(2,1)S(1)} %get-tuple-element.45.before_ref, bf16[2,416,416]{2,1,0:T(8,128)(2,1)S(1)} %get-tuple-element.46.after_ref, ...), custom_call_target="tpu_custom_call" | custom-call | flops 863895552 | bytes 1048576 | tf_op jit(solution)/shard_map/pallas_call | solution.py:557
  38.0 0.0 copy-start.1
  38.0 0.0 collective-permute-done.2.second_ref
  38.0 2.6 %shard_map.72 = (bf16[2,416,416]{2,1,0:T(8,128)(2,1)S(1)}, bf16[2,2,64,128]{3,2,1,0:T(8,128)(2,1)S(1)}) custom-call(bf16[2704,128]{1,0:T(8,128)(2,1)S(1)} %collective-permute-done.2.second_ref, bf16[2,416,416]{2,1,0:T(8,128)(2,1)S(1)} %shard_map.69.first_planes, bf16[2,416,416]{2,1,0:T(8,128)(2,1)S(1)} %get-tuple-element.45.before_ref, ...), custom_call_target="tpu_custom_call" | custom-call | flops 863895552 | bytes 1048576 | tf_op jit(solution)/shard_map/pallas_call | solution.py:560
  40.6 0.7 %collective-permute-start.7 = (bf16[2,2,64,128]{3,2,1,0:T(8,128)(2,1)S(1)}, bf16[2,2,64,128]{3,2,1,0:T(8,128)(2,1)S(1)}, u32[]{:S(2)}, u32[]{:S(2)}) collective-permute-start(bf16[2,2,64,128]{3,2,1,0:T(8,128)(2,1)S(1)} %get-tuple-element.50.rest_0_), channel_id=1, source_target_pairs={{8,16},{12,20},{16,8},{20,12},{9,17},{13,21},{17,9},{21,13},{10,18... | collective-permute-start | bytes 196616 | tf_op jit(solution)/shard_map/ppermute | solution.py:574
  41.2 3.7 %collective-permute-start.5 = (bf16[2,2,64,128]{3,2,1,0:T(8,128)(2,1)S(1)}, bf16[2,2,64,128]{3,2,1,0:T(8,128)(2,1)S(1)}, u32[]{:S(2)}, u32[]{:S(2)}) collective-permute-start(bf16[2,2,64,128]{3,2,1,0:T(8,128)(2,1)S(1)} %get-tuple-element.50.rest_0_), channel_id=1, source_target_pairs={{0,8},{4,12},{8,0},{12,4},{16,24},{20,28},{24,16},{28,20},{1,9},{5... | collective-permute-start | bytes 196616 | tf_op jit(solution)/shard_map/ppermute | solution.py:575
  44.9 2.3 %collective-permute-start.4 = (bf16[2,2,64,128]{3,2,1,0:T(8,128)(2,1)S(1)}, bf16[2,2,64,128]{3,2,1,0:T(8,128)(2,1)S(1)}, u32[]{:S(2)}, u32[]{:S(2)}) collective-permute-start(bf16[2,2,64,128]{3,2,1,0:T(8,128)(2,1)S(1)} %get-tuple-element.50.rest_0_), channel_id=1, source_target_pairs={{0,4},{4,0},{8,12},{12,8},{16,20},{20,16},{24,28},{28,24},{1,5},{5... | collective-permute-start | bytes 196616 | tf_op jit(solution)/shard_map/ppermute | solution.py:578
  47.3 0.0 collective-permute-done.7.rest_4_
  47.3 0.0 collective-permute-start.8
  47.3 0.0 collective-permute-done.5.rest_2_
  47.3 2.8 %collective-permute-start.6 = (bf16[2,2,64,128]{3,2,1,0:T(8,128)(2,1)S(1)}, bf16[2,2,64,128]{3,2,1,0:T(8,128)(2,1)S(1)}, u32[]{:S(2)}, u32[]{:S(2)}) collective-permute-start(bf16[2,2,64,128]{3,2,1,0:T(8,128)(2,1)S(1)} %collective-permute-done.5.rest_2_), channel_id=1, source_target_pairs={{0,4},{4,0},{8,12},{12,8},{16,20},{20,16},{24,28},{28,24},{1,5},{5... | collective-permute-start | bytes 196616 | tf_op jit(solution)/shard_map/ppermute | solution.py:578
  50.1 0.0 collective-permute-done.4.rest_1_
  50.1 0.0 collective-permute-done.8.rest_5_
  50.2 0.9 %collective-permute-done.6.rest_3_ = bf16[2,2,64,128]{3,2,1,0:T(8,128)(2,1)S(1)} collective-permute-done((bf16[2,2,64,128]{3,2,1,0:T(8,128)(2,1)S(1)}, bf16[2,2,64,128]{3,2,1,0:T(8,128)(2,1)S(1)}, u32[]{:S(2)}, u32[]{:S(2)}) %collective-permute-start.6) | collective-permute-done | bytes 65568 | tf_op jit(solution)/shard_map/ppermute | solution.py:578
  51.0 0.0 copy-done.1
  51.1 5.9 %shard_map.73 = bf16[2,1,2,416,416]{4,3,2,1,0:T(8,128)(2,1)} custom-call(s32[16]{0:T(128)S(1)} %copy-done.1, bf16[16,2,64,128]{3,2,1,0:T(8,128)(2,1)S(1)} %all_gather.3.samples_ref, s32[416,512]{1,0:T(8,128)S(1)} %get-tuple-element.36.slots_ref, bf16[2,416,416]{2,1,0:T(8,128)(2,1)S(1)} %get-tuple-element.41.green_even_ref, ...), custom_call_target="tpu_custom_call" | custom-call | flops 2303721472 | bytes 1048576 | tf_op jit(solution)/shard_map/pallas_call | solution.py:582
Async XLA Ops:
  0.0 14.2 %copy-start.2 = (s32[1,416,16]{1,2,0:T(8,128)S(1)}, s32[1,416,16]{1,2,0:T(8,128)}, u32[]{:S(2)}) copy-start(s32[1,416,16]{1,2,0:T(8,128)} %param.10) | copy-start | bytes 79876
  3.5 10.9 %copy-start = (bf16[2,1,2,6656]{3,2,1,0:T(2,128)(2,1)S(1)}, bf16[2,1,2,6656]{3,2,1,0:T(2,128)(2,1)}, u32[]{:S(2)}) copy-start(bf16[2,1,2,6656]{3,2,1,0:T(2,128)(2,1)} %phonon_ref.1) | copy-start | bytes 159748
  3.5 27.4 %collective-permute-start.1 = (bf16[2704,128]{1,0:T(8,128)(2,1)}, bf16[2704,128]{1,0:T(8,128)(2,1)S(1)}, u32[]{:S(2)}, u32[]{:S(2)}) collective-permute-start(bf16[2704,128]{1,0:T(8,128)(2,1)} %get-tuple-element.28), channel_id=1, source_target_pairs={{0,1},{1,0},{2,3},{3,2},{4,5},{5,4},{6,7},{7,6},{8,9},{9,8},{10,11... | collective-permute-start | bytes 2076680 | tf_op jit(solution)/shard_map/ppermute | solution.py:500
  4.9 26.2 %collective-permute-start = (bf16[2704,128]{1,0:T(8,128)(2,1)}, bf16[2704,128]{1,0:T(8,128)(2,1)}, u32[]{:S(2)}, u32[]{:S(2)}) collective-permute-start(bf16[2704,128]{1,0:T(8,128)(2,1)} %get-tuple-element.37), channel_id=1, source_target_pairs={{1,2},{2,1},{5,6},{6,5},{9,10},{10,9},{13,14},{14,13},{17,18},{18,... | collective-permute-start | bytes 2076680 | tf_op jit(solution)/shard_map/ppermute | solution.py:500
  10.0 26.0 %collective-permute-start.3 = (bf16[2704,128]{1,0:T(8,128)(2,1)}, bf16[2704,128]{1,0:T(8,128)(2,1)S(1)}, u32[]{:S(2)}, u32[]{:S(2)}) collective-permute-start(bf16[2704,128]{1,0:T(8,128)(2,1)} %get-tuple-element.31), channel_id=1, source_target_pairs={{0,1},{1,0},{2,3},{3,2},{4,5},{5,4},{6,7},{7,6},{8,9},{9,8},{10,11... | collective-permute-start | bytes 2076680 | tf_op jit(solution)/shard_map/ppermute | solution.py:500
  10.5 27.5 %collective-permute-start.2 = (bf16[2704,128]{1,0:T(8,128)(2,1)S(1)}, bf16[2704,128]{1,0:T(8,128)(2,1)S(1)}, u32[]{:S(2)}, u32[]{:S(2)}) collective-permute-start(bf16[2704,128]{1,0:T(8,128)(2,1)S(1)} %get-tuple-element.42), channel_id=1, source_target_pairs={{1,2},{2,1},{5,6},{6,5},{9,10},{10,9},{13,14},{14,13},{17,18},{18,... | collective-permute-start | bytes 2076680 | tf_op jit(solution)/shard_map/ppermute | solution.py:500
  38.0 13.1 %copy-start.1 = (s32[16]{0:T(128)S(1)}, s32[16]{0:T(128)}, u32[]{:S(2)}) copy-start(s32[16]{0:T(128)} %shifts_ref.1) | copy-start | bytes 196
  40.6 6.7 %collective-permute-start.7 = (bf16[2,2,64,128]{3,2,1,0:T(8,128)(2,1)S(1)}, bf16[2,2,64,128]{3,2,1,0:T(8,128)(2,1)S(1)}, u32[]{:S(2)}, u32[]{:S(2)}) collective-permute-start(bf16[2,2,64,128]{3,2,1,0:T(8,128)(2,1)S(1)} %get-tuple-element.50.rest_0_), channel_id=1, source_target_pairs={{8,16},{12,20},{16,8},{20,12},{9,17},{13,21},{17,9},{21,13},{10,18... | collective-permute-start | bytes 196616 | tf_op jit(solution)/shard_map/ppermute | solution.py:574
  41.2 6.1 %collective-permute-start.5 = (bf16[2,2,64,128]{3,2,1,0:T(8,128)(2,1)S(1)}, bf16[2,2,64,128]{3,2,1,0:T(8,128)(2,1)S(1)}, u32[]{:S(2)}, u32[]{:S(2)}) collective-permute-start(bf16[2,2,64,128]{3,2,1,0:T(8,128)(2,1)S(1)} %get-tuple-element.50.rest_0_), channel_id=1, source_target_pairs={{0,8},{4,12},{8,0},{12,4},{16,24},{20,28},{24,16},{28,20},{1,9},{5... | collective-permute-start | bytes 196616 | tf_op jit(solution)/shard_map/ppermute | solution.py:575
  44.9 5.2 %collective-permute-start.4 = (bf16[2,2,64,128]{3,2,1,0:T(8,128)(2,1)S(1)}, bf16[2,2,64,128]{3,2,1,0:T(8,128)(2,1)S(1)}, u32[]{:S(2)}, u32[]{:S(2)}) collective-permute-start(bf16[2,2,64,128]{3,2,1,0:T(8,128)(2,1)S(1)} %get-tuple-element.50.rest_0_), channel_id=1, source_target_pairs={{0,4},{4,0},{8,12},{12,8},{16,20},{20,16},{24,28},{28,24},{1,5},{5... | collective-permute-start | bytes 196616 | tf_op jit(solution)/shard_map/ppermute | solution.py:578
  47.3 2.9 %collective-permute-start.8 = (bf16[2,2,64,128]{3,2,1,0:T(8,128)(2,1)S(1)}, bf16[2,2,64,128]{3,2,1,0:T(8,128)(2,1)S(1)}, u32[]{:S(2)}, u32[]{:S(2)}) collective-permute-start(bf16[2,2,64,128]{3,2,1,0:T(8,128)(2,1)S(1)} %collective-permute-done.7.rest_4_), channel_id=1, source_target_pairs={{0,4},{4,0},{8,12},{12,8},{16,20},{20,16},{24,28},{28,24},{1,5},{5... | collective-permute-start | bytes 196616 | tf_op jit(solution)/shard_map/ppermute | solution.py:578
  47.3 3.7 %collective-permute-start.6 = (bf16[2,2,64,128]{3,2,1,0:T(8,128)(2,1)S(1)}, bf16[2,2,64,128]{3,2,1,0:T(8,128)(2,1)S(1)}, u32[]{:S(2)}, u32[]{:S(2)}) collective-permute-start(bf16[2,2,64,128]{3,2,1,0:T(8,128)(2,1)S(1)} %collective-permute-done.5.rest_2_), channel_id=1, source_target_pairs={{0,4},{4,0},{8,12},{12,8},{16,20},{20,16},{24,28},{28,24},{1,5},{5... | collective-permute-start | bytes 196616 | tf_op jit(solution)/shard_map/ppermute | solution.py:578

commit v4 on v3

--- a/solution.py
+++ b/solution.py
@@ -211,7 +211,7 @@
 
 def green_kernel(
     width, second_ref, first_planes, lead_ref, inverses_ref, coupling_ref, columns_ref,
-    green_ref, pair_ref, previous, right_self, inverse, wide, flat, sems,
+    green_ref, pair_ref, previous, right_self, inverse, packed, wide, flat, sems,
 ):
     orbitals = inverse.shape[1]
     copies = [
@@ -221,32 +221,44 @@
         copy.start()
     domain = lax.axis_index("domain")
     even = domain % 2 == 0
+    fetch = pltpu.make_async_copy(second_ref, packed, sems.at[2])
+
+    @pl.when(domain > 0)
+    def _():
+        fetch.start()
 
     @pl.when(domain == 0)
     def _():
         previous[...] = lead_ref[0]
 
+    @pl.when(even)
+    def _():
+        right_self[...] = first_planes[...]
+
+    @pl.when(jnp.logical_not(even))
+    def _():
+        previous[...] = first_planes[...]
+
     @pl.when(even & (domain > 0))
     def _():
-        unpack_planes(second_ref, previous)
-
-    @pl.when(even)
-    def _():
-        right_self[...] = first_planes[...]
-
-    @pl.when(jnp.logical_not(even))
-    def _():
-        previous[...] = first_planes[...]
-        unpack_planes(second_ref, right_self)
+        fetch.wait()
+        unpack_planes(packed, previous)
 
     coupling = coupling_ref[0]
-    coupled = []
+    left_self = []
     for c in range(2):
         left_product = product(previous[c], coupling).astype(jnp.bfloat16)
-        left_self = product_tn(coupling, left_product).astype(jnp.bfloat16)
-        coupled.append(
-            (left_self.astype(jnp.float32) + right_self[c].astype(jnp.float32)).astype(jnp.bfloat16)
-        )
+        left_self.append(product_tn(coupling, left_product).astype(jnp.bfloat16))
+
+    @pl.when(jnp.logical_not(even))
+    def _():
+        fetch.wait()
+        unpack_planes(packed, right_self)
+
+    coupled = [
+        (left_self[c].astype(jnp.float32) + right_self[c].astype(jnp.float32)).astype(jnp.bfloat16)
+        for c in range(2)
+    ]
     for copy in copies:
         copy.wait()
     own = [inverse[c] for c in range(2)]
@@ -282,11 +294,15 @@
 
 
 def early_kernel(
-    first_planes, lead_ref, before_ref, after_ref, inverse_ref, sum_ref
+    first_ref, lead_ref, before_ref, after_ref, inverse_ref, sum_ref, first_planes
 ):
     domain = lax.axis_index("domain")
     none = (domain % 2 == 1) & (domain == lax.axis_size("domain") - 1)
 
+    @pl.when((domain > 0) & jnp.logical_not(none))
+    def _():
+        unpack_planes(first_ref, first_planes)
+
     def write(values):
         for c in range(2):
             sum_ref[c] = values[c]
@@ -310,7 +326,7 @@
 
 
 def late_kernel(
-    width, second_ref, first_planes, before_ref, after_ref, inverse_ref, sum_ref, columns_ref, pair_before,
+    width, second_ref, first_ref, before_ref, after_ref, inverse_ref, sum_ref, columns_ref, pair_before,
     green_ref, pair_ref, middle, wide, flat,
 ):
     orbitals = inverse_ref.shape[1]
@@ -319,7 +335,7 @@
 
     @pl.when(ends)
     def _():
-        middle[...] = first_planes[...]
+        unpack_planes(first_ref, middle)
 
     @pl.when(jnp.logical_not(ends))
     def _():
@@ -365,9 +381,23 @@
     pair_ref[place] = flat[...].astype(jnp.bfloat16)
 
 
-def final_kernel(shifts_ref, samples_ref, slots_ref, green_even_ref, green_odd_ref, *rest):
+def group_kernel(shifts_ref, samples_ref, grouped_ref):
+    reach = grouped_ref.shape[0] // 2
+    grouped_ref[...] = jnp.zeros(grouped_ref.shape, grouped_ref.dtype)
+
+    def add_point(w, carry):
+        place = jnp.clip(shifts_ref[w] + reach, 0, 2 * reach)
+        for c in range(2):
+            grouped_ref[place, c] = grouped_ref[place, c] + samples_ref[w, c].astype(jnp.float32)
+        return carry
+
+    lax.fori_loop(0, samples_ref.shape[0], add_point, 0)
+
+
+def final_kernel(grouped_ref, slots_ref, green_even_ref, green_odd_ref, *rest):
     *pairs, out_ref, sources, merged, self_block, result, sems = rest
-    points = shifts_ref.shape[0]
+    points = sources.shape[0]
+    reach = grouped_ref.shape[0] // 2
     orbitals = result.shape[2]
     groups = orbitals // SUBLANES
     tiles = slots_ref.shape[1] // LANES
@@ -388,12 +418,11 @@
                 for c in range(2):
                     sources[2 * owner + e, c] = array[e, c].astype(jnp.float32)
 
-    def add_point(w, sums):
-        shift = shifts_ref[w]
-        sample = [samples_ref[w, c].astype(jnp.float32)[:used] for c in range(2)]
+    def add_shift(place, sums):
+        sample = [grouped_ref[place, c, :used, :] for c in range(2)]
         after = []
         for e in range(2):
-            source = 2 * me + e - shift
+            source = 2 * me + e + reach - place
             keep = jnp.where((source >= 0) & (source < points), 1.0, 0.0)
             source = jnp.clip(source, 0, points - 1)
             real, imag = (sources[source, c, :used, :] for c in range(2))
@@ -406,7 +435,7 @@
         return tuple(after)
 
     zero = jnp.zeros((used, LANES), jnp.float32)
-    sums = lax.fori_loop(0, points, add_point, ((zero, zero), (zero, zero)), unroll=4)
+    sums = lax.fori_loop(0, 2 * reach + 1, add_shift, ((zero, zero), (zero, zero)), unroll=3)
     for e in range(2):
         for c in range(2):
             merged[e, c] = sums[e][c]
@@ -429,10 +458,16 @@
         green = [green_ref[c] for c in range(2)]
         sigma = [self_block[e, c, :, :orbitals] for c in range(2)]
         scattered = [part.astype(jnp.bfloat16) for part in complex_product(green, sigma)]
-        for c, part in enumerate(complex_product(scattered, green)):
+        reals = product(scattered[0], green[0])
+        imags = product(scattered[1], green[1])
+
+        def put(c, part):
             result[e, c] = (green[c].astype(jnp.float32) + part).astype(jnp.bfloat16)
             copies.append(pltpu.make_async_copy(result.at[e, c], out_ref.at[e, 0, c], sems.at[e, c]))
             copies[-1].start()
+
+        put(0, reals - imags)
+        put(1, product(scattered[0] + scattered[1], green[0] + green[1]) - reals - imags)
     for copy in copies:
         copy.wait()
 
@@ -458,6 +493,7 @@
     energies = inverses.shape[0]
     orbitals = inverses.shape[3]
     width = neighbors.shape[2]
+    points = shifts.shape[0]
     rows = packed_rows(orbitals)
     groups = orbitals * width // LANES
     used = -(-groups // SUBLANES) * SUBLANES
@@ -538,24 +574,34 @@
     green_even, pair = call(
         functools.partial(green_kernel, width),
         (block, shape(pair_shape, bf16)),
-        [IN_VMEM] * 3 + [IN_HBM] + [IN_VMEM] * 2,
+        [IN_HBM] + [IN_VMEM] * 2 + [IN_HBM] + [IN_VMEM] * 2,
         [
             pltpu.VMEM((2, *plane), bf16),
             pltpu.VMEM((2, *plane), bf16),
             pltpu.VMEM((2, *plane), bf16),
+            pltpu.VMEM((rows, LANES), bf16),
             pltpu.VMEM((2, orbitals, padded), f32),
             pltpu.VMEM((2, height, LANES), f32),
-            pltpu.SemaphoreType.DMA((2,)),
+            pltpu.SemaphoreType.DMA((3,)),
         ],
         flops=12 * cube,
         limit=12,
-    )(second, unpacked(first), lead, in_hbm[0], coupling, columns)
+    )(pltpu.with_memory_space_constraint(second, pltpu.HBM), unpacked(first), lead, in_hbm[0], coupling, columns)
+
+    reach = points // 4
+    grouped = call(
+        group_kernel, shape((2 * reach + 1, 2, height, LANES), f32), [IN_SMEM, IN_VMEM]
+    )(shifts, samples)
 
     first, second = received[1]
-    first, pair = lax.optimization_barrier((first, pair))
-    first = unpacked(first)
+    first, pair, grouped = lax.optimization_barrier((first, pair, grouped))
     partial_sum = call(
-        early_kernel, shape((2, *plane), f32), [IN_VMEM] * 5, flops=6 * cube, limit=12
+        early_kernel,
+        shape((2, *plane), f32),
+        [IN_VMEM] * 5,
+        [pltpu.VMEM((2, *plane), bf16)],
+        flops=6 * cube,
+        limit=12,
     )(first, lead, before, after, inverse)
     green_odd, pair = call(
         functools.partial(late_kernel, width),
@@ -582,9 +628,9 @@
     return call(
         final_kernel,
         shape((energies, 1, 2, *plane), bf16),
-        [IN_SMEM] + [IN_VMEM] * (4 + len(sources)),
+        [IN_VMEM] * (4 + len(sources)),
         [
-            pltpu.VMEM((shifts.shape[0], 2, height, LANES), f32),
+            pltpu.VMEM((points, 2, height, LANES), f32),
             pltpu.VMEM((2, 2, used, LANES), f32),
             pltpu.VMEM((2, 2, orbitals, padded), bf16),
             pltpu.VMEM((2, 2, *plane), bf16),
@@ -593,7 +639,7 @@
         flops=16 * cube,
         out_spec=IN_HBM,
         limit=16,
-    )(shifts, samples, slots, green_even, green_odd, *sources)
+    )(grouped, slots, green_even, green_odd, *sources)
 
 
 def solution(mesh):

time: 57.4 us -> 57.2 us (level)
  starting transfers between devices: 17.1 us -> 14.5 us
  waiting for transfers between devices: 0.92 us -> 2.68 us
  Pallas kernels: 27.4 us -> 28.1 us
    ppermute x3, starting transfers between devices: 5.19 us -> 2.59 us  [body(): lax.ppermute(array, 'energy', [(i, i ^ 1) for i in range(8)])]
    ppermute x1, waiting for transfers between devices: 0.01 us -> 1.77 us  [body(): beside = lax.ppermute(pair, 'energy', [(i, i ^ 2) for i in range(8)])]
    pallas_call x1, Pallas kernels: 4.78 us -> 5.42 us  [body(): call(functools.partial(green_kernel, width), (block, shape(pair_shape, bf...]
    pallas_call x2 -> x3, Pallas kernels: 7.63 us -> 7.93 us  [the longest x1 5.24 us: body(): call(final_kernel, shape((energies, 1, 2, *plane), bf16), [IN_VMEM] * (4...]
  transfers between devices with their start and end apart: 9 -> 9, of which waited for: 1 -> 2; matrix products, arithmetic and copies ran while one was open for 0% -> 0% of each run, Pallas kernels for 27% -> 29%
where the time goes in v4:
time: 57.2 us; the launch traced here: 57 us
  Pallas kernels  28.1 us (49%)
  starting transfers between devices  14.5 us (25%)
  blocking collectives  11.2 us (20%)
  waiting for transfers between devices  2.68 us (5%)
    all_gather x1, blocking collectives, body(): samples = lax.all_gather(samples, 'energy', axis=0, tiled=True)  11.2 us
    ppermute x4, starting transfers between devices, body(): lax.ppermute(x, 'domain', route)  7.53 us
    pallas_call x2, Pallas kernels, body(): call(functools.partial(send_kernel, e), (shape((rows, LANES), bf16), shap...  6.63 us
    pallas_call x1, Pallas kernels, body(): call(functools.partial(green_kernel, width), (block, shape(pair_shape, bf...  5.42 us
    pallas_call x1, Pallas kernels, body(): call(final_kernel, shape((energies, 1, 2, *plane), bf16), [IN_VMEM] * (4...  5.24 us
    ppermute x1, starting transfers between devices, body(): beside = lax.ppermute(pair, 'energy', [(i, i ^ 2) for i in range(8)])  3.71 us
    pallas_call x1, Pallas kernels, body(): call(functools.partial(table_kernel, width), (shape((orbitals, LANES), jn...  2.99 us
    ppermute x3, starting transfers between devices, body(): lax.ppermute(array, 'energy', [(i, i ^ 1) for i in range(8)])  2.59 us
  transfers between devices with their start and end apart: 9, of which 2 were waited for; matrix products, arithmetic and copies ran while one was open for 0% of the time, Pallas kernels for 29%

profile of v4, /device:TPU:17, one launch (start us, length us, event | category | flops | bytes accessed | tf_op | source)
XLA Modules:
  0.0 57.0 jit_solution(12448832312805971552)
XLA Ops:
  0.0 0.0 copy-start.2
  0.0 3.5 %shard_map.64 = (bf16[2704,128]{1,0:T(8,128)(2,1)}, bf16[2704,128]{1,0:T(8,128)(2,1)}) custom-call(bf16[2,1,2,416,416]{4,3,2,1,0:T(8,128)(2,1)} %inverses_ref.6, bf16[1,416,416]{2,1,0:T(8,128)(2,1)} %coupling_ref.5), custom_call_target="tpu_custom_call" | custom-call | flops 575930368 | bytes 1048576 | tf_op jit(solution)/shard_map/pallas_call | solution.py:520
  3.5 0.0 copy-start
  3.5 1.4 %collective-permute-start.2 = (bf16[2704,128]{1,0:T(8,128)(2,1)}, bf16[2704,128]{1,0:T(8,128)(2,1)S(1)}, u32[]{:S(2)}, u32[]{:S(2)}) collective-permute-start(bf16[2704,128]{1,0:T(8,128)(2,1)} %get-tuple-element.29), channel_id=1, source_target_pairs={{0,1},{1,0},{2,3},{3,2},{4,5},{5,4},{6,7},{7,6},{8,9},{9,8},{10,11... | collective-permute-start | bytes 2076680 | tf_op jit(solution)/shard_map/ppermute | solution.py:536
  4.9 1.9 %collective-permute-start.1 = (bf16[2704,128]{1,0:T(8,128)(2,1)}, bf16[2704,128]{1,0:T(8,128)(2,1)}, u32[]{:S(2)}, u32[]{:S(2)}) collective-permute-start(bf16[2704,128]{1,0:T(8,128)(2,1)} %get-tuple-element.32), channel_id=1, source_target_pairs={{1,2},{2,1},{5,6},{6,5},{9,10},{10,9},{13,14},{14,13},{17,18},{18,... | collective-permute-start | bytes 2076680 | tf_op jit(solution)/shard_map/ppermute | solution.py:536
  6.8 3.1 %shard_map.65 = (bf16[2704,128]{1,0:T(8,128)(2,1)}, bf16[2704,128]{1,0:T(8,128)(2,1)S(1)}) custom-call(bf16[2,1,2,416,416]{4,3,2,1,0:T(8,128)(2,1)} %inverses_ref.6, bf16[1,416,416]{2,1,0:T(8,128)(2,1)} %coupling_ref.5), custom_call_target="tpu_custom_call" | custom-call | flops 575930368 | bytes 1048576 | tf_op jit(solution)/shard_map/pallas_call | solution.py:520
  10.0 0.0 copy-start.1
  10.0 0.5 collective-permute-start
  10.5 3.7 %collective-permute-start.3 = (bf16[2704,128]{1,0:T(8,128)(2,1)S(1)}, bf16[2704,128]{1,0:T(8,128)(2,1)S(1)}, u32[]{:S(2)}, u32[]{:S(2)}) collective-permute-start(bf16[2704,128]{1,0:T(8,128)(2,1)S(1)} %get-tuple-element.45), channel_id=1, source_target_pairs={{1,2},{2,1},{5,6},{6,5},{9,10},{10,9},{13,14},{14,13},{17,18},{18,... | collective-permute-start | bytes 2076680 | tf_op jit(solution)/shard_map/ppermute | solution.py:536
  14.2 0.0 copy-done.2
  14.2 0.1 copy.8.neighbors_ref
  14.4 0.0 copy-done
  14.4 3.0 %shard_map.67 = (s32[416,128]{1,0:T(8,128)S(1)}, s32[416,512]{1,0:T(8,128)S(1)}, bf16[2,2,64,128]{3,2,1,0:T(8,128)(2,1)S(1)}, bf16[2,2,416,416]{3,2,1,0:T(8,128)(2,1)S(1)}, bf16[1,416,416]{2,1,0:T(8,128)(2,1)S(1)}) custom-call(s32[1,416,16]{2,1,0:T(8,128)S(1)} %copy.8.neighbors_ref, bf16[2,1,2,6656]{3,2,1,0:T(2,128)(2,1)S(1)} %copy-done, ...), custom_call_target="tpu_custom_call" | custom-call | flops 575930368 | bytes 1048576 | tf_op jit(solution)/shard_map/pallas_call | solution.py:539
  17.4 11.2 %all_gather.3.samples_ref = bf16[16,2,64,128]{3,2,1,0:T(8,128)(2,1)S(1)} all-gather(bf16[2,2,64,128]{3,2,1,0:T(8,128)(2,1)S(1)} %get-tuple-element.38), channel_id=1, replica_groups=mesh['energy'=8,'domain'=4] {'energy'}, dimensions={0}, use_global_device_ids=true | all-gather | bytes 589824 | tf_op jit(solution)/shard_map/all_gather | solution.py:557
  28.6 0.0 copy-done.1
  28.6 0.8 %shard_map.69.grouped_ref = f32[9,2,64,128]{3,2,1,0:T(8,128)S(1)} custom-call(s32[16]{0:T(128)S(1)} %copy-done.1, bf16[16,2,64,128]{3,2,1,0:T(8,128)(2,1)S(1)} %all_gather.3.samples_ref), custom_call_target="tpu_custom_call" | custom-call | bytes 1048576 | tf_op jit(solution)/shard_map/pallas_call | solution.py:592
  29.4 2.3 %shard_map.70 = (bf16[2,416,416]{2,1,0:T(8,128)(2,1)S(1)}, bf16[2,416,416]{2,1,0:T(8,128)(2,1)S(1)}, bf16[2,416,416]{2,1,0:T(8,128)(2,1)S(1)}) custom-call(bf16[2,1,2,416,416]{4,3,2,1,0:T(8,128)(2,1)} %inverses_ref.6, bf16[1,416,416]{2,1,0:T(8,128)(2,1)S(1)} %get-tuple-element.36.coupling_ref), custom_call_target="tpu_custom_call" | custom-call | flops 575930368 | bytes 1048576 | tf_op jit(solution)/shard_map/pallas_call | solution.py:562
  31.7 0.0 collective-permute-done.2.packed_ref
  31.7 0.3 shard_map.66.first_planes
  32.0 0.0 collective-permute-done.1.second_ref
  32.0 5.4 %shard_map.68 = (bf16[2,416,416]{2,1,0:T(8,128)(2,1)S(1)}, bf16[1,2,64,128]{3,2,1,0:T(8,128)(2,1)S(1)}) custom-call(bf16[2704,128]{1,0:T(8,128)(2,1)} %collective-permute-done.1.second_ref, bf16[2,416,416]{2,1,0:T(8,128)(2,1)S(1)} %shard_map.66.first_planes, bf16[2,2,416,416]{3,2,1,0:T(8,128)(2,1)S(1)} %get-tuple-element.35.lead_ref, ...), custom_call_target="tpu_custom_call" | custom-call | flops 1727791104 | bytes 1048576 | tf_op jit(solution)/shard_map/pallas_call | solution.py:574
  37.4 0.0 collective-permute-done.first_ref
  37.4 1.9 %shard_map.71.sum_ref = f32[2,416,416]{2,1,0:T(8,128)S(1)} custom-call(bf16[2704,128]{1,0:T(8,128)(2,1)S(1)} %collective-permute-done.first_ref, bf16[2,2,416,416]{3,2,1,0:T(8,128)(2,1)S(1)} %get-tuple-element.35.lead_ref, bf16[2,416,416]{2,1,0:T(8,128)(2,1)S(1)} %get-tuple-element.47.before_ref, bf16[2,416,416]{2,1,0:T(8,128)(2,1)S(1)} %get-tuple-element.48.after_ref, ...), custom_call_target="tpu_custom_call" | custom-call | flops 863895552 | bytes 1048576 | tf_op jit(solution)/shard_map/pallas_call | solution.py:598
  39.3 0.0 collective-permute-done.3.second_ref
  39.3 2.6 %shard_map.72 = (bf16[2,416,416]{2,1,0:T(8,128)(2,1)S(1)}, bf16[2,2,64,128]{3,2,1,0:T(8,128)(2,1)S(1)}) custom-call(bf16[2704,128]{1,0:T(8,128)(2,1)S(1)} %collective-permute-done.3.second_ref, bf16[2704,128]{1,0:T(8,128)(2,1)S(1)} %collective-permute-done.first_ref, bf16[2,416,416]{2,1,0:T(8,128)(2,1)S(1)} %get-tuple-element.47.before_ref, ...), custom_call_target="tpu_custom_call" | custom-call | flops 863895552 | bytes 1048576 | tf_op jit(solution)/shard_map/pallas_call | solution.py:606
  41.9 0.7 %collective-permute-start.7 = (bf16[2,2,64,128]{3,2,1,0:T(8,128)(2,1)S(1)}, bf16[2,2,64,128]{3,2,1,0:T(8,128)(2,1)S(1)}, u32[]{:S(2)}, u32[]{:S(2)}) collective-permute-start(bf16[2,2,64,128]{3,2,1,0:T(8,128)(2,1)S(1)} %get-tuple-element.52.rest_0_), channel_id=1, source_target_pairs={{8,16},{12,20},{16,8},{20,12},{9,17},{13,21},{17,9},{21,13},{10,18... | collective-permute-start | bytes 196616 | tf_op jit(solution)/shard_map/ppermute | solution.py:620
  42.6 3.7 %collective-permute-start.5 = (bf16[2,2,64,128]{3,2,1,0:T(8,128)(2,1)S(1)}, bf16[2,2,64,128]{3,2,1,0:T(8,128)(2,1)S(1)}, u32[]{:S(2)}, u32[]{:S(2)}) collective-permute-start(bf16[2,2,64,128]{3,2,1,0:T(8,128)(2,1)S(1)} %get-tuple-element.52.rest_0_), channel_id=1, source_target_pairs={{0,8},{4,12},{8,0},{12,4},{16,24},{20,28},{24,16},{28,20},{1,9},{5... | collective-permute-start | bytes 196616 | tf_op jit(solution)/shard_map/ppermute | solution.py:621
  46.3 1.0 %collective-permute-start.4 = (bf16[2,2,64,128]{3,2,1,0:T(8,128)(2,1)S(1)}, bf16[2,2,64,128]{3,2,1,0:T(8,128)(2,1)S(1)}, u32[]{:S(2)}, u32[]{:S(2)}) collective-permute-start(bf16[2,2,64,128]{3,2,1,0:T(8,128)(2,1)S(1)} %get-tuple-element.52.rest_0_), channel_id=1, source_target_pairs={{0,4},{4,0},{8,12},{12,8},{16,20},{20,16},{24,28},{28,24},{1,5},{5... | collective-permute-start | bytes 196616 | tf_op jit(solution)/shard_map/ppermute | solution.py:624
  47.3 0.0 collective-permute-done.7.rest_4_
  47.3 0.0 collective-permute-start.8
  47.3 1.8 %collective-permute-done.5.rest_2_ = bf16[2,2,64,128]{3,2,1,0:T(8,128)(2,1)S(1)} collective-permute-done((bf16[2,2,64,128]{3,2,1,0:T(8,128)(2,1)S(1)}, bf16[2,2,64,128]{3,2,1,0:T(8,128)(2,1)S(1)}, u32[]{:S(2)}, u32[]{:S(2)}) %collective-permute-start.5) | collective-permute-done | bytes 65568 | tf_op jit(solution)/shard_map/ppermute | solution.py:621
  49.1 1.6 %collective-permute-start.6 = (bf16[2,2,64,128]{3,2,1,0:T(8,128)(2,1)S(1)}, bf16[2,2,64,128]{3,2,1,0:T(8,128)(2,1)S(1)}, u32[]{:S(2)}, u32[]{:S(2)}) collective-permute-start(bf16[2,2,64,128]{3,2,1,0:T(8,128)(2,1)S(1)} %collective-permute-done.5.rest_2_), channel_id=1, source_target_pairs={{0,4},{4,0},{8,12},{12,8},{16,20},{20,16},{24,28},{28,24},{1,5},{5... | collective-permute-start | bytes 196616 | tf_op jit(solution)/shard_map/ppermute | solution.py:624
  50.6 0.0 collective-permute-done.4.rest_1_
  50.7 0.0 collective-permute-done.8.rest_5_
  50.7 0.9 %collective-permute-done.6.rest_3_ = bf16[2,2,64,128]{3,2,1,0:T(8,128)(2,1)S(1)} collective-permute-done((bf16[2,2,64,128]{3,2,1,0:T(8,128)(2,1)S(1)}, bf16[2,2,64,128]{3,2,1,0:T(8,128)(2,1)S(1)}, u32[]{:S(2)}, u32[]{:S(2)}) %collective-permute-start.6) | collective-permute-done | bytes 65568 | tf_op jit(solution)/shard_map/ppermute | solution.py:624
  51.6 5.2 %shard_map.73 = bf16[2,1,2,416,416]{4,3,2,1,0:T(8,128)(2,1)} custom-call(f32[9,2,64,128]{3,2,1,0:T(8,128)S(1)} %shard_map.69.grouped_ref, s32[416,512]{1,0:T(8,128)S(1)} %get-tuple-element.43.slots_ref, bf16[2,416,416]{2,1,0:T(8,128)(2,1)S(1)} %get-tuple-element.44.green_even_ref, bf16[2,416,416]{2,1,0:T(8,128)(2,1)S(1)} %get-tuple-element.51.green_odd_ref, ...), custom_call_target="tpu_custom_call" | custom-call | flops 2303721472 | bytes 1048576 | tf_op jit(solution)/shard_map/pallas_call | solution.py:628
Async XLA Ops:
  0.0 14.2 %copy-start.2 = (s32[1,416,16]{1,2,0:T(8,128)S(1)}, s32[1,416,16]{1,2,0:T(8,128)}, u32[]{:S(2)}) copy-start(s32[1,416,16]{1,2,0:T(8,128)} %param.10) | copy-start | bytes 79876
  3.5 10.9 %copy-start = (bf16[2,1,2,6656]{3,2,1,0:T(2,128)(2,1)S(1)}, bf16[2,1,2,6656]{3,2,1,0:T(2,128)(2,1)}, u32[]{:S(2)}) copy-start(bf16[2,1,2,6656]{3,2,1,0:T(2,128)(2,1)} %phonon_ref.1) | copy-start | bytes 159748
  3.5 28.2 %collective-permute-start.2 = (bf16[2704,128]{1,0:T(8,128)(2,1)}, bf16[2704,128]{1,0:T(8,128)(2,1)S(1)}, u32[]{:S(2)}, u32[]{:S(2)}) collective-permute-start(bf16[2704,128]{1,0:T(8,128)(2,1)} %get-tuple-element.29), channel_id=1, source_target_pairs={{0,1},{1,0},{2,3},{3,2},{4,5},{5,4},{6,7},{7,6},{8,9},{9,8},{10,11... | collective-permute-start | bytes 2076680 | tf_op jit(solution)/shard_map/ppermute | solution.py:536
  4.9 27.0 %collective-permute-start.1 = (bf16[2704,128]{1,0:T(8,128)(2,1)}, bf16[2704,128]{1,0:T(8,128)(2,1)}, u32[]{:S(2)}, u32[]{:S(2)}) collective-permute-start(bf16[2704,128]{1,0:T(8,128)(2,1)} %get-tuple-element.32), channel_id=1, source_target_pairs={{1,2},{2,1},{5,6},{6,5},{9,10},{10,9},{13,14},{14,13},{17,18},{18,... | collective-permute-start | bytes 2076680 | tf_op jit(solution)/shard_map/ppermute | solution.py:536
  10.0 18.6 %copy-start.1 = (s32[16]{0:T(128)S(1)}, s32[16]{0:T(128)}, u32[]{:S(2)}) copy-start(s32[16]{0:T(128)} %shifts_ref.1) | copy-start | bytes 196
  10.0 27.4 %collective-permute-start = (bf16[2704,128]{1,0:T(8,128)(2,1)}, bf16[2704,128]{1,0:T(8,128)(2,1)S(1)}, u32[]{:S(2)}, u32[]{:S(2)}) collective-permute-start(bf16[2704,128]{1,0:T(8,128)(2,1)} %get-tuple-element.31), channel_id=1, source_target_pairs={{0,1},{1,0},{2,3},{3,2},{4,5},{5,4},{6,7},{7,6},{8,9},{9,8},{10,11... | collective-permute-start | bytes 2076680 | tf_op jit(solution)/shard_map/ppermute | solution.py:536
  10.5 28.8 %collective-permute-start.3 = (bf16[2704,128]{1,0:T(8,128)(2,1)S(1)}, bf16[2704,128]{1,0:T(8,128)(2,1)S(1)}, u32[]{:S(2)}, u32[]{:S(2)}) collective-permute-start(bf16[2704,128]{1,0:T(8,128)(2,1)S(1)} %get-tuple-element.45), channel_id=1, source_target_pairs={{1,2},{2,1},{5,6},{6,5},{9,10},{10,9},{13,14},{14,13},{17,18},{18,... | collective-permute-start | bytes 2076680 | tf_op jit(solution)/shard_map/ppermute | solution.py:536
  41.9 5.4 %collective-permute-start.7 = (bf16[2,2,64,128]{3,2,1,0:T(8,128)(2,1)S(1)}, bf16[2,2,64,128]{3,2,1,0:T(8,128)(2,1)S(1)}, u32[]{:S(2)}, u32[]{:S(2)}) collective-permute-start(bf16[2,2,64,128]{3,2,1,0:T(8,128)(2,1)S(1)} %get-tuple-element.52.rest_0_), channel_id=1, source_target_pairs={{8,16},{12,20},{16,8},{20,12},{9,17},{13,21},{17,9},{21,13},{10,18... | collective-permute-start | bytes 196616 | tf_op jit(solution)/shard_map/ppermute | solution.py:620
  42.6 6.5 %collective-permute-start.5 = (bf16[2,2,64,128]{3,2,1,0:T(8,128)(2,1)S(1)}, bf16[2,2,64,128]{3,2,1,0:T(8,128)(2,1)S(1)}, u32[]{:S(2)}, u32[]{:S(2)}) collective-permute-start(bf16[2,2,64,128]{3,2,1,0:T(8,128)(2,1)S(1)} %get-tuple-element.52.rest_0_), channel_id=1, source_target_pairs={{0,8},{4,12},{8,0},{12,4},{16,24},{20,28},{24,16},{28,20},{1,9},{5... | collective-permute-start | bytes 196616 | tf_op jit(solution)/shard_map/ppermute | solution.py:621
  46.3 4.4 %collective-permute-start.4 = (bf16[2,2,64,128]{3,2,1,0:T(8,128)(2,1)S(1)}, bf16[2,2,64,128]{3,2,1,0:T(8,128)(2,1)S(1)}, u32[]{:S(2)}, u32[]{:S(2)}) collective-permute-start(bf16[2,2,64,128]{3,2,1,0:T(8,128)(2,1)S(1)} %get-tuple-element.52.rest_0_), channel_id=1, source_target_pairs={{0,4},{4,0},{8,12},{12,8},{16,20},{20,16},{24,28},{28,24},{1,5},{5... | collective-permute-start | bytes 196616 | tf_op jit(solution)/shard_map/ppermute | solution.py:624
  47.3 3.4 %collective-permute-start.8 = (bf16[2,2,64,128]{3,2,1,0:T(8,128)(2,1)S(1)}, bf16[2,2,64,128]{3,2,1,0:T(8,128)(2,1)S(1)}, u32[]{:S(2)}, u32[]{:S(2)}) collective-permute-start(bf16[2,2,64,128]{3,2,1,0:T(8,128)(2,1)S(1)} %collective-permute-done.7.rest_4_), channel_id=1, source_target_pairs={{0,4},{4,0},{8,12},{12,8},{16,20},{20,16},{24,28},{28,24},{1,5},{5... | collective-permute-start | bytes 196616 | tf_op jit(solution)/shard_map/ppermute | solution.py:624
  49.1 2.5 %collective-permute-start.6 = (bf16[2,2,64,128]{3,2,1,0:T(8,128)(2,1)S(1)}, bf16[2,2,64,128]{3,2,1,0:T(8,128)(2,1)S(1)}, u32[]{:S(2)}, u32[]{:S(2)}) collective-permute-start(bf16[2,2,64,128]{3,2,1,0:T(8,128)(2,1)S(1)} %collective-permute-done.5.rest_2_), channel_id=1, source_target_pairs={{0,4},{4,0},{8,12},{12,8},{16,20},{20,16},{24,28},{28,24},{1,5},{5... | collective-permute-start | bytes 196616 | tf_op jit(solution)/shard_map/ppermute | solution.py:624

commit v5 on v4

--- a/solution.py
+++ b/solution.py
@@ -8,7 +8,7 @@
 from jax.sharding import PartitionSpec as P
 
 LANES = 128
-NEAR = (0, 2, 6)
+NEAR = (0, 6, 2)
 SUBLANES = 8
 MIB = 1024 * 1024
 
@@ -210,27 +210,21 @@
 
 
 def green_kernel(
-    width, second_ref, first_planes, lead_ref, inverses_ref, coupling_ref, columns_ref,
-    green_ref, pair_ref, previous, right_self, inverse, packed, wide, flat, sems,
+    width, second_ref, first_planes, lead_ref, inverse_ref, coupling_ref, columns_ref,
+    green_ref, pair_ref, previous, right_self, wide, flat,
 ):
-    orbitals = inverse.shape[1]
-    copies = [
-        pltpu.make_async_copy(inverses_ref.at[0, 0, c], inverse.at[c], sems.at[c]) for c in range(2)
-    ]
-    for copy in copies:
-        copy.start()
+    orbitals = inverse_ref.shape[1]
     domain = lax.axis_index("domain")
     even = domain % 2 == 0
-    fetch = pltpu.make_async_copy(second_ref, packed, sems.at[2])
-
-    @pl.when(domain > 0)
-    def _():
-        fetch.start()
 
     @pl.when(domain == 0)
     def _():
         previous[...] = lead_ref[0]
 
+    @pl.when(even & (domain > 0))
+    def _():
+        unpack_planes(second_ref, previous)
+
     @pl.when(even)
     def _():
         right_self[...] = first_planes[...]
@@ -238,30 +232,17 @@
     @pl.when(jnp.logical_not(even))
     def _():
         previous[...] = first_planes[...]
-
-    @pl.when(even & (domain > 0))
-    def _():
-        fetch.wait()
-        unpack_planes(packed, previous)
+        unpack_planes(second_ref, right_self)
 
     coupling = coupling_ref[0]
-    left_self = []
+    coupled = []
     for c in range(2):
         left_product = product(previous[c], coupling).astype(jnp.bfloat16)
-        left_self.append(product_tn(coupling, left_product).astype(jnp.bfloat16))
-
-    @pl.when(jnp.logical_not(even))
-    def _():
-        fetch.wait()
-        unpack_planes(packed, right_self)
-
-    coupled = [
-        (left_self[c].astype(jnp.float32) + right_self[c].astype(jnp.float32)).astype(jnp.bfloat16)
-        for c in range(2)
-    ]
-    for copy in copies:
-        copy.wait()
-    own = [inverse[c] for c in range(2)]
+        left_self = product_tn(coupling, left_product).astype(jnp.bfloat16)
+        coupled.append(
+            (left_self.astype(jnp.float32) + right_self[c].astype(jnp.float32)).astype(jnp.bfloat16)
+        )
+    own = [inverse_ref[c] for c in range(2)]
     inner = [part.astype(jnp.bfloat16) for part in complex_product(coupled, own)]
     for c, part in enumerate(complex_product(own, inner)):
         green = (own[c].astype(jnp.float32) + part).astype(jnp.bfloat16)
@@ -270,12 +251,16 @@
     gather_pairs(width, wide, columns_ref, flat, pair_ref, 0)
 
 
-def sides_kernel(inverses_ref, coupling_ref, before_ref, after_ref, inverse_ref, sems):
+def sides_kernel(
+    inverses_ref, second_ref, coupling_ref, before_ref, after_ref, inverse_ref, first_inverse, packed, sems
+):
     last = inverses_ref.shape[0] - 1
     copies = [
-        pltpu.make_async_copy(inverses_ref.at[last, 0, c], inverse_ref.at[c], sems.at[c])
+        pltpu.make_async_copy(inverses_ref.at[e, 0, c], held.at[c], sems.at[k, c])
+        for k, (e, held) in enumerate(((last, inverse_ref), (0, first_inverse)))
         for c in range(2)
     ]
+    copies.append(pltpu.make_async_copy(second_ref, packed, sems.at[2, 0]))
     for copy in copies:
         copy.start()
     coupling = coupling_ref[0]
@@ -283,6 +268,8 @@
         copies[c].wait()
         before_ref[c] = product_nt(inverse_ref[c], coupling).astype(jnp.bfloat16)
         after_ref[c] = product(coupling, inverse_ref[c]).astype(jnp.bfloat16)
+    for copy in copies[2:]:
+        copy.wait()
 
 
 def add_side(left, value, middle, right):
@@ -559,34 +546,32 @@
 
     pair_shape = (1, 2, height, LANES)
     block = shape((2, *plane), bf16)
-    before, after, inverse = call(
-        sides_kernel,
-        (block,) * 3,
-        [IN_HBM, IN_VMEM],
-        [pltpu.SemaphoreType.DMA((2,))],
-        flops=4 * cube,
-    )(in_hbm[0], coupling)
 
     def unpacked(first):
         return call(unpack_kernel, block, [IN_VMEM])(first)
 
     first, second = received[0]
+    first, second = lax.optimization_barrier((unpacked(first), second))
+    before, after, inverse, first_inverse, second = call(
+        sides_kernel,
+        (*(block,) * 4, shape((rows, LANES), bf16)),
+        [IN_HBM, IN_HBM, IN_VMEM],
+        [pltpu.SemaphoreType.DMA((3, 2))],
+        flops=4 * cube,
+    )(in_hbm[0], pltpu.with_memory_space_constraint(second, pltpu.HBM), coupling)
     green_even, pair = call(
         functools.partial(green_kernel, width),
         (block, shape(pair_shape, bf16)),
-        [IN_HBM] + [IN_VMEM] * 2 + [IN_HBM] + [IN_VMEM] * 2,
+        [IN_VMEM] * 6,
         [
             pltpu.VMEM((2, *plane), bf16),
             pltpu.VMEM((2, *plane), bf16),
-            pltpu.VMEM((2, *plane), bf16),
-            pltpu.VMEM((rows, LANES), bf16),
             pltpu.VMEM((2, orbitals, padded), f32),
             pltpu.VMEM((2, height, LANES), f32),
-            pltpu.SemaphoreType.DMA((3,)),
         ],
         flops=12 * cube,
         limit=12,
-    )(pltpu.with_memory_space_constraint(second, pltpu.HBM), unpacked(first), lead, in_hbm[0], coupling, columns)
+    )(second, first, lead, first_inverse, coupling, columns)
 
     reach = points // 4
     grouped = call(
@@ -617,11 +602,12 @@
     )(second, first, before, after, inverse, partial_sum, columns, pair)
     devices = lax.axis_size("energy")
     if devices == 8 and energies == 2:
+        swap = [(i, i ^ 1) for i in range(devices)]
+        beside = lax.ppermute(pair, "energy", [(i, i ^ 2) for i in range(devices)])
         across = lax.ppermute(pair, "energy", [(i, i ^ 6) for i in range(2, 6)])
-        beside = lax.ppermute(pair, "energy", [(i, i ^ 2) for i in range(8)])
         sources = []
-        for array in (pair, beside, across):
-            sources += [array, lax.ppermute(array, "energy", [(i, i ^ 1) for i in range(8)])]
+        for array in (pair, across, beside):
+            sources += [array, lax.ppermute(array, "energy", swap)]
     else:
         sources = [lax.all_gather(pair, "energy", axis=0, tiled=True)]
 

time: 57.2 us -> 56.7 us (level)
  starting transfers between devices: 14.5 us -> 17.2 us
  Pallas kernels: 28.1 us -> 26.1 us
  waiting for transfers between devices: 2.68 us -> 1.45 us
    ppermute x4, starting transfers between devices: 6.3 us -> 9 us  [the longest x3 5.27 us: body(): sources += [array, lax.ppermute(array, 'energy', swap)]]
    pallas_call x1, Pallas kernels: 5.42 us -> 3.44 us  [body(): call(functools.partial(green_kernel, width), (block, shape(pair_shape, bf...]
    ppermute x4, waiting for transfers between devices: 2.67 us -> 0.9 us  [the longest x3 0.9 us: body(): sources += [array, lax.ppermute(array, 'energy', swap)]]
  transfers between devices with their start and end apart: 9 -> 9, of which waited for: 2 -> 2; matrix products, arithmetic and copies ran while one was open for 0% -> 0% of each run, Pallas kernels for 29% -> 26%
where the time goes in v5:
time: 56.7 us; the launch traced here: 56.5 us
  Pallas kernels  26.1 us (46%)
  starting transfers between devices  17.2 us (30%)
  blocking collectives  11.2 us (20%)
  waiting for transfers between devices  1.45 us (3%)
    all_gather x1, blocking collectives, body(): samples = lax.all_gather(samples, 'energy', axis=0, tiled=True)  11.2 us
    ppermute x4, starting transfers between devices, body(): lax.ppermute(x, 'domain', route)  7.53 us
    pallas_call x2, Pallas kernels, body(): call(functools.partial(send_kernel, e), (shape((rows, LANES), bf16), shap...  6.63 us
    ppermute x3, starting transfers between devices, body(): sources += [array, lax.ppermute(array, 'energy', swap)]  5.27 us
    pallas_call x1, Pallas kernels, body(): call(final_kernel, shape((energies, 1, 2, *plane), bf16), [IN_VMEM] * (4...  5.24 us
    ppermute x1, starting transfers between devices, body(): beside = lax.ppermute(pair, 'energy', [(i, i ^ 2) for i in range(devices)])  3.73 us
    pallas_call x1, Pallas kernels, body(): call(functools.partial(green_kernel, width), (block, shape(pair_shape, bf...  3.44 us
    pallas_call x1, Pallas kernels, body(): call(functools.partial(table_kernel, width), (shape((orbitals, LANES), jn...  2.99 us
  transfers between devices with their start and end apart: 9, of which 2 were waited for; matrix products, arithmetic and copies ran while one was open for 0% of the time, Pallas kernels for 26%

profile of v5, /device:TPU:17, one launch (start us, length us, event | category | flops | bytes accessed | tf_op | source)
XLA Modules:
  0.0 56.5 jit_solution(2148655203393974932)
XLA Ops:
  0.0 0.0 copy-start.2
  0.0 3.5 %shard_map.64 = (bf16[2704,128]{1,0:T(8,128)(2,1)}, bf16[2704,128]{1,0:T(8,128)(2,1)}) custom-call(bf16[2,1,2,416,416]{4,3,2,1,0:T(8,128)(2,1)} %inverses_ref.4, bf16[1,416,416]{2,1,0:T(8,128)(2,1)} %coupling_ref.5), custom_call_target="tpu_custom_call" | custom-call | flops 575930368 | bytes 1048576 | tf_op jit(solution)/shard_map/pallas_call | solution.py:507
  3.5 0.0 copy-start
  3.5 1.4 %collective-permute-start.1 = (bf16[2704,128]{1,0:T(8,128)(2,1)}, bf16[2704,128]{1,0:T(8,128)(2,1)S(1)}, u32[]{:S(2)}, u32[]{:S(2)}) collective-permute-start(bf16[2704,128]{1,0:T(8,128)(2,1)} %get-tuple-element.33), channel_id=1, source_target_pairs={{0,1},{1,0},{2,3},{3,2},{4,5},{5,4},{6,7},{7,6},{8,9},{9,8},{10,11... | collective-permute-start | bytes 2076680 | tf_op jit(solution)/shard_map/ppermute | solution.py:523
  4.9 1.9 %collective-permute-start.2 = (bf16[2704,128]{1,0:T(8,128)(2,1)}, bf16[2704,128]{1,0:T(8,128)(2,1)}, u32[]{:S(2)}, u32[]{:S(2)}) collective-permute-start(bf16[2704,128]{1,0:T(8,128)(2,1)} %get-tuple-element.36), channel_id=1, source_target_pairs={{1,2},{2,1},{5,6},{6,5},{9,10},{10,9},{13,14},{14,13},{17,18},{18,... | collective-permute-start | bytes 2076680 | tf_op jit(solution)/shard_map/ppermute | solution.py:523
  6.8 3.1 %shard_map.65 = (bf16[2704,128]{1,0:T(8,128)(2,1)}, bf16[2704,128]{1,0:T(8,128)(2,1)S(1)}) custom-call(bf16[2,1,2,416,416]{4,3,2,1,0:T(8,128)(2,1)} %inverses_ref.4, bf16[1,416,416]{2,1,0:T(8,128)(2,1)} %coupling_ref.5), custom_call_target="tpu_custom_call" | custom-call | flops 575930368 | bytes 1048576 | tf_op jit(solution)/shard_map/pallas_call | solution.py:507
  10.0 0.0 copy-start.1
  10.0 0.5 collective-permute-start
  10.5 3.7 %collective-permute-start.3 = (bf16[2704,128]{1,0:T(8,128)(2,1)S(1)}, bf16[2704,128]{1,0:T(8,128)(2,1)S(1)}, u32[]{:S(2)}, u32[]{:S(2)}) collective-permute-start(bf16[2704,128]{1,0:T(8,128)(2,1)S(1)} %get-tuple-element.53), channel_id=1, source_target_pairs={{1,2},{2,1},{5,6},{6,5},{9,10},{10,9},{13,14},{14,13},{17,18},{18,... | collective-permute-start | bytes 2076680 | tf_op jit(solution)/shard_map/ppermute | solution.py:523
  14.2 0.0 copy-done.2
  14.2 0.1 copy.8.neighbors_ref
  14.4 0.0 copy-done
  14.4 3.0 %shard_map.67 = (s32[416,128]{1,0:T(8,128)S(1)}, s32[416,512]{1,0:T(8,128)S(1)}, bf16[2,2,64,128]{3,2,1,0:T(8,128)(2,1)S(1)}, bf16[2,2,416,416]{3,2,1,0:T(8,128)(2,1)S(1)}, bf16[1,416,416]{2,1,0:T(8,128)(2,1)S(1)}) custom-call(s32[1,416,16]{2,1,0:T(8,128)S(1)} %copy.8.neighbors_ref, bf16[2,1,2,6656]{3,2,1,0:T(2,128)(2,1)S(1)} %copy-done, ...), custom_call_target="tpu_custom_call" | custom-call | flops 575930368 | bytes 1048576 | tf_op jit(solution)/shard_map/pallas_call | solution.py:526
  17.4 11.2 %all_gather.3.samples_ref = bf16[16,2,64,128]{3,2,1,0:T(8,128)(2,1)S(1)} all-gather(bf16[2,2,64,128]{3,2,1,0:T(8,128)(2,1)S(1)} %get-tuple-element.46), channel_id=1, replica_groups=mesh['energy'=8,'domain'=4] {'energy'}, dimensions={0}, use_global_device_ids=true | all-gather | bytes 589824 | tf_op jit(solution)/shard_map/all_gather | solution.py:544
  28.6 0.0 copy-done.1
  28.6 0.8 %shard_map.70.grouped_ref = f32[9,2,64,128]{3,2,1,0:T(8,128)S(1)} custom-call(s32[16]{0:T(128)S(1)} %copy-done.1, bf16[16,2,64,128]{3,2,1,0:T(8,128)(2,1)S(1)} %all_gather.3.samples_ref), custom_call_target="tpu_custom_call" | custom-call | bytes 1048576 | tf_op jit(solution)/shard_map/pallas_call | solution.py:577
  29.4 0.0 collective-permute-done.1.packed_ref
  29.4 0.3 shard_map.66.first_planes
  29.6 0.0 collective-permute-done.2.second_ref
  29.7 2.3 %shard_map.68 = (bf16[2,416,416]{2,1,0:T(8,128)(2,1)S(1)}, bf16[2,416,416]{2,1,0:T(8,128)(2,1)S(1)}, bf16[2,416,416]{2,1,0:T(8,128)(2,1)S(1)}, bf16[2,416,416]{2,1,0:T(8,128)(2,1)S(1)}, bf16[2704,128]{1,0:T(8,128)(2,1)S(1)}) custom-call(bf16[2,1,2,416,416]{4,3,2,1,0:T(8,128)(2,1)} %inverses_ref.4, bf16[2704,128]{1,0:T(8,128)(2,1)} %collective-permute-done.2.second_ref, ...), custom_call_target="tpu_custom_call" | custom-call | flops 575930368 | bytes 1048576 | tf_op jit(solution)/shard_map/pallas_call | solution.py:555
  32.0 3.4 %shard_map.69 = (bf16[2,416,416]{2,1,0:T(8,128)(2,1)S(1)}, bf16[1,2,64,128]{3,2,1,0:T(8,128)(2,1)S(1)}) custom-call(bf16[2704,128]{1,0:T(8,128)(2,1)S(1)} %get-tuple-element.41.second_ref, bf16[2,416,416]{2,1,0:T(8,128)(2,1)S(1)} %shard_map.66.first_planes, bf16[2,2,416,416]{3,2,1,0:T(8,128)(2,1)S(1)} %get-tuple-element.43.lead_ref, ...), custom_call_target="tpu_custom_call" | custom-call | flops 1727791104 | bytes 1048576 | tf_op jit(solution)/shard_map/pallas_call | solution.py:562
  35.5 0.0 collective-permute-done.first_ref
  35.5 1.9 %shard_map.71.sum_ref = f32[2,416,416]{2,1,0:T(8,128)S(1)} custom-call(bf16[2704,128]{1,0:T(8,128)(2,1)S(1)} %collective-permute-done.first_ref, bf16[2,2,416,416]{3,2,1,0:T(8,128)(2,1)S(1)} %get-tuple-element.43.lead_ref, bf16[2,416,416]{2,1,0:T(8,128)(2,1)S(1)} %get-tuple-element.55.before_ref, bf16[2,416,416]{2,1,0:T(8,128)(2,1)S(1)} %get-tuple-element.56.after_ref, ...), custom_call_target="tpu_custom_call" | custom-call | flops 863895552 | bytes 1048576 | tf_op jit(solution)/shard_map/pallas_call | solution.py:583
  37.4 0.5 collective-permute-done.3.second_ref
  37.9 2.6 %shard_map.72 = (bf16[2,416,416]{2,1,0:T(8,128)(2,1)S(1)}, bf16[2,2,64,128]{3,2,1,0:T(8,128)(2,1)S(1)}) custom-call(bf16[2704,128]{1,0:T(8,128)(2,1)S(1)} %collective-permute-done.3.second_ref, bf16[2704,128]{1,0:T(8,128)(2,1)S(1)} %collective-permute-done.first_ref, bf16[2,416,416]{2,1,0:T(8,128)(2,1)S(1)} %get-tuple-element.55.before_ref, ...), custom_call_target="tpu_custom_call" | custom-call | flops 863895552 | bytes 1048576 | tf_op jit(solution)/shard_map/pallas_call | solution.py:591
  40.5 0.7 %collective-permute-start.5 = (bf16[2,2,64,128]{3,2,1,0:T(8,128)(2,1)S(1)}, bf16[2,2,64,128]{3,2,1,0:T(8,128)(2,1)S(1)}, u32[]{:S(2)}, u32[]{:S(2)}) collective-permute-start(bf16[2,2,64,128]{3,2,1,0:T(8,128)(2,1)S(1)} %get-tuple-element.60.rest_0_), channel_id=1, source_target_pairs={{8,16},{12,20},{16,8},{20,12},{9,17},{13,21},{17,9},{21,13},{10,18... | collective-permute-start | bytes 196616 | tf_op jit(solution)/shard_map/ppermute | solution.py:607
  41.1 3.7 %collective-permute-start.7 = (bf16[2,2,64,128]{3,2,1,0:T(8,128)(2,1)S(1)}, bf16[2,2,64,128]{3,2,1,0:T(8,128)(2,1)S(1)}, u32[]{:S(2)}, u32[]{:S(2)}) collective-permute-start(bf16[2,2,64,128]{3,2,1,0:T(8,128)(2,1)S(1)} %get-tuple-element.60.rest_0_), channel_id=1, source_target_pairs={{0,8},{4,12},{8,0},{12,4},{16,24},{20,28},{24,16},{28,20},{1,9},{5... | collective-permute-start | bytes 196616 | tf_op jit(solution)/shard_map/ppermute | solution.py:606
  44.9 2.4 %collective-permute-start.4 = (bf16[2,2,64,128]{3,2,1,0:T(8,128)(2,1)S(1)}, bf16[2,2,64,128]{3,2,1,0:T(8,128)(2,1)S(1)}, u32[]{:S(2)}, u32[]{:S(2)}) collective-permute-start(bf16[2,2,64,128]{3,2,1,0:T(8,128)(2,1)S(1)} %get-tuple-element.60.rest_0_), channel_id=1, source_target_pairs={{0,4},{4,0},{8,12},{12,8},{16,20},{20,16},{24,28},{28,24},{1,5},{5... | collective-permute-start | bytes 196616 | tf_op jit(solution)/shard_map/ppermute | solution.py:610
  47.3 0.0 collective-permute-done.5.rest_2_
  47.3 0.0 collective-permute-start.6
  47.3 0.0 collective-permute-done.7.rest_4_
  47.3 2.8 %collective-permute-start.8 = (bf16[2,2,64,128]{3,2,1,0:T(8,128)(2,1)S(1)}, bf16[2,2,64,128]{3,2,1,0:T(8,128)(2,1)S(1)}, u32[]{:S(2)}, u32[]{:S(2)}) collective-permute-start(bf16[2,2,64,128]{3,2,1,0:T(8,128)(2,1)S(1)} %collective-permute-done.7.rest_4_), channel_id=1, source_target_pairs={{0,4},{4,0},{8,12},{12,8},{16,20},{20,16},{24,28},{28,24},{1,5},{5... | collective-permute-start | bytes 196616 | tf_op jit(solution)/shard_map/ppermute | solution.py:610
  50.2 0.0 collective-permute-done.4.rest_1_
  50.2 0.0 collective-permute-done.6.rest_3_
  50.2 0.9 %collective-permute-done.8.rest_5_ = bf16[2,2,64,128]{3,2,1,0:T(8,128)(2,1)S(1)} collective-permute-done((bf16[2,2,64,128]{3,2,1,0:T(8,128)(2,1)S(1)}, bf16[2,2,64,128]{3,2,1,0:T(8,128)(2,1)S(1)}, u32[]{:S(2)}, u32[]{:S(2)}) %collective-permute-start.8) | collective-permute-done | bytes 65568 | tf_op jit(solution)/shard_map/ppermute | solution.py:610
  51.1 5.2 %shard_map.73 = bf16[2,1,2,416,416]{4,3,2,1,0:T(8,128)(2,1)} custom-call(f32[9,2,64,128]{3,2,1,0:T(8,128)S(1)} %shard_map.70.grouped_ref, s32[416,512]{1,0:T(8,128)S(1)} %get-tuple-element.51.slots_ref, bf16[2,416,416]{2,1,0:T(8,128)(2,1)S(1)} %get-tuple-element.52.green_even_ref, bf16[2,416,416]{2,1,0:T(8,128)(2,1)S(1)} %get-tuple-element.59.green_odd_ref, ...), custom_call_target="tpu_custom_call" | custom-call | flops 2303721472 | bytes 1048576 | tf_op jit(solution)/shard_map/pallas_call | solution.py:614
Async XLA Ops:
  0.0 14.2 %copy-start.2 = (s32[1,416,16]{1,2,0:T(8,128)S(1)}, s32[1,416,16]{1,2,0:T(8,128)}, u32[]{:S(2)}) copy-start(s32[1,416,16]{1,2,0:T(8,128)} %param.10) | copy-start | bytes 79876
  3.5 10.9 %copy-start = (bf16[2,1,2,6656]{3,2,1,0:T(2,128)(2,1)S(1)}, bf16[2,1,2,6656]{3,2,1,0:T(2,128)(2,1)}, u32[]{:S(2)}) copy-start(bf16[2,1,2,6656]{3,2,1,0:T(2,128)(2,1)} %phonon_ref.1) | copy-start | bytes 159748
  3.5 25.9 %collective-permute-start.1 = (bf16[2704,128]{1,0:T(8,128)(2,1)}, bf16[2704,128]{1,0:T(8,128)(2,1)S(1)}, u32[]{:S(2)}, u32[]{:S(2)}) collective-permute-start(bf16[2704,128]{1,0:T(8,128)(2,1)} %get-tuple-element.33), channel_id=1, source_target_pairs={{0,1},{1,0},{2,3},{3,2},{4,5},{5,4},{6,7},{7,6},{8,9},{9,8},{10,11... | collective-permute-start | bytes 2076680 | tf_op jit(solution)/shard_map/ppermute | solution.py:523
  4.9 24.7 %collective-permute-start.2 = (bf16[2704,128]{1,0:T(8,128)(2,1)}, bf16[2704,128]{1,0:T(8,128)(2,1)}, u32[]{:S(2)}, u32[]{:S(2)}) collective-permute-start(bf16[2704,128]{1,0:T(8,128)(2,1)} %get-tuple-element.36), channel_id=1, source_target_pairs={{1,2},{2,1},{5,6},{6,5},{9,10},{10,9},{13,14},{14,13},{17,18},{18,... | collective-permute-start | bytes 2076680 | tf_op jit(solution)/shard_map/ppermute | solution.py:523
  10.0 18.6 %copy-start.1 = (s32[16]{0:T(128)S(1)}, s32[16]{0:T(128)}, u32[]{:S(2)}) copy-start(s32[16]{0:T(128)} %shifts_ref.1) | copy-start | bytes 196
  10.0 25.5 %collective-permute-start = (bf16[2704,128]{1,0:T(8,128)(2,1)}, bf16[2704,128]{1,0:T(8,128)(2,1)S(1)}, u32[]{:S(2)}, u32[]{:S(2)}) collective-permute-start(bf16[2704,128]{1,0:T(8,128)(2,1)} %get-tuple-element.35), channel_id=1, source_target_pairs={{0,1},{1,0},{2,3},{3,2},{4,5},{5,4},{6,7},{7,6},{8,9},{9,8},{10,11... | collective-permute-start | bytes 2076680 | tf_op jit(solution)/shard_map/ppermute | solution.py:523
  10.5 27.4 %collective-permute-start.3 = (bf16[2704,128]{1,0:T(8,128)(2,1)S(1)}, bf16[2704,128]{1,0:T(8,128)(2,1)S(1)}, u32[]{:S(2)}, u32[]{:S(2)}) collective-permute-start(bf16[2704,128]{1,0:T(8,128)(2,1)S(1)} %get-tuple-element.53), channel_id=1, source_target_pairs={{1,2},{2,1},{5,6},{6,5},{9,10},{10,9},{13,14},{14,13},{17,18},{18,... | collective-permute-start | bytes 2076680 | tf_op jit(solution)/shard_map/ppermute | solution.py:523
  40.5 6.8 %collective-permute-start.5 = (bf16[2,2,64,128]{3,2,1,0:T(8,128)(2,1)S(1)}, bf16[2,2,64,128]{3,2,1,0:T(8,128)(2,1)S(1)}, u32[]{:S(2)}, u32[]{:S(2)}) collective-permute-start(bf16[2,2,64,128]{3,2,1,0:T(8,128)(2,1)S(1)} %get-tuple-element.60.rest_0_), channel_id=1, source_target_pairs={{8,16},{12,20},{16,8},{20,12},{9,17},{13,21},{17,9},{21,13},{10,18... | collective-permute-start | bytes 196616 | tf_op jit(solution)/shard_map/ppermute | solution.py:607
  41.1 6.2 %collective-permute-start.7 = (bf16[2,2,64,128]{3,2,1,0:T(8,128)(2,1)S(1)}, bf16[2,2,64,128]{3,2,1,0:T(8,128)(2,1)S(1)}, u32[]{:S(2)}, u32[]{:S(2)}) collective-permute-start(bf16[2,2,64,128]{3,2,1,0:T(8,128)(2,1)S(1)} %get-tuple-element.60.rest_0_), channel_id=1, source_target_pairs={{0,8},{4,12},{8,0},{12,4},{16,24},{20,28},{24,16},{28,20},{1,9},{5... | collective-permute-start | bytes 196616 | tf_op jit(solution)/shard_map/ppermute | solution.py:606
  44.9 5.3 %collective-permute-start.4 = (bf16[2,2,64,128]{3,2,1,0:T(8,128)(2,1)S(1)}, bf16[2,2,64,128]{3,2,1,0:T(8,128)(2,1)S(1)}, u32[]{:S(2)}, u32[]{:S(2)}) collective-permute-start(bf16[2,2,64,128]{3,2,1,0:T(8,128)(2,1)S(1)} %get-tuple-element.60.rest_0_), channel_id=1, source_target_pairs={{0,4},{4,0},{8,12},{12,8},{16,20},{20,16},{24,28},{28,24},{1,5},{5... | collective-permute-start | bytes 196616 | tf_op jit(solution)/shard_map/ppermute | solution.py:610
  47.3 2.9 %collective-permute-start.6 = (bf16[2,2,64,128]{3,2,1,0:T(8,128)(2,1)S(1)}, bf16[2,2,64,128]{3,2,1,0:T(8,128)(2,1)S(1)}, u32[]{:S(2)}, u32[]{:S(2)}) collective-permute-start(bf16[2,2,64,128]{3,2,1,0:T(8,128)(2,1)S(1)} %collective-permute-done.5.rest_2_), channel_id=1, source_target_pairs={{0,4},{4,0},{8,12},{12,8},{16,20},{20,16},{24,28},{28,24},{1,5},{5... | collective-permute-start | bytes 196616 | tf_op jit(solution)/shard_map/ppermute | solution.py:610
  47.3 3.7 %collective-permute-start.8 = (bf16[2,2,64,128]{3,2,1,0:T(8,128)(2,1)S(1)}, bf16[2,2,64,128]{3,2,1,0:T(8,128)(2,1)S(1)}, u32[]{:S(2)}, u32[]{:S(2)}) collective-permute-start(bf16[2,2,64,128]{3,2,1,0:T(8,128)(2,1)S(1)} %collective-permute-done.7.rest_4_), channel_id=1, source_target_pairs={{0,4},{4,0},{8,12},{12,8},{16,20},{20,16},{24,28},{28,24},{1,5},{5... | collective-permute-start | bytes 196616 | tf_op jit(solution)/shard_map/ppermute | solution.py:610

commit v6 on v5

--- a/solution.py
+++ b/solution.py
@@ -139,6 +139,22 @@
 
 def along_lanes(values, lanes):
     return jnp.take_along_axis(values, lanes, axis=1, mode="promise_in_bounds")
+
+
+def along_lanes_of_halves(values, lanes):
+    return lax.gather(
+        values,
+        lanes[..., None],
+        lax.GatherDimensionNumbers(
+            offset_dims=(),
+            collapsed_slice_dims=(1,),
+            start_index_map=(1,),
+            operand_batching_dims=(0,),
+            start_indices_batching_dims=(0,),
+        ),
+        slice_sizes=(1, 1),
+        mode=lax.GatherScatterMode.PROMISE_IN_BOUNDS,
+    )
 
 
 def table_kernel(
@@ -178,8 +194,13 @@
             slot = sublane * width + k
             for t in range(tiles):
                 found[t] = jnp.where(column == lane + t * LANES, slot, found[t])
-        for t in range(tiles):
-            slots_ref[rows, t * LANES : (t + 1) * LANES] = found[t]
+        if r % 2 == 1:
+            both = slice((r - 1) * SUBLANES, (r + 1) * SUBLANES)
+            for t in range(tiles):
+                slots_ref[both, t * LANES : (t + 1) * LANES] = jnp.concatenate(
+                    [found_before[t], found[t]], axis=0
+                ).astype(jnp.int16)
+        found_before = found
         for e in range(energies):
             samples[e, :, r, :] = phonon_ref[e, 0, :, r * LANES : (r + 1) * LANES].astype(
                 jnp.float32
@@ -429,17 +450,24 @@
     copies = []
     for e, green_ref in enumerate((green_even_ref, green_odd_ref)):
         for q in range(groups // 2):
+            both = slice(q * 16, (q + 1) * 16)
+            held = [
+                jnp.concatenate(
+                    [
+                        jnp.broadcast_to(merged[e, c, r : r + 1, :], (SUBLANES, LANES))
+                        for r in (2 * q, 2 * q + 1)
+                    ],
+                    axis=0,
+                ).astype(jnp.bfloat16)
+                for c in range(2)
+            ]
             for t in range(tiles):
-                found = [[], []]
-                for r in (2 * q, 2 * q + 1):
-                    slot = slots_ref[r * SUBLANES : (r + 1) * SUBLANES, t * LANES : (t + 1) * LANES]
-                    within = slot & (LANES - 1)
-                    for c in range(2):
-                        row = jnp.broadcast_to(merged[e, c, r : r + 1, :], (SUBLANES, LANES))
-                        found[c].append(jnp.where(slot >= 0, along_lanes(row, within), 0.0))
+                columns = slice(t * LANES, (t + 1) * LANES)
+                slot = slots_ref[both, columns]
+                within = slot & jnp.int16(LANES - 1)
                 for c in range(2):
-                    self_block[e, c, q * 16 : (q + 1) * 16, t * LANES : (t + 1) * LANES] = (
-                        jnp.concatenate(found[c], axis=0).astype(jnp.bfloat16)
+                    self_block[e, c, both, columns] = jnp.where(
+                        slot >= 0, along_lanes_of_halves(held[c], within), jnp.bfloat16(0)
                     )
     for e, green_ref in enumerate((green_even_ref, green_odd_ref)):
         green = [green_ref[c] for c in range(2)]
@@ -527,7 +555,7 @@
         functools.partial(table_kernel, width),
         (
             shape((orbitals, LANES), jnp.int32),
-            shape((orbitals, padded), jnp.int32),
+            shape((orbitals, padded), jnp.int16),
             shape((energies, 2, height, LANES), bf16),
             pltpu.VMEM(lead_green.shape, bf16),
             pltpu.VMEM(coupling.shape, bf16),

time: 56.7 us -> 56.1 us (0.989)
    pallas_call x1, Pallas kernels: 5.24 us -> 4.66 us  [body(): call(final_kernel, shape((energies, 1, 2, *plane), bf16), [IN_VMEM] * (4...]
  transfers between devices with their start and end apart: 9 -> 9, of which waited for: 2 -> 2; matrix products, arithmetic and copies ran while one was open for 0% -> 0% of each run, Pallas kernels for 26% -> 27%
where the time goes in v6:
time: 56.1 us; the launch traced here: 55.9 us
  Pallas kernels  25.6 us (46%)
  starting transfers between devices  17.2 us (31%)
  blocking collectives  11.2 us (20%)
  waiting for transfers between devices  1.45 us (3%)
    all_gather x1, blocking collectives, body(): samples = lax.all_gather(samples, 'energy', axis=0, tiled=True)  11.2 us
    ppermute x4, starting transfers between devices, body(): lax.ppermute(x, 'domain', route)  7.53 us
    pallas_call x2, Pallas kernels, body(): call(functools.partial(send_kernel, e), (shape((rows, LANES), bf16), shap...  6.63 us
    ppermute x3, starting transfers between devices, body(): sources += [array, lax.ppermute(array, 'energy', swap)]  5.27 us
    pallas_call x1, Pallas kernels, body(): call(final_kernel, shape((energies, 1, 2, *plane), bf16), [IN_VMEM] * (4...  4.66 us
    ppermute x1, starting transfers between devices, body(): beside = lax.ppermute(pair, 'energy', [(i, i ^ 2) for i in range(devices)])  3.73 us
    pallas_call x1, Pallas kernels, body(): call(functools.partial(green_kernel, width), (block, shape(pair_shape, bf...  3.44 us
    pallas_call x1, Pallas kernels, body(): call(functools.partial(table_kernel, width), (shape((orbitals, LANES), jn...  2.99 us
  transfers between devices with their start and end apart: 9, of which 2 were waited for; matrix products, arithmetic and copies ran while one was open for 0% of the time, Pallas kernels for 27%

profile of v6, /device:TPU:17, one launch (start us, length us, event | category | flops | bytes accessed | tf_op | source)
XLA Modules:
  0.0 55.9 jit_solution(7042938850477857398)
XLA Ops:
  0.0 0.0 copy-start.2
  0.0 3.5 %shard_map.64 = (bf16[2704,128]{1,0:T(8,128)(2,1)}, bf16[2704,128]{1,0:T(8,128)(2,1)}) custom-call(bf16[2,1,2,416,416]{4,3,2,1,0:T(8,128)(2,1)} %inverses_ref.4, bf16[1,416,416]{2,1,0:T(8,128)(2,1)} %coupling_ref.5), custom_call_target="tpu_custom_call" | custom-call | flops 575930368 | bytes 1048576 | tf_op jit(solution)/shard_map/pallas_call | solution.py:535
  3.5 0.0 copy-start
  3.5 1.4 %collective-permute-start.1 = (bf16[2704,128]{1,0:T(8,128)(2,1)}, bf16[2704,128]{1,0:T(8,128)(2,1)S(1)}, u32[]{:S(2)}, u32[]{:S(2)}) collective-permute-start(bf16[2704,128]{1,0:T(8,128)(2,1)} %get-tuple-element.33), channel_id=1, source_target_pairs={{0,1},{1,0},{2,3},{3,2},{4,5},{5,4},{6,7},{7,6},{8,9},{9,8},{10,11... | collective-permute-start | bytes 2076680 | tf_op jit(solution)/shard_map/ppermute | solution.py:551
  4.9 1.9 %collective-permute-start.2 = (bf16[2704,128]{1,0:T(8,128)(2,1)}, bf16[2704,128]{1,0:T(8,128)(2,1)}, u32[]{:S(2)}, u32[]{:S(2)}) collective-permute-start(bf16[2704,128]{1,0:T(8,128)(2,1)} %get-tuple-element.36), channel_id=1, source_target_pairs={{1,2},{2,1},{5,6},{6,5},{9,10},{10,9},{13,14},{14,13},{17,18},{18,... | collective-permute-start | bytes 2076680 | tf_op jit(solution)/shard_map/ppermute | solution.py:551
  6.8 3.1 %shard_map.65 = (bf16[2704,128]{1,0:T(8,128)(2,1)}, bf16[2704,128]{1,0:T(8,128)(2,1)S(1)}) custom-call(bf16[2,1,2,416,416]{4,3,2,1,0:T(8,128)(2,1)} %inverses_ref.4, bf16[1,416,416]{2,1,0:T(8,128)(2,1)} %coupling_ref.5), custom_call_target="tpu_custom_call" | custom-call | flops 575930368 | bytes 1048576 | tf_op jit(solution)/shard_map/pallas_call | solution.py:535
  10.0 0.0 copy-start.1
  10.0 0.5 collective-permute-start
  10.5 3.7 %collective-permute-start.3 = (bf16[2704,128]{1,0:T(8,128)(2,1)S(1)}, bf16[2704,128]{1,0:T(8,128)(2,1)S(1)}, u32[]{:S(2)}, u32[]{:S(2)}) collective-permute-start(bf16[2704,128]{1,0:T(8,128)(2,1)S(1)} %get-tuple-element.53), channel_id=1, source_target_pairs={{1,2},{2,1},{5,6},{6,5},{9,10},{10,9},{13,14},{14,13},{17,18},{18,... | collective-permute-start | bytes 2076680 | tf_op jit(solution)/shard_map/ppermute | solution.py:551
  14.2 0.0 copy-done.2
  14.2 0.1 copy.8.neighbors_ref
  14.4 0.0 copy-done
  14.4 3.0 %shard_map.67 = (s32[416,128]{1,0:T(8,128)S(1)}, s16[416,512]{1,0:T(8,128)(2,1)S(1)}, bf16[2,2,64,128]{3,2,1,0:T(8,128)(2,1)S(1)}, bf16[2,2,416,416]{3,2,1,0:T(8,128)(2,1)S(1)}, bf16[1,416,416]{2,1,0:T(8,128)(2,1)S(1)}) custom-call(s32[1,416,16]{2,1,0:T(8,128)S(1)} %copy.8.neighbors_ref, bf16[2,1,2,6656]{3,2,1,0:T(2,128)(2,1)S(1)} %copy-done, ...), custom_call_target="tpu_custom_call" | custom-call | flops 575930368 | bytes 1048576 | tf_op jit(solution)/shard_map/pallas_call | solution.py:554
  17.4 11.2 %all_gather.3.samples_ref = bf16[16,2,64,128]{3,2,1,0:T(8,128)(2,1)S(1)} all-gather(bf16[2,2,64,128]{3,2,1,0:T(8,128)(2,1)S(1)} %get-tuple-element.46), channel_id=1, replica_groups=mesh['energy'=8,'domain'=4] {'energy'}, dimensions={0}, use_global_device_ids=true | all-gather | bytes 589824 | tf_op jit(solution)/shard_map/all_gather | solution.py:572
  28.6 0.0 copy-done.1
  28.6 0.8 %shard_map.70.grouped_ref = f32[9,2,64,128]{3,2,1,0:T(8,128)S(1)} custom-call(s32[16]{0:T(128)S(1)} %copy-done.1, bf16[16,2,64,128]{3,2,1,0:T(8,128)(2,1)S(1)} %all_gather.3.samples_ref), custom_call_target="tpu_custom_call" | custom-call | bytes 1048576 | tf_op jit(solution)/shard_map/pallas_call | solution.py:605
  29.4 0.0 collective-permute-done.1.packed_ref
  29.4 0.3 shard_map.66.first_planes
  29.6 0.0 collective-permute-done.2.second_ref
  29.7 2.3 %shard_map.68 = (bf16[2,416,416]{2,1,0:T(8,128)(2,1)S(1)}, bf16[2,416,416]{2,1,0:T(8,128)(2,1)S(1)}, bf16[2,416,416]{2,1,0:T(8,128)(2,1)S(1)}, bf16[2,416,416]{2,1,0:T(8,128)(2,1)S(1)}, bf16[2704,128]{1,0:T(8,128)(2,1)S(1)}) custom-call(bf16[2,1,2,416,416]{4,3,2,1,0:T(8,128)(2,1)} %inverses_ref.4, bf16[2704,128]{1,0:T(8,128)(2,1)} %collective-permute-done.2.second_ref, ...), custom_call_target="tpu_custom_call" | custom-call | flops 575930368 | bytes 1048576 | tf_op jit(solution)/shard_map/pallas_call | solution.py:583
  32.0 3.4 %shard_map.69 = (bf16[2,416,416]{2,1,0:T(8,128)(2,1)S(1)}, bf16[1,2,64,128]{3,2,1,0:T(8,128)(2,1)S(1)}) custom-call(bf16[2704,128]{1,0:T(8,128)(2,1)S(1)} %get-tuple-element.41.second_ref, bf16[2,416,416]{2,1,0:T(8,128)(2,1)S(1)} %shard_map.66.first_planes, bf16[2,2,416,416]{3,2,1,0:T(8,128)(2,1)S(1)} %get-tuple-element.43.lead_ref, ...), custom_call_target="tpu_custom_call" | custom-call | flops 1727791104 | bytes 1048576 | tf_op jit(solution)/shard_map/pallas_call | solution.py:590
  35.5 0.0 collective-permute-done.first_ref
  35.5 1.9 %shard_map.71.sum_ref = f32[2,416,416]{2,1,0:T(8,128)S(1)} custom-call(bf16[2704,128]{1,0:T(8,128)(2,1)S(1)} %collective-permute-done.first_ref, bf16[2,2,416,416]{3,2,1,0:T(8,128)(2,1)S(1)} %get-tuple-element.43.lead_ref, bf16[2,416,416]{2,1,0:T(8,128)(2,1)S(1)} %get-tuple-element.55.before_ref, bf16[2,416,416]{2,1,0:T(8,128)(2,1)S(1)} %get-tuple-element.56.after_ref, ...), custom_call_target="tpu_custom_call" | custom-call | flops 863895552 | bytes 1048576 | tf_op jit(solution)/shard_map/pallas_call | solution.py:611
  37.4 0.5 collective-permute-done.3.second_ref
  37.9 2.6 %shard_map.72 = (bf16[2,416,416]{2,1,0:T(8,128)(2,1)S(1)}, bf16[2,2,64,128]{3,2,1,0:T(8,128)(2,1)S(1)}) custom-call(bf16[2704,128]{1,0:T(8,128)(2,1)S(1)} %collective-permute-done.3.second_ref, bf16[2704,128]{1,0:T(8,128)(2,1)S(1)} %collective-permute-done.first_ref, bf16[2,416,416]{2,1,0:T(8,128)(2,1)S(1)} %get-tuple-element.55.before_ref, ...), custom_call_target="tpu_custom_call" | custom-call | flops 863895552 | bytes 1048576 | tf_op jit(solution)/shard_map/pallas_call | solution.py:619
  40.5 0.7 %collective-permute-start.5 = (bf16[2,2,64,128]{3,2,1,0:T(8,128)(2,1)S(1)}, bf16[2,2,64,128]{3,2,1,0:T(8,128)(2,1)S(1)}, u32[]{:S(2)}, u32[]{:S(2)}) collective-permute-start(bf16[2,2,64,128]{3,2,1,0:T(8,128)(2,1)S(1)} %get-tuple-element.60.rest_0_), channel_id=1, source_target_pairs={{8,16},{12,20},{16,8},{20,12},{9,17},{13,21},{17,9},{21,13},{10,18... | collective-permute-start | bytes 196616 | tf_op jit(solution)/shard_map/ppermute | solution.py:635
  41.1 3.7 %collective-permute-start.7 = (bf16[2,2,64,128]{3,2,1,0:T(8,128)(2,1)S(1)}, bf16[2,2,64,128]{3,2,1,0:T(8,128)(2,1)S(1)}, u32[]{:S(2)}, u32[]{:S(2)}) collective-permute-start(bf16[2,2,64,128]{3,2,1,0:T(8,128)(2,1)S(1)} %get-tuple-element.60.rest_0_), channel_id=1, source_target_pairs={{0,8},{4,12},{8,0},{12,4},{16,24},{20,28},{24,16},{28,20},{1,9},{5... | collective-permute-start | bytes 196616 | tf_op jit(solution)/shard_map/ppermute | solution.py:634
  44.9 2.4 %collective-permute-start.4 = (bf16[2,2,64,128]{3,2,1,0:T(8,128)(2,1)S(1)}, bf16[2,2,64,128]{3,2,1,0:T(8,128)(2,1)S(1)}, u32[]{:S(2)}, u32[]{:S(2)}) collective-permute-start(bf16[2,2,64,128]{3,2,1,0:T(8,128)(2,1)S(1)} %get-tuple-element.60.rest_0_), channel_id=1, source_target_pairs={{0,4},{4,0},{8,12},{12,8},{16,20},{20,16},{24,28},{28,24},{1,5},{5... | collective-permute-start | bytes 196616 | tf_op jit(solution)/shard_map/ppermute | solution.py:638
  47.3 0.0 collective-permute-done.5.rest_2_
  47.3 0.0 collective-permute-start.6
  47.3 0.0 collective-permute-done.7.rest_4_
  47.3 2.8 %collective-permute-start.8 = (bf16[2,2,64,128]{3,2,1,0:T(8,128)(2,1)S(1)}, bf16[2,2,64,128]{3,2,1,0:T(8,128)(2,1)S(1)}, u32[]{:S(2)}, u32[]{:S(2)}) collective-permute-start(bf16[2,2,64,128]{3,2,1,0:T(8,128)(2,1)S(1)} %collective-permute-done.7.rest_4_), channel_id=1, source_target_pairs={{0,4},{4,0},{8,12},{12,8},{16,20},{20,16},{24,28},{28,24},{1,5},{5... | collective-permute-start | bytes 196616 | tf_op jit(solution)/shard_map/ppermute | solution.py:638
  50.2 0.0 collective-permute-done.4.rest_1_
  50.2 0.0 collective-permute-done.6.rest_3_
  50.2 0.9 %collective-permute-done.8.rest_5_ = bf16[2,2,64,128]{3,2,1,0:T(8,128)(2,1)S(1)} collective-permute-done((bf16[2,2,64,128]{3,2,1,0:T(8,128)(2,1)S(1)}, bf16[2,2,64,128]{3,2,1,0:T(8,128)(2,1)S(1)}, u32[]{:S(2)}, u32[]{:S(2)}) %collective-permute-start.8) | collective-permute-done | bytes 65568 | tf_op jit(solution)/shard_map/ppermute | solution.py:638
  51.1 4.7 %shard_map.73 = bf16[2,1,2,416,416]{4,3,2,1,0:T(8,128)(2,1)} custom-call(f32[9,2,64,128]{3,2,1,0:T(8,128)S(1)} %shard_map.70.grouped_ref, s16[416,512]{1,0:T(8,128)(2,1)S(1)} %get-tuple-element.51.slots_ref, bf16[2,416,416]{2,1,0:T(8,128)(2,1)S(1)} %get-tuple-element.52.green_even_ref, bf16[2,416,416]{2,1,0:T(8,128)(2,1)S(1)} %get-tuple-element.59.green_odd_ref, ...), custom_call_target="tpu_custom_call" | custom-call | flops 2303721472 | bytes 1048576 | tf_op jit(solution)/shard_map/pallas_call | solution.py:642
Async XLA Ops:
  0.0 14.2 %copy-start.2 = (s32[1,416,16]{1,2,0:T(8,128)S(1)}, s32[1,416,16]{1,2,0:T(8,128)}, u32[]{:S(2)}) copy-start(s32[1,416,16]{1,2,0:T(8,128)} %param.10) | copy-start | bytes 79876
  3.5 10.9 %copy-start = (bf16[2,1,2,6656]{3,2,1,0:T(2,128)(2,1)S(1)}, bf16[2,1,2,6656]{3,2,1,0:T(2,128)(2,1)}, u32[]{:S(2)}) copy-start(bf16[2,1,2,6656]{3,2,1,0:T(2,128)(2,1)} %phonon_ref.1) | copy-start | bytes 159748
  3.5 25.9 %collective-permute-start.1 = (bf16[2704,128]{1,0:T(8,128)(2,1)}, bf16[2704,128]{1,0:T(8,128)(2,1)S(1)}, u32[]{:S(2)}, u32[]{:S(2)}) collective-permute-start(bf16[2704,128]{1,0:T(8,128)(2,1)} %get-tuple-element.33), channel_id=1, source_target_pairs={{0,1},{1,0},{2,3},{3,2},{4,5},{5,4},{6,7},{7,6},{8,9},{9,8},{10,11... | collective-permute-start | bytes 2076680 | tf_op jit(solution)/shard_map/ppermute | solution.py:551
  4.9 24.7 %collective-permute-start.2 = (bf16[2704,128]{1,0:T(8,128)(2,1)}, bf16[2704,128]{1,0:T(8,128)(2,1)}, u32[]{:S(2)}, u32[]{:S(2)}) collective-permute-start(bf16[2704,128]{1,0:T(8,128)(2,1)} %get-tuple-element.36), channel_id=1, source_target_pairs={{1,2},{2,1},{5,6},{6,5},{9,10},{10,9},{13,14},{14,13},{17,18},{18,... | collective-permute-start | bytes 2076680 | tf_op jit(solution)/shard_map/ppermute | solution.py:551
  10.0 18.6 %copy-start.1 = (s32[16]{0:T(128)S(1)}, s32[16]{0:T(128)}, u32[]{:S(2)}) copy-start(s32[16]{0:T(128)} %shifts_ref.1) | copy-start | bytes 196
  10.0 25.5 %collective-permute-start = (bf16[2704,128]{1,0:T(8,128)(2,1)}, bf16[2704,128]{1,0:T(8,128)(2,1)S(1)}, u32[]{:S(2)}, u32[]{:S(2)}) collective-permute-start(bf16[2704,128]{1,0:T(8,128)(2,1)} %get-tuple-element.35), channel_id=1, source_target_pairs={{0,1},{1,0},{2,3},{3,2},{4,5},{5,4},{6,7},{7,6},{8,9},{9,8},{10,11... | collective-permute-start | bytes 2076680 | tf_op jit(solution)/shard_map/ppermute | solution.py:551
  10.5 27.4 %collective-permute-start.3 = (bf16[2704,128]{1,0:T(8,128)(2,1)S(1)}, bf16[2704,128]{1,0:T(8,128)(2,1)S(1)}, u32[]{:S(2)}, u32[]{:S(2)}) collective-permute-start(bf16[2704,128]{1,0:T(8,128)(2,1)S(1)} %get-tuple-element.53), channel_id=1, source_target_pairs={{1,2},{2,1},{5,6},{6,5},{9,10},{10,9},{13,14},{14,13},{17,18},{18,... | collective-permute-start | bytes 2076680 | tf_op jit(solution)/shard_map/ppermute | solution.py:551
  40.5 6.8 %collective-permute-start.5 = (bf16[2,2,64,128]{3,2,1,0:T(8,128)(2,1)S(1)}, bf16[2,2,64,128]{3,2,1,0:T(8,128)(2,1)S(1)}, u32[]{:S(2)}, u32[]{:S(2)}) collective-permute-start(bf16[2,2,64,128]{3,2,1,0:T(8,128)(2,1)S(1)} %get-tuple-element.60.rest_0_), channel_id=1, source_target_pairs={{8,16},{12,20},{16,8},{20,12},{9,17},{13,21},{17,9},{21,13},{10,18... | collective-permute-start | bytes 196616 | tf_op jit(solution)/shard_map/ppermute | solution.py:635
  41.1 6.2 %collective-permute-start.7 = (bf16[2,2,64,128]{3,2,1,0:T(8,128)(2,1)S(1)}, bf16[2,2,64,128]{3,2,1,0:T(8,128)(2,1)S(1)}, u32[]{:S(2)}, u32[]{:S(2)}) collective-permute-start(bf16[2,2,64,128]{3,2,1,0:T(8,128)(2,1)S(1)} %get-tuple-element.60.rest_0_), channel_id=1, source_target_pairs={{0,8},{4,12},{8,0},{12,4},{16,24},{20,28},{24,16},{28,20},{1,9},{5... | collective-permute-start | bytes 196616 | tf_op jit(solution)/shard_map/ppermute | solution.py:634
  44.9 5.3 %collective-permute-start.4 = (bf16[2,2,64,128]{3,2,1,0:T(8,128)(2,1)S(1)}, bf16[2,2,64,128]{3,2,1,0:T(8,128)(2,1)S(1)}, u32[]{:S(2)}, u32[]{:S(2)}) collective-permute-start(bf16[2,2,64,128]{3,2,1,0:T(8,128)(2,1)S(1)} %get-tuple-element.60.rest_0_), channel_id=1, source_target_pairs={{0,4},{4,0},{8,12},{12,8},{16,20},{20,16},{24,28},{28,24},{1,5},{5... | collective-permute-start | bytes 196616 | tf_op jit(solution)/shard_map/ppermute | solution.py:638
  47.3 2.9 %collective-permute-start.6 = (bf16[2,2,64,128]{3,2,1,0:T(8,128)(2,1)S(1)}, bf16[2,2,64,128]{3,2,1,0:T(8,128)(2,1)S(1)}, u32[]{:S(2)}, u32[]{:S(2)}) collective-permute-start(bf16[2,2,64,128]{3,2,1,0:T(8,128)(2,1)S(1)} %collective-permute-done.5.rest_2_), channel_id=1, source_target_pairs={{0,4},{4,0},{8,12},{12,8},{16,20},{20,16},{24,28},{28,24},{1,5},{5... | collective-permute-start | bytes 196616 | tf_op jit(solution)/shard_map/ppermute | solution.py:638
  47.3 3.7 %collective-permute-start.8 = (bf16[2,2,64,128]{3,2,1,0:T(8,128)(2,1)S(1)}, bf16[2,2,64,128]{3,2,1,0:T(8,128)(2,1)S(1)}, u32[]{:S(2)}, u32[]{:S(2)}) collective-permute-start(bf16[2,2,64,128]{3,2,1,0:T(8,128)(2,1)S(1)} %collective-permute-done.7.rest_4_), channel_id=1, source_target_pairs={{0,4},{4,0},{8,12},{12,8},{16,20},{20,16},{24,28},{28,24},{1,5},{5... | collective-permute-start | bytes 196616 | tf_op jit(solution)/shard_map/ppermute | solution.py:638

commit v7 on v6

--- a/solution.py
+++ b/solution.py
@@ -184,7 +184,6 @@
         rows = slice(r * SUBLANES, (r + 1) * SUBLANES)
         group = wide[rows, :]
         columns = along_lanes(group, lane % width)
-        columns_ref[rows, :] = columns
         flat[r : r + 1, :] = jnp.sum(
             jnp.where(own, columns.astype(jnp.float32), 0.0), axis=0, keepdims=True
         )
@@ -196,11 +195,12 @@
                 found[t] = jnp.where(column == lane + t * LANES, slot, found[t])
         if r % 2 == 1:
             both = slice((r - 1) * SUBLANES, (r + 1) * SUBLANES)
+            columns_ref[both, :] = jnp.concatenate([columns_before, columns], axis=0).astype(jnp.int16)
             for t in range(tiles):
                 slots_ref[both, t * LANES : (t + 1) * LANES] = jnp.concatenate(
                     [found_before[t], found[t]], axis=0
                 ).astype(jnp.int16)
-        found_before = found
+        found_before, columns_before = found, columns
         for e in range(energies):
             samples[e, :, r, :] = phonon_ref[e, 0, :, r * LANES : (r + 1) * LANES].astype(
                 jnp.float32
@@ -268,7 +268,7 @@
     for c, part in enumerate(complex_product(own, inner)):
         green = (own[c].astype(jnp.float32) + part).astype(jnp.bfloat16)
         green_ref[c] = green
-        wide[c, :, :orbitals] = green.astype(jnp.float32)
+        wide[c, :, :orbitals] = green
     gather_pairs(width, wide, columns_ref, flat, pair_ref, 0)
 
 
@@ -355,7 +355,7 @@
         for c in range(2):
             green = values[c].astype(jnp.bfloat16)
             green_ref[c] = green
-            wide[c, :, :orbitals] = green.astype(jnp.float32)
+            wide[c, :, :orbitals] = green
 
     @pl.when(from_before)
     def _():
@@ -375,17 +375,19 @@
     sublane, lane = group_iotas()
     own = sublane == lane // width
     flat[...] = jnp.zeros(flat.shape, flat.dtype)
-    for r in range(orbitals // SUBLANES):
-        rows = slice(r * SUBLANES, (r + 1) * SUBLANES)
-        columns = columns_ref[rows, :]
-        within = columns & (LANES - 1)
-        tile = columns // LANES
+    for q in range(orbitals // 16):
+        both = slice(q * 16, (q + 1) * 16)
+        columns = columns_ref[both, :]
+        within = columns & jnp.int16(LANES - 1)
         for c in range(2):
-            taken = jnp.zeros((SUBLANES, LANES), jnp.float32)
-            for t in range(tiles):
-                candidate = along_lanes(wide[c, rows, t * LANES : (t + 1) * LANES], within)
-                taken = jnp.where(own & (tile == t), candidate, taken)
-            flat[c, r : r + 1, :] = jnp.sum(taken, axis=0, keepdims=True)
+            taken = along_lanes_of_halves(wide[c, both, :LANES], within)
+            for t in range(1, tiles):
+                candidate = along_lanes_of_halves(wide[c, both, t * LANES : (t + 1) * LANES], within)
+                taken = jnp.where(columns >= jnp.int16(t * LANES), candidate, taken)
+            values = taken.astype(jnp.float32)
+            for k in range(2):
+                half = jnp.where(own, values[k * SUBLANES : (k + 1) * SUBLANES], 0.0)
+                flat[c, 2 * q + k : 2 * q + k + 1, :] = jnp.sum(half, axis=0, keepdims=True)
     pair_ref[place] = flat[...].astype(jnp.bfloat16)
 
 
@@ -554,7 +556,7 @@
     columns, slots, samples, lead, coupling = call(
         functools.partial(table_kernel, width),
         (
-            shape((orbitals, LANES), jnp.int32),
+            shape((orbitals, LANES), jnp.int16),
             shape((orbitals, padded), jnp.int16),
             shape((energies, 2, height, LANES), bf16),
             pltpu.VMEM(lead_green.shape, bf16),
@@ -594,7 +596,7 @@
         [
             pltpu.VMEM((2, *plane), bf16),
             pltpu.VMEM((2, *plane), bf16),
-            pltpu.VMEM((2, orbitals, padded), f32),
+            pltpu.VMEM((2, orbitals, padded), bf16),
             pltpu.VMEM((2, height, LANES), f32),
         ],
         flops=12 * cube,
@@ -622,7 +624,7 @@
         [IN_VMEM] * 8,
         [
             pltpu.VMEM((2, *plane), bf16),
-            pltpu.VMEM((2, orbitals, padded), f32),
+            pltpu.VMEM((2, orbitals, padded), bf16),
             pltpu.VMEM((2, height, LANES), f32),
         ],
         flops=6 * cube,

time: 56.1 us -> 55.6 us (level)
  Pallas kernels: 25.6 us -> 24.7 us
  transfers between devices with their start and end apart: 9 -> 9, of which waited for: 2 -> 2; matrix products, arithmetic and copies ran while one was open for 0% -> 0% of each run, Pallas kernels for 27% -> 26%
where the time goes in v7:
time: 55.6 us; the launch traced here: 55.4 us
  Pallas kernels  24.7 us (44%)
  starting transfers between devices  17.2 us (31%)
  blocking collectives  11.2 us (20%)
  waiting for transfers between devices  1.8 us (3%)
    all_gather x1, blocking collectives, body(): samples = lax.all_gather(samples, 'energy', axis=0, tiled=True)  11.2 us
    ppermute x4, starting transfers between devices, body(): lax.ppermute(x, 'domain', route)  7.53 us
    pallas_call x2, Pallas kernels, body(): call(functools.partial(send_kernel, e), (shape((rows, LANES), bf16), shap...  6.63 us
    ppermute x3, starting transfers between devices, body(): sources += [array, lax.ppermute(array, 'energy', swap)]  5.28 us
    pallas_call x1, Pallas kernels, body(): call(final_kernel, shape((energies, 1, 2, *plane), bf16), [IN_VMEM] * (4...  4.61 us
    ppermute x1, starting transfers between devices, body(): beside = lax.ppermute(pair, 'energy', [(i, i ^ 2) for i in range(devices)])  3.72 us
    pallas_call x1, Pallas kernels, body(): call(functools.partial(green_kernel, width), (block, shape(pair_shape, bf...  3.13 us
    pallas_call x1, Pallas kernels, body(): call(functools.partial(table_kernel, width), (shape((orbitals, LANES), jn...  2.98 us
  transfers between devices with their start and end apart: 9, of which 2 were waited for; matrix products, arithmetic and copies ran while one was open for 0% of the time, Pallas kernels for 26%

profile of v7, /device:TPU:17, one launch (start us, length us, event | category | flops | bytes accessed | tf_op | source)
XLA Modules:
  0.0 55.4 jit_solution(5270672132218887327)
XLA Ops:
  0.0 0.0 copy-start.2
  0.0 3.5 %shard_map.64 = (bf16[2704,128]{1,0:T(8,128)(2,1)}, bf16[2704,128]{1,0:T(8,128)(2,1)}) custom-call(bf16[2,1,2,416,416]{4,3,2,1,0:T(8,128)(2,1)} %inverses_ref.4, bf16[1,416,416]{2,1,0:T(8,128)(2,1)} %coupling_ref.5), custom_call_target="tpu_custom_call" | custom-call | flops 575930368 | bytes 1048576 | tf_op jit(solution)/shard_map/pallas_call | solution.py:537
  3.5 0.0 copy-start
  3.5 1.4 %collective-permute-start.1 = (bf16[2704,128]{1,0:T(8,128)(2,1)}, bf16[2704,128]{1,0:T(8,128)(2,1)S(1)}, u32[]{:S(2)}, u32[]{:S(2)}) collective-permute-start(bf16[2704,128]{1,0:T(8,128)(2,1)} %get-tuple-element.33), channel_id=1, source_target_pairs={{0,1},{1,0},{2,3},{3,2},{4,5},{5,4},{6,7},{7,6},{8,9},{9,8},{10,11... | collective-permute-start | bytes 2076680 | tf_op jit(solution)/shard_map/ppermute | solution.py:553
  4.9 1.9 %collective-permute-start.2 = (bf16[2704,128]{1,0:T(8,128)(2,1)}, bf16[2704,128]{1,0:T(8,128)(2,1)}, u32[]{:S(2)}, u32[]{:S(2)}) collective-permute-start(bf16[2704,128]{1,0:T(8,128)(2,1)} %get-tuple-element.36), channel_id=1, source_target_pairs={{1,2},{2,1},{5,6},{6,5},{9,10},{10,9},{13,14},{14,13},{17,18},{18,... | collective-permute-start | bytes 2076680 | tf_op jit(solution)/shard_map/ppermute | solution.py:553
  6.8 3.1 %shard_map.65 = (bf16[2704,128]{1,0:T(8,128)(2,1)}, bf16[2704,128]{1,0:T(8,128)(2,1)S(1)}) custom-call(bf16[2,1,2,416,416]{4,3,2,1,0:T(8,128)(2,1)} %inverses_ref.4, bf16[1,416,416]{2,1,0:T(8,128)(2,1)} %coupling_ref.5), custom_call_target="tpu_custom_call" | custom-call | flops 575930368 | bytes 1048576 | tf_op jit(solution)/shard_map/pallas_call | solution.py:537
  10.0 0.0 copy-start.1
  10.0 0.5 collective-permute-start
  10.5 3.7 %collective-permute-start.3 = (bf16[2704,128]{1,0:T(8,128)(2,1)S(1)}, bf16[2704,128]{1,0:T(8,128)(2,1)S(1)}, u32[]{:S(2)}, u32[]{:S(2)}) collective-permute-start(bf16[2704,128]{1,0:T(8,128)(2,1)S(1)} %get-tuple-element.53), channel_id=1, source_target_pairs={{1,2},{2,1},{5,6},{6,5},{9,10},{10,9},{13,14},{14,13},{17,18},{18,... | collective-permute-start | bytes 2076680 | tf_op jit(solution)/shard_map/ppermute | solution.py:553
  14.2 0.0 copy-done.2
  14.2 0.1 copy.8.neighbors_ref
  14.4 0.0 copy-done
  14.4 3.0 %shard_map.67 = (s16[416,128]{1,0:T(8,128)(2,1)S(1)}, s16[416,512]{1,0:T(8,128)(2,1)S(1)}, bf16[2,2,64,128]{3,2,1,0:T(8,128)(2,1)S(1)}, bf16[2,2,416,416]{3,2,1,0:T(8,128)(2,1)S(1)}, bf16[1,416,416]{2,1,0:T(8,128)(2,1)S(1)}) custom-call(s32[1,416,16]{2,1,0:T(8,128)S(1)} %copy.8.neighbors_ref, bf16[2,1,2,6656]{3,2,1,0:T(2,128)(2,1)S(1)} %copy-done, ...), custom_call_target="tpu_custom_call" | custom-call | flops 575930368 | bytes 1048576 | tf_op jit(solution)/shard_map/pallas_call | solution.py:556
  17.4 11.2 %all_gather.3.samples_ref = bf16[16,2,64,128]{3,2,1,0:T(8,128)(2,1)S(1)} all-gather(bf16[2,2,64,128]{3,2,1,0:T(8,128)(2,1)S(1)} %get-tuple-element.46), channel_id=1, replica_groups=mesh['energy'=8,'domain'=4] {'energy'}, dimensions={0}, use_global_device_ids=true | all-gather | bytes 589824 | tf_op jit(solution)/shard_map/all_gather | solution.py:574
  28.6 0.0 copy-done.1
  28.6 0.8 %shard_map.70.grouped_ref = f32[9,2,64,128]{3,2,1,0:T(8,128)S(1)} custom-call(s32[16]{0:T(128)S(1)} %copy-done.1, bf16[16,2,64,128]{3,2,1,0:T(8,128)(2,1)S(1)} %all_gather.3.samples_ref), custom_call_target="tpu_custom_call" | custom-call | bytes 1048576 | tf_op jit(solution)/shard_map/pallas_call | solution.py:607
  29.4 0.0 collective-permute-done.1.packed_ref
  29.4 0.3 shard_map.66.first_planes
  29.6 0.0 collective-permute-done.2.second_ref
  29.7 2.4 %shard_map.68 = (bf16[2,416,416]{2,1,0:T(8,128)(2,1)S(1)}, bf16[2,416,416]{2,1,0:T(8,128)(2,1)S(1)}, bf16[2,416,416]{2,1,0:T(8,128)(2,1)S(1)}, bf16[2,416,416]{2,1,0:T(8,128)(2,1)S(1)}, bf16[2704,128]{1,0:T(8,128)(2,1)S(1)}) custom-call(bf16[2,1,2,416,416]{4,3,2,1,0:T(8,128)(2,1)} %inverses_ref.4, bf16[2704,128]{1,0:T(8,128)(2,1)} %collective-permute-done.2.second_ref, ...), custom_call_target="tpu_custom_call" | custom-call | flops 575930368 | bytes 1048576 | tf_op jit(solution)/shard_map/pallas_call | solution.py:585
  32.0 3.1 %shard_map.69 = (bf16[2,416,416]{2,1,0:T(8,128)(2,1)S(1)}, bf16[1,2,64,128]{3,2,1,0:T(8,128)(2,1)S(1)}) custom-call(bf16[2704,128]{1,0:T(8,128)(2,1)S(1)} %get-tuple-element.41.second_ref, bf16[2,416,416]{2,1,0:T(8,128)(2,1)S(1)} %shard_map.66.first_planes, bf16[2,2,416,416]{3,2,1,0:T(8,128)(2,1)S(1)} %get-tuple-element.43.lead_ref, ...), custom_call_target="tpu_custom_call" | custom-call | flops 1727791104 | bytes 1048576 | tf_op jit(solution)/shard_map/pallas_call | solution.py:592
  35.2 0.0 collective-permute-done.first_ref
  35.2 1.9 %shard_map.71.sum_ref = f32[2,416,416]{2,1,0:T(8,128)S(1)} custom-call(bf16[2704,128]{1,0:T(8,128)(2,1)S(1)} %collective-permute-done.first_ref, bf16[2,2,416,416]{3,2,1,0:T(8,128)(2,1)S(1)} %get-tuple-element.43.lead_ref, bf16[2,416,416]{2,1,0:T(8,128)(2,1)S(1)} %get-tuple-element.55.before_ref, bf16[2,416,416]{2,1,0:T(8,128)(2,1)S(1)} %get-tuple-element.56.after_ref, ...), custom_call_target="tpu_custom_call" | custom-call | flops 863895552 | bytes 1048576 | tf_op jit(solution)/shard_map/pallas_call | solution.py:613
  37.0 0.9 %collective-permute-done.3.second_ref = bf16[2704,128]{1,0:T(8,128)(2,1)S(1)} collective-permute-done((bf16[2704,128]{1,0:T(8,128)(2,1)S(1)}, bf16[2704,128]{1,0:T(8,128)(2,1)S(1)}, u32[]{:S(2)}, u32[]{:S(2)}) %collective-permute-start.3) | collective-permute-done | bytes 692256 | tf_op jit(solution)/shard_map/ppermute | solution.py:553
  37.9 2.1 %shard_map.72 = (bf16[2,416,416]{2,1,0:T(8,128)(2,1)S(1)}, bf16[2,2,64,128]{3,2,1,0:T(8,128)(2,1)S(1)}) custom-call(bf16[2704,128]{1,0:T(8,128)(2,1)S(1)} %collective-permute-done.3.second_ref, bf16[2704,128]{1,0:T(8,128)(2,1)S(1)} %collective-permute-done.first_ref, bf16[2,416,416]{2,1,0:T(8,128)(2,1)S(1)} %get-tuple-element.55.before_ref, ...), custom_call_target="tpu_custom_call" | custom-call | flops 863895552 | bytes 1048576 | tf_op jit(solution)/shard_map/pallas_call | solution.py:621
  40.0 0.7 %collective-permute-start.5 = (bf16[2,2,64,128]{3,2,1,0:T(8,128)(2,1)S(1)}, bf16[2,2,64,128]{3,2,1,0:T(8,128)(2,1)S(1)}, u32[]{:S(2)}, u32[]{:S(2)}) collective-permute-start(bf16[2,2,64,128]{3,2,1,0:T(8,128)(2,1)S(1)} %get-tuple-element.60.rest_0_), channel_id=1, source_target_pairs={{8,16},{12,20},{16,8},{20,12},{9,17},{13,21},{17,9},{21,13},{10,18... | collective-permute-start | bytes 196616 | tf_op jit(solution)/shard_map/ppermute | solution.py:637
  40.7 3.7 %collective-permute-start.7 = (bf16[2,2,64,128]{3,2,1,0:T(8,128)(2,1)S(1)}, bf16[2,2,64,128]{3,2,1,0:T(8,128)(2,1)S(1)}, u32[]{:S(2)}, u32[]{:S(2)}) collective-permute-start(bf16[2,2,64,128]{3,2,1,0:T(8,128)(2,1)S(1)} %get-tuple-element.60.rest_0_), channel_id=1, source_target_pairs={{0,8},{4,12},{8,0},{12,4},{16,24},{20,28},{24,16},{28,20},{1,9},{5... | collective-permute-start | bytes 196616 | tf_op jit(solution)/shard_map/ppermute | solution.py:636
  44.4 2.4 %collective-permute-start.4 = (bf16[2,2,64,128]{3,2,1,0:T(8,128)(2,1)S(1)}, bf16[2,2,64,128]{3,2,1,0:T(8,128)(2,1)S(1)}, u32[]{:S(2)}, u32[]{:S(2)}) collective-permute-start(bf16[2,2,64,128]{3,2,1,0:T(8,128)(2,1)S(1)} %get-tuple-element.60.rest_0_), channel_id=1, source_target_pairs={{0,4},{4,0},{8,12},{12,8},{16,20},{20,16},{24,28},{28,24},{1,5},{5... | collective-permute-start | bytes 196616 | tf_op jit(solution)/shard_map/ppermute | solution.py:640
  46.8 0.0 collective-permute-done.5.rest_2_
  46.8 0.0 collective-permute-start.6
  46.9 0.0 collective-permute-done.7.rest_4_
  46.9 2.8 %collective-permute-start.8 = (bf16[2,2,64,128]{3,2,1,0:T(8,128)(2,1)S(1)}, bf16[2,2,64,128]{3,2,1,0:T(8,128)(2,1)S(1)}, u32[]{:S(2)}, u32[]{:S(2)}) collective-permute-start(bf16[2,2,64,128]{3,2,1,0:T(8,128)(2,1)S(1)} %collective-permute-done.7.rest_4_), channel_id=1, source_target_pairs={{0,4},{4,0},{8,12},{12,8},{16,20},{20,16},{24,28},{28,24},{1,5},{5... | collective-permute-start | bytes 196616 | tf_op jit(solution)/shard_map/ppermute | solution.py:640
  49.7 0.0 collective-permute-done.4.rest_1_
  49.7 0.0 collective-permute-done.6.rest_3_
  49.7 0.9 %collective-permute-done.8.rest_5_ = bf16[2,2,64,128]{3,2,1,0:T(8,128)(2,1)S(1)} collective-permute-done((bf16[2,2,64,128]{3,2,1,0:T(8,128)(2,1)S(1)}, bf16[2,2,64,128]{3,2,1,0:T(8,128)(2,1)S(1)}, u32[]{:S(2)}, u32[]{:S(2)}) %collective-permute-start.8) | collective-permute-done | bytes 65568 | tf_op jit(solution)/shard_map/ppermute | solution.py:640
  50.6 4.6 %shard_map.73 = bf16[2,1,2,416,416]{4,3,2,1,0:T(8,128)(2,1)} custom-call(f32[9,2,64,128]{3,2,1,0:T(8,128)S(1)} %shard_map.70.grouped_ref, s16[416,512]{1,0:T(8,128)(2,1)S(1)} %get-tuple-element.51.slots_ref, bf16[2,416,416]{2,1,0:T(8,128)(2,1)S(1)} %get-tuple-element.52.green_even_ref, bf16[2,416,416]{2,1,0:T(8,128)(2,1)S(1)} %get-tuple-element.59.green_odd_ref, ...), custom_call_target="tpu_custom_call" | custom-call | flops 2303721472 | bytes 1048576 | tf_op jit(solution)/shard_map/pallas_call | solution.py:644
Async XLA Ops:
  0.0 14.2 %copy-start.2 = (s32[1,416,16]{1,2,0:T(8,128)S(1)}, s32[1,416,16]{1,2,0:T(8,128)}, u32[]{:S(2)}) copy-start(s32[1,416,16]{1,2,0:T(8,128)} %param.10) | copy-start | bytes 79876
  3.5 10.9 %copy-start = (bf16[2,1,2,6656]{3,2,1,0:T(2,128)(2,1)S(1)}, bf16[2,1,2,6656]{3,2,1,0:T(2,128)(2,1)}, u32[]{:S(2)}) copy-start(bf16[2,1,2,6656]{3,2,1,0:T(2,128)(2,1)} %phonon_ref.1) | copy-start | bytes 159748
  3.5 25.9 %collective-permute-start.1 = (bf16[2704,128]{1,0:T(8,128)(2,1)}, bf16[2704,128]{1,0:T(8,128)(2,1)S(1)}, u32[]{:S(2)}, u32[]{:S(2)}) collective-permute-start(bf16[2704,128]{1,0:T(8,128)(2,1)} %get-tuple-element.33), channel_id=1, source_target_pairs={{0,1},{1,0},{2,3},{3,2},{4,5},{5,4},{6,7},{7,6},{8,9},{9,8},{10,11... | collective-permute-start | bytes 2076680 | tf_op jit(solution)/shard_map/ppermute | solution.py:553
  4.9 24.7 %collective-permute-start.2 = (bf16[2704,128]{1,0:T(8,128)(2,1)}, bf16[2704,128]{1,0:T(8,128)(2,1)}, u32[]{:S(2)}, u32[]{:S(2)}) collective-permute-start(bf16[2704,128]{1,0:T(8,128)(2,1)} %get-tuple-element.36), channel_id=1, source_target_pairs={{1,2},{2,1},{5,6},{6,5},{9,10},{10,9},{13,14},{14,13},{17,18},{18,... | collective-permute-start | bytes 2076680 | tf_op jit(solution)/shard_map/ppermute | solution.py:553
  10.0 18.6 %copy-start.1 = (s32[16]{0:T(128)S(1)}, s32[16]{0:T(128)}, u32[]{:S(2)}) copy-start(s32[16]{0:T(128)} %shifts_ref.1) | copy-start | bytes 196
  10.0 25.2 %collective-permute-start = (bf16[2704,128]{1,0:T(8,128)(2,1)}, bf16[2704,128]{1,0:T(8,128)(2,1)S(1)}, u32[]{:S(2)}, u32[]{:S(2)}) collective-permute-start(bf16[2704,128]{1,0:T(8,128)(2,1)} %get-tuple-element.35), channel_id=1, source_target_pairs={{0,1},{1,0},{2,3},{3,2},{4,5},{5,4},{6,7},{7,6},{8,9},{9,8},{10,11... | collective-permute-start | bytes 2076680 | tf_op jit(solution)/shard_map/ppermute | solution.py:553
  10.5 27.4 %collective-permute-start.3 = (bf16[2704,128]{1,0:T(8,128)(2,1)S(1)}, bf16[2704,128]{1,0:T(8,128)(2,1)S(1)}, u32[]{:S(2)}, u32[]{:S(2)}) collective-permute-start(bf16[2704,128]{1,0:T(8,128)(2,1)S(1)} %get-tuple-element.53), channel_id=1, source_target_pairs={{1,2},{2,1},{5,6},{6,5},{9,10},{10,9},{13,14},{14,13},{17,18},{18,... | collective-permute-start | bytes 2076680 | tf_op jit(solution)/shard_map/ppermute | solution.py:553
  40.0 6.8 %collective-permute-start.5 = (bf16[2,2,64,128]{3,2,1,0:T(8,128)(2,1)S(1)}, bf16[2,2,64,128]{3,2,1,0:T(8,128)(2,1)S(1)}, u32[]{:S(2)}, u32[]{:S(2)}) collective-permute-start(bf16[2,2,64,128]{3,2,1,0:T(8,128)(2,1)S(1)} %get-tuple-element.60.rest_0_), channel_id=1, source_target_pairs={{8,16},{12,20},{16,8},{20,12},{9,17},{13,21},{17,9},{21,13},{10,18... | collective-permute-start | bytes 196616 | tf_op jit(solution)/shard_map/ppermute | solution.py:637
  40.7 6.2 %collective-permute-start.7 = (bf16[2,2,64,128]{3,2,1,0:T(8,128)(2,1)S(1)}, bf16[2,2,64,128]{3,2,1,0:T(8,128)(2,1)S(1)}, u32[]{:S(2)}, u32[]{:S(2)}) collective-permute-start(bf16[2,2,64,128]{3,2,1,0:T(8,128)(2,1)S(1)} %get-tuple-element.60.rest_0_), channel_id=1, source_target_pairs={{0,8},{4,12},{8,0},{12,4},{16,24},{20,28},{24,16},{28,20},{1,9},{5... | collective-permute-start | bytes 196616 | tf_op jit(solution)/shard_map/ppermute | solution.py:636
  44.4 5.3 %collective-permute-start.4 = (bf16[2,2,64,128]{3,2,1,0:T(8,128)(2,1)S(1)}, bf16[2,2,64,128]{3,2,1,0:T(8,128)(2,1)S(1)}, u32[]{:S(2)}, u32[]{:S(2)}) collective-permute-start(bf16[2,2,64,128]{3,2,1,0:T(8,128)(2,1)S(1)} %get-tuple-element.60.rest_0_), channel_id=1, source_target_pairs={{0,4},{4,0},{8,12},{12,8},{16,20},{20,16},{24,28},{28,24},{1,5},{5... | collective-permute-start | bytes 196616 | tf_op jit(solution)/shard_map/ppermute | solution.py:640
  46.8 2.9 %collective-permute-start.6 = (bf16[2,2,64,128]{3,2,1,0:T(8,128)(2,1)S(1)}, bf16[2,2,64,128]{3,2,1,0:T(8,128)(2,1)S(1)}, u32[]{:S(2)}, u32[]{:S(2)}) collective-permute-start(bf16[2,2,64,128]{3,2,1,0:T(8,128)(2,1)S(1)} %collective-permute-done.5.rest_2_), channel_id=1, source_target_pairs={{0,4},{4,0},{8,12},{12,8},{16,20},{20,16},{24,28},{28,24},{1,5},{5... | collective-permute-start | bytes 196616 | tf_op jit(solution)/shard_map/ppermute | solution.py:640
  46.9 3.7 %collective-permute-start.8 = (bf16[2,2,64,128]{3,2,1,0:T(8,128)(2,1)S(1)}, bf16[2,2,64,128]{3,2,1,0:T(8,128)(2,1)S(1)}, u32[]{:S(2)}, u32[]{:S(2)}) collective-permute-start(bf16[2,2,64,128]{3,2,1,0:T(8,128)(2,1)S(1)} %collective-permute-done.7.rest_4_), channel_id=1, source_target_pairs={{0,4},{4,0},{8,12},{12,8},{16,20},{20,16},{24,28},{28,24},{1,5},{5... | collective-permute-start | bytes 196616 | tf_op jit(solution)/shard_map/ppermute | solution.py:640
